TPU v7x, 32 devices: a whole 2x2x4 slice. The times are simulated.
32 devices in a mesh: dp: 4 (over z), expert: 4 (over y, x), seq: 2 (over core).
Axes of the slice: x: 2, y: 2, z: 4, core: 2. Of those that a mesh axis runs over, the one named last changes fastest.
Arguments:
- queries: bfloat16 [4096, 2560], P(('dp', 'expert', 'seq')), may hold values from -64 to 64
- memory: bfloat16 [2, 512, 2560], P(None, ('dp', 'expert', 'seq')), may hold values from -6 to 6
- residual: bfloat16 [4096, 2560], P(('dp', 'expert', 'seq')), may hold values from -3 to 3
- norm_gain: float32 [2560], replicated, may hold values from 0.5 to 1.5
- expert_ids: int32 [4096, 2], P(('dp', 'expert', 'seq')), may hold values from 0 to 3, all different within a row; in each aligned block of 128 rows (0 to 127, 128 to 255, ...) at most 80 rows name the same one
- route_gates: float32 [4096, 2], P(('dp', 'expert', 'seq')), may hold values from 0.1 to 1
- weight_in: bfloat16 [4, 2560, 320], P('expert'), may hold values from -0.125 to 0.125
- weight_out: bfloat16 [4, 320, 2560], P('expert'), may hold values from -0.3125 to 0.3125
- layer_grad: bfloat16 [4096, 2560], P(('dp', 'expert', 'seq')), may hold values from -6 to 6
Outputs:
- layer_output: bfloat16 [4096, 2560], P(('dp', 'expert', 'seq'))
- weight_grads: float32 [4, 2560, 320], P('expert', ('dp', 'seq'))
Inputs may be any that keep to these rules, and one draw needn't show every extreme that they name: `expert_ids`: within each aligned block of 128 tokens (the tokens of one device) no expert is named more than 80 times, and in some block one expert is named exactly 80 times.
All inputs are finite; a program needn't handle non-finite values.
Results may differ from a plain program's by a relative error of at most 0.01.
Values may be sent and summed in bfloat16 or wider, within the bound.
No kernel may reach another device: no remote copies, remote signals or barrier semaphores. Data moves between devices by JAX's collectives and lax.ppermute only.
A program may use at most 64 MiB of HBM per device.

v0:
```python
import jax
import jax.numpy as jnp
from jax import lax
from jax.sharding import PartitionSpec as P

HEAD_SIZE = 64


def gelu_tanh(values):
    return jax.nn.gelu(values, approximate=True)


def per_device(
    queries, memory, residual, norm_gain, expert_ids, route_gates, weight_in, weight_out, layer_grad
):
    tokens_here, model_width = queries.shape
    head_count = model_width // HEAD_SIZE
    memory_all = lax.all_gather(memory, "seq", axis=1, tiled=True)
    query_per_head = queries.reshape(tokens_here, head_count, HEAD_SIZE)
    key_per_head = memory_all[0].reshape(-1, head_count, HEAD_SIZE)
    value_per_head = memory_all[1].reshape(-1, head_count, HEAD_SIZE)
    attention_scores = jnp.einsum(
        "gvc,rvc->vgr", query_per_head, key_per_head, preferred_element_type=jnp.float32
    ) * HEAD_SIZE ** (-0.5)
    largest = jnp.max(attention_scores, axis=-1, keepdims=True)
    exponent = jnp.exp(attention_scores - largest)
    attention_probabilities = (exponent / jnp.sum(exponent, axis=-1, keepdims=True)).astype(
        jnp.bfloat16
    )
    attended_values = jnp.einsum(
        "nqz,zny->qny", attention_probabilities, value_per_head, preferred_element_type=jnp.float32
    )
    attended_values = attended_values.astype(jnp.bfloat16).reshape(tokens_here, model_width)
    stream = residual.astype(jnp.float32) + attended_values.astype(jnp.float32)
    scale_factor = lax.rsqrt(jnp.mean(stream * stream, axis=-1, keepdims=True) + 1e-06)
    normed = (stream * scale_factor * norm_gain).astype(jnp.bfloat16)
    expert_count = lax.axis_size("expert")
    capacity = (5 * tokens_here + 2 * expert_count - 1) // (2 * expert_count)
    flat_ids = expert_ids.reshape(-1)
    one_hot = (flat_ids[:, None] == jnp.arange(expert_count, dtype=jnp.int32)[None, :]).astype(
        jnp.int32
    )
    earlier = jnp.cumsum(one_hot, axis=0) - one_hot
    slot_index = jnp.sum(earlier * one_hot, axis=1)
    positions = flat_ids * capacity + slot_index
    slot_count = expert_count * capacity
    matches = positions[None, :] == jnp.arange(slot_count, dtype=jnp.int32)[:, None]
    pair_index = jnp.sum(
        jnp.where(matches, jnp.arange(2 * tokens_here, dtype=jnp.int32)[None, :], 0), axis=1
    )
    valid_slot = jnp.any(matches, axis=1)[:, None]
    zero_value = jnp.zeros((), jnp.bfloat16)
    send_rows = jnp.where(valid_slot, normed[pair_index // 2], zero_value)
    pair_grads = (
        (route_gates[:, :, None] * layer_grad.astype(jnp.float32)[:, None, :])
        .astype(jnp.bfloat16)
        .reshape(-1, model_width)
    )
    send_grads = jnp.where(valid_slot, pair_grads[pair_index], zero_value)
    send_rows = send_rows.reshape(expert_count, capacity, model_width)
    send_grads = send_grads.reshape(expert_count, capacity, model_width)
    received_rows = lax.all_to_all(send_rows, "expert", split_axis=0, concat_axis=0, tiled=True)
    token_rows = received_rows.reshape(-1, model_width)
    matrix_in = weight_in[0]
    matrix_out = weight_out[0]
    preact = jnp.dot(token_rows, matrix_in, preferred_element_type=jnp.float32)
    activated, gelu_back = jax.vjp(gelu_tanh, preact)
    hidden = activated.astype(jnp.bfloat16)
    expert_outputs = jnp.dot(hidden, matrix_out, preferred_element_type=jnp.float32).astype(
        jnp.bfloat16
    )
    expert_outputs = expert_outputs.reshape(expert_count, capacity, model_width)
    returned = lax.all_to_all(expert_outputs, "expert", split_axis=0, concat_axis=0, tiled=True)
    returned_flat = returned.reshape(-1, model_width)
    picked = returned_flat[positions.reshape(tokens_here, 2)]
    expert_mix = jnp.sum(picked.astype(jnp.float32) * route_gates[:, :, None], axis=1)
    layer_output = (stream + expert_mix).astype(jnp.bfloat16)
    received_grads = lax.all_to_all(send_grads, "expert", split_axis=0, concat_axis=0, tiled=True)
    cotangent_rows = received_grads.reshape(-1, model_width)
    hidden_grad = lax.dot_general(
        cotangent_rows, matrix_out, (((1,), (1,)), ((), ())), preferred_element_type=jnp.float32
    )
    preact_grad = gelu_back(hidden_grad)[0].astype(jnp.bfloat16)
    grads_here = lax.psum_scatter(
        lax.dot_general(
            token_rows, preact_grad, (((0,), (0,)), ((), ())), preferred_element_type=jnp.float32
        ),
        ("dp", "seq"),
        scatter_dimension=0,
        tiled=True,
    )
    return (layer_output, grads_here[None])


def solution(mesh):
    return jax.shard_map(
        per_device,
        mesh=mesh,
        in_specs=(
            P(("dp", "expert", "seq"), None),
            P(None, ("dp", "expert", "seq"), None),
            P(("dp", "expert", "seq"), None),
            P(),
            P(("dp", "expert", "seq"), None),
            P(("dp", "expert", "seq"), None),
            P("expert", None, None),
            P("expert", None, None),
            P(("dp", "expert", "seq"), None),
        ),
        out_specs=(P(("dp", "expert", "seq"), None), P("expert", ("dp", "seq"), None)),
        check_vma=False,
    )
```

profile of v0, /device:TPU:0, one launch (start us, length us, event | category | flops | bytes accessed | tf_op | source)
XLA Modules:
  0.0 152.1 jit_solution(13744618428979548729)
XLA Ops:
  7.2 0.0 copy-start
  7.2 0.9 copy.44
  8.1 0.1 eq.39
  8.2 0.1 reshape.151
  8.4 1.2 reduce-window.6
  9.6 0.1 slice.24
  9.7 0.1 copy.46
  9.8 0.1 copy.47
  9.9 0.1 add_bitcast_fusion
  10.0 0.2 select_reduce_fusion
  10.2 0.2 fusion.25
  10.3 3.3 %mul.133 = f32[128,2,2560]{2,1,0:T(2,128)} broadcast(bf16[128,2560]{1,0:T(8,128)(2,1)} %param.17), dimensions={0,2} | broadcast | bytes 3276800 | tf_op jit(solution)/shard_map/mul | solution.py:55
  13.6 0.0 copy-start.8
  13.6 0.0 copy-start.5
  13.6 4.6 %mul.134 = f32[256,2560]{1,0:T(8,128)} reshape(f32[128,2,2560]{2,1,0:T(2,128)} %mul.133) | data formatting | bytes 5242880 | tf_op jit(solution)/shard_map/mul | solution.py:55
  18.2 0.0 copy-done.8
  18.2 0.0 copy-start.4
  18.2 0.1 copy.50
  18.3 0.1 mul.131
  18.5 0.1 broadcast_in_dim.50
  18.6 0.0 copy-done.5
  18.6 2.1 %all_gather.3 = bf16[2,32,2560]{2,1,0:T(8,128)(2,1)S(1)} all-gather(bf16[2,16,2560]{2,1,0:T(8,128)(2,1)S(1)} %copy-done.5), channel_id=1, replica_groups=mesh['dp'=4,'expert'=4,'seq'=2] {'seq'}, dimensions={1}, use_global_device_ids=true | all-gather | bytes 491520 | tf_op jit(solution)/shard_map/all_gather | solution.py:18
  20.7 0.9 reshape_squeeze.7
  21.7 0.0 copy-done.4
  21.7 0.3 copy.40
  22.0 0.2 reshape_squeeze.6
  22.2 0.3 convolution_multiply_fusion
  22.5 0.2 fusion.55
  22.7 2.5 %fusion.7 = f32[40,128,64]{1,2,0:T(8,128)} fusion(bf16[32,40,64]{2,1,0:T(8,128)(2,1)} %reshape_squeeze.7, f32[40,128]{1,0:T(8,128)S(1)} %fusion.55, f32[40,128,32]{1,2,0:T(8,128)S(1)} %convolution_multiply_fusion), kind=kOutput, calls=%fused_computation.16 | convolution fusion | flops 22123552 | bytes 2150400 | tf_op jit(solution)/shard_map/nqz,zny->qny/dot_general | solution.py:30
  25.1 1.7 %copy.43 = f32[128,2560]{1,0:T(8,128)S(1)} copy(f32[128,2560]{0,1:T(8,128)} %bitcast.55) | data formatting | bytes 2621440 | tf_op jit(solution)/shard_map/convert_element_type | solution.py:34
  26.9 0.0 copy-start.1
  26.9 1.8 %multiply_reduce_fusion.1 = f32[128]{0:T(128)S(1)} fusion(f32[128,2560]{1,0:T(8,128)S(1)} %copy.43, bf16[128,2560]{1,0:T(8,128)(2,1)} %param.11), kind=kLoop, calls=%fused_computation.19 | loop fusion | flops 1310592 | bytes 1966592 | tf_op jit(solution)/shard_map/reduce_sum | solution.py:35
  28.7 0.0 copy-done.1
  28.7 1.9 %multiply_convert_fusion = bf16[256,2560]{1,0:T(8,128)(2,1)S(1)} fusion(f32[256,2560]{1,0:T(8,128)} %mul.134, f32[256]{0:T(256)S(1)} %mul.131), kind=kLoop, calls=%fused_computation.5 | loop fusion | flops 1310720 | bytes 3933184 | tf_op jit(solution)/shard_map/convert_element_type | solution.py:56
  30.7 0.0 copy-start.6
  30.7 3.2 %gather_fusion.2 = bf16[320,2560]{1,0:T(8,128)(2,1)} fusion(bf16[256,2560]{1,0:T(8,128)(2,1)S(1)} %multiply_convert_fusion, s32[1024]{0:T(1024)S(1)} %get-tuple-element.8), kind=kCustom, calls=%fused_computation.2 | custom fusion | bytes 3278080 | tf_op jit(solution)/shard_map/gather | solution.py:59
  33.9 0.0 copy-done.6
  33.9 1.7 %multiply_convert_fusion.1 = bf16[128,2560]{1,0:T(8,128)(2,1)S(1)} fusion(f32[2560]{0:T(1024)S(1)} %copy-done.6, f32[128]{0:T(128)S(1)} %add_rsqrt_fusion, f32[128,2560]{1,0:T(8,128)} %copy-done.1, bf16[128,2560]{1,0:T(8,128)(2,1)} %param.11), kind=kLoop, calls=%fused_computation.18 | loop fusion | flops 1638400 | bytes 2632192 | tf_op jit(solution)/shard_map/convert_element_type | solution.py:36
  35.6 3.2 %gather_fusion = bf16[320,2560]{1,0:T(8,128)(2,1)} fusion(bf16[128,2560]{1,0:T(8,128)(2,1)S(1)} %multiply_convert_fusion.1, s32[1024]{0:T(1024)S(1)} %get-tuple-element.9), kind=kCustom, calls=%fused_computation | custom fusion | bytes 3278080 | tf_op jit(solution)/shard_map/gather | solution.py:53
  38.7 3.4 %broadcast_select_fusion = (bf16[4,80,2560]{2,1,0:T(8,128)(2,1)}, bf16[4,80,2560]{2,1,0:T(8,128)(2,1)S(1)}) fusion(bf16[4,80,2560]{2,1,0:T(8,128)(2,1)} %bitcast.49, pred[4,80]{1,0:T(4,128)(4,1)S(1)} %broadcast_in_dim.50, bf16[4,80,2560]{2,1,0:T(8,128)(2,1)} %bitcast.50), kind=kLoop, calls=%fused_computation.12 | loop fusion | flops 1638400 | bytes 6553920 | tf_op jit(solution)/shard_map/jit(_where)/select_n | solution.py:59
  42.1 25.8 %all_to_all.15 = bf16[4,80,2560]{2,1,0:T(8,128)(2,1)S(1)} all-to-all(bf16[4,80,2560]{2,1,0:T(8,128)(2,1)S(1)} %get-tuple-element.7), channel_id=1, replica_groups=mesh['dp'=4,'expert'=4,'seq'=2] {'expert'}, dimensions={0} | all-to-all | bytes 3276800 | tf_op jit(solution)/shard_map/all_to_all | solution.py:62
  67.9 4.3 %all-to-all-start.2 = ((bf16[4,80,2560]{2,1,0:T(8,128)(2,1)}), bf16[4,80,2560]{2,1,0:T(8,128)(2,1)}, u32[]{:S(2)}, u32[]{:S(2)}) async-start(bf16[4,80,2560]{2,1,0:T(8,128)(2,1)} %get-tuple-element.6), calls=%async_computation.2 | async-start | bytes 3276800 | tf_op jit(solution)/shard_map/all_to_all | solution.py:78
  72.3 0.0 reduce-scatter.2.cloned.1.call-start
  72.3 3.2 %fusion.4 = f32[320,320]{1,0:T(8,128)} fusion(bf16[320,2560]{1,0:T(8,128)(2,1)S(1)} %bitcast.53, bf16[1,2560,320]{1,2,0:T(8,128)(2,1)} %param.15), kind=kOutput, calls=%fused_computation.10 | convolution fusion | flops 524288000 | bytes 3686400 | tf_op jit(solution)/shard_map/dot_general | solution.py:66
  75.6 15.8 %all-to-all-done.2 = bf16[4,80,2560]{2,1,0:T(8,128)(2,1)} async-done(((bf16[4,80,2560]{2,1,0:T(8,128)(2,1)}), bf16[4,80,2560]{2,1,0:T(8,128)(2,1)}, u32[]{:S(2)}, u32[]{:S(2)}) %all-to-all-start.2) | async-done | bytes 1638432 | tf_op jit(solution)/shard_map/all_to_all | solution.py:78
  91.3 0.0 copy-done
  91.4 5.9 %fusion.19 = f32[2560,320]{1,0:T(8,128)} fusion(bf16[320,2560]{1,0:T(8,128)(2,1)S(1)} %bitcast.54, f32[320,320]{1,0:T(8,128)} %fusion.4, bf16[320,2560]{1,0:T(8,128)(2,1)} %bitcast.12, bf16[1,320,2560]{2,1,0:T(8,128)(2,1)S(1)} %copy-done), kind=kOutput, calls=%fused_computation.33 | convolution fusion | flops 1050624000 | bytes 8601600 | tf_op jit(solution)/shard_map/dot_general | solution.py:85
  97.2 0.0 reduce-scatter.2.cloned.1.call-update
  97.3 1.0 copy-done.9
  98.3 2.2 %convolution_convert_fusion = bf16[320,2560]{1,0:T(8,128)(2,1)} fusion(bf16[1,320,2560]{2,1,0:T(8,128)(2,1)S(1)} %copy-done, f32[320,320]{1,0:T(8,128)S(1)} %copy-done.9), kind=kOutput, calls=%fused_computation.4 | convolution fusion | flops 526028800 | bytes 3686400 | tf_op jit(solution)/shard_map/dot_general | solution.py:69
  100.5 3.9 %all-to-all-start.1 = ((bf16[4,80,2560]{2,1,0:T(8,128)(2,1)}), bf16[4,80,2560]{2,1,0:T(8,128)(2,1)S(1)}, u32[]{:S(2)}, u32[]{:S(2)}) async-start(bf16[4,80,2560]{2,1,0:T(8,128)(2,1)} %bitcast.52), calls=%async_computation.1 | async-start | bytes 3276800 | tf_op jit(solution)/shard_map/all_to_all | solution.py:73
  104.4 0.1 reduce_sum.54
  104.5 0.1 copy.48
  104.6 0.0 copy-done.7
  104.6 0.1 copy.49
  104.7 0.1 reshape.168
  104.9 18.7 %all-to-all-done.1 = bf16[4,80,2560]{2,1,0:T(8,128)(2,1)S(1)} async-done(((bf16[4,80,2560]{2,1,0:T(8,128)(2,1)}), bf16[4,80,2560]{2,1,0:T(8,128)(2,1)S(1)}, u32[]{:S(2)}, u32[]{:S(2)}) %all-to-all-start.1) | async-done | bytes 1638432 | tf_op jit(solution)/shard_map/all_to_all | solution.py:73
  123.5 2.6 %gather_fusion.1 = bf16[256,2560]{1,0:T(8,128)(2,1)} fusion(bf16[320,2560]{1,0:T(8,128)(2,1)S(1)} %bitcast.48, s32[1024]{0:T(1024)S(1)} %pad_clamp_fusion.1), kind=kCustom, calls=%fused_computation.1 | custom fusion | bytes 2622464 | tf_op jit(solution)/shard_map/gather | solution.py:75
  126.2 4.2 %reshape.184 = f32[128,2,2560]{2,1,0:T(2,128)} reshape(bf16[256,2560]{1,0:T(8,128)(2,1)} %gather_fusion.1) | data formatting | bytes 3932160 | tf_op jit(solution)/shard_map/convert_element_type | solution.py:76
  130.3 5.7 %multiply_reduce_fusion = f32[128,2560]{1,0:T(8,128)S(1)} fusion(f32[128,2,2560]{2,1,0:T(2,128)} %reshape.184, f32[128,2]{1,0:T(8,128)S(1)} %copy.50), kind=kLoop, calls=%fused_computation.6 | loop fusion | flops 983040 | bytes 3933184 | tf_op jit(solution)/shard_map/reduce_sum | solution.py:76
  136.0 0.0 copy-done.2
  136.0 0.0 copy-done.3
  136.0 1.0 add_convert_fusion
  137.1 8.2 %reduce-scatter.2.cloned.1.call-done = f32[320,320]{1,0:T(8,128)} async-done(((f32[2560,320]{1,0:T(8,128)}), f32[320,320]{1,0:T(8,128)}) %reduce-scatter.2.cloned.1.call-update) | async-done | bytes 409616 | tf_op jit(solution)/shard_map/reduce_scatter | solution.py:84
  (15 shorter events, 0.2 us)
Async XLA Ops:
  7.2 84.2 %copy-start = (bf16[1,320,2560]{2,1,0:T(8,128)(2,1)S(1)}, bf16[1,320,2560]{2,1,0:T(8,128)(2,1)}, u32[]{:S(2)}) copy-start(bf16[1,320,2560]{2,1,0:T(8,128)(2,1)} %param.16) | copy-start | bytes 4915204
  13.6 4.6 %copy-start.8 = (f32[128,2]{0,1:T(2,128)S(1)}, f32[128,2]{0,1:T(2,128)}, u32[]{:S(2)}) copy-start(f32[128,2]{0,1:T(2,128)} %param.14) | copy-start | bytes 3076
  13.6 4.9 %copy-start.5 = (bf16[2,16,2560]{2,1,0:T(8,128)(2,1)S(1)}, bf16[2,16,2560]{2,1,0:T(8,128)(2,1)}, u32[]{:S(2)}) copy-start(bf16[2,16,2560]{2,1,0:T(8,128)(2,1)} %param.10) | copy-start | bytes 491524
  18.2 3.5 %copy-start.4 = (bf16[128,2560]{1,0:T(8,128)(2,1)S(1)}, bf16[128,2560]{1,0:T(8,128)(2,1)}, u32[]{:S(2)}) copy-start(bf16[128,2560]{1,0:T(8,128)(2,1)} %param.9) | copy-start | bytes 1966084
  26.9 1.8 %copy-start.1 = (f32[128,2560]{1,0:T(8,128)}, f32[128,2560]{1,0:T(8,128)S(1)}, u32[]{:S(2)}) copy-start(f32[128,2560]{1,0:T(8,128)S(1)} %copy.43) | copy-start | bytes 3932164
  30.7 3.2 %copy-start.6 = (f32[2560]{0:T(1024)S(1)}, f32[2560]{0:T(1024)}, u32[]{:S(2)}) copy-start(f32[2560]{0:T(1024)} %param.12) | copy-start | bytes 30724
  67.9 23.4 %all-to-all-start.2 = ((bf16[4,80,2560]{2,1,0:T(8,128)(2,1)}), bf16[4,80,2560]{2,1,0:T(8,128)(2,1)}, u32[]{:S(2)}, u32[]{:S(2)}) async-start(bf16[4,80,2560]{2,1,0:T(8,128)(2,1)} %get-tuple-element.6), calls=%async_computation.2 | async-start | bytes 3276800 | tf_op jit(solution)/shard_map/all_to_all | solution.py:78
  72.3 72.9 %reduce-scatter.2.cloned.1.call-start = ((), (), s32[]{:S(2)}) async-start(), calls=%async_computation.4 | async-start | bytes 4423680 | tf_op jit(solution)/shard_map/reduce_scatter | solution.py:84
  97.2 1.0 copy-start.9
  100.5 4.1 %copy-start.7 = (s32[128,2]{0,1:T(2,128)S(1)}, s32[128,2]{0,1:T(2,128)}, u32[]{:S(2)}) copy-start(s32[128,2]{0,1:T(2,128)} %param.13) | copy-start | bytes 3076
  100.5 23.1 %all-to-all-start.1 = ((bf16[4,80,2560]{2,1,0:T(8,128)(2,1)}), bf16[4,80,2560]{2,1,0:T(8,128)(2,1)S(1)}, u32[]{:S(2)}, u32[]{:S(2)}) async-start(bf16[4,80,2560]{2,1,0:T(8,128)(2,1)} %bitcast.52), calls=%async_computation.1 | async-start | bytes 3276800 | tf_op jit(solution)/shard_map/all_to_all | solution.py:73
  130.3 5.7 %copy-start.2 = (f32[128,2560]{1,0:T(8,128)S(1)}, f32[128,2560]{1,0:T(8,128)}, u32[]{:S(2)}) copy-start(f32[128,2560]{1,0:T(8,128)} %copy-done.1) | copy-start | bytes 3932164
  130.3 5.7 %copy-start.3 = (bf16[128,2560]{1,0:T(8,128)(2,1)S(1)}, bf16[128,2560]{1,0:T(8,128)(2,1)}, u32[]{:S(2)}) copy-start(bf16[128,2560]{1,0:T(8,128)(2,1)} %param.11) | copy-start | bytes 1966084
Sparse Core Ops, SparseCore 0:
  97.4 47.7 reduce-scatter.1
where the time goes:
time: 153 us; the launch traced here: 152 us
  waiting for transfers between devices  42.6 us (28%)
  blocking collectives  27.9 us (18%)
  local copies, waits for them, and re-layouts  27.5 us (18%)
  other arithmetic  17.5 us (11%)
  between operations  14.2 us (9%)
  matrix products  14.1 us (9%)
  starting transfers between devices  8.28 us (5%)
    all_to_all x1, blocking collectives, per_device(): lax.all_to_all(send_rows, 'expert', split_axis=0, concat_axis=0, tiled=True)  25.8 us
    all_to_all x1, waiting for transfers between devices, per_device(): lax.all_to_all(expert_outputs, 'expert', split_axis=0, concat_axis=0, til...  18.7 us
    all_to_all x1, waiting for transfers between devices, per_device(): lax.all_to_all(send_grads, 'expert', split_axis=0, concat_axis=0, tiled=T...  15.8 us
    reduce_scatter x1, waiting for transfers between devices, per_device(): lax.psum_scatter(lax.dot_general(token_rows, preact_grad, (((0,), (0,)),...  8.16 us
    mul x2, local copies, waits for them, and re-layouts, per_device(): route_gates[:, :, None] * layer_grad.astype(jnp.float32)[:, None, :]  7.86 us
    dot_general x1, matrix products, per_device(): lax.dot_general(token_rows, preact_grad, (((0,), (0,)), ((), ())), prefer...  5.88 us
    reduce_sum x1, other arithmetic, per_device(): jnp.sum(picked.astype(jnp.float32) * route_gates[:, :, None], axis=1)  5.68 us
    all_to_all x1, starting transfers between devices, per_device(): lax.all_to_all(send_grads, 'expert', split_axis=0, concat_axis=0, tiled=T...  4.35 us
  transfers between devices with their start and end apart: 3, of which 3 were waited for; matrix products, arithmetic and copies ran while one was open for 13% of the time, Pallas kernels for 0%

commit v1 on v0

v1 whole, which is shorter than its diff:
```python
import functools

import jax
import jax.numpy as jnp
from jax import lax
from jax.experimental import pallas as pl
from jax.experimental.pallas import tpu as pltpu
from jax.sharding import PartitionSpec as P

HEAD_SIZE = 64
GROUP = 256
CHUNK = 512
VMEM_LIMIT = 24 * 1024 * 1024
GELU_C = 0.7978845608028654
GELU_A = 0.044715
BF16 = jnp.bfloat16
F32 = jnp.float32


def params():
    return pltpu.CompilerParams(vmem_limit_bytes=VMEM_LIMIT)


def call(kernel, out_shapes, scratch=()):
    return pl.pallas_call(
        kernel, out_shape=out_shapes, scratch_shapes=list(scratch), compiler_params=params()
    )


def shape(dims, dtype):
    return jax.ShapeDtypeStruct(dims, dtype)


def slots_of(ids_ref):
    tokens = ids_ref.shape[1]
    me = lax.axis_index("expert")
    expert = lax.broadcasted_iota(jnp.int32, (8, tokens), 0) ^ me
    first = ids_ref[0:1, :] == expert
    chosen = first | (ids_ref[1:2, :] == expert)
    earlier = lax.broadcasted_iota(jnp.int32, (tokens, tokens), 0) < lax.broadcasted_iota(
        jnp.int32, (tokens, tokens), 1
    )
    count = jnp.dot(
        jnp.where(chosen, 1.0, 0.0).astype(BF16),
        jnp.where(earlier, 1.0, 0.0).astype(BF16),
        preferred_element_type=F32,
    )
    return jnp.where(chosen, count.astype(jnp.int32), -1), first


def gates_of(gates_ref, first):
    return jnp.where(first, gates_ref[0:1, :], gates_ref[1:2, :])


def one_hot(slots, k, capacity):
    tokens = slots.shape[1]
    return lax.broadcasted_iota(jnp.int32, (capacity, tokens), 0) == slots[k : k + 1, :]


def as_bf16(mask):
    return jnp.where(mask, 1.0, 0.0).astype(BF16)


def dispatch_grads(count, ids_ref, gates_ref, grad_ref, *out_refs):
    slots, first = slots_of(ids_ref)
    gates = gates_of(gates_ref, first)
    width = grad_ref.shape[1]
    for k in range(count):
        mask = one_hot(slots, k, out_refs[k].shape[0])
        gate = jnp.sum(jnp.where(mask, gates[k : k + 1, :], 0.0), axis=1, keepdims=True)
        pick = as_bf16(mask)
        for at in range(0, width, CHUNK):
            cols = slice(at, at + CHUNK)
            rows = jnp.dot(pick, grad_ref[:, cols], preferred_element_type=F32)
            out_refs[k][:, cols] = (rows * gate).astype(BF16)


def attend(count, parts, *refs):
    ids_ref, query_ref = refs[0:2]
    memory_refs = refs[2 : 2 + parts]
    residual_ref, gain_ref = refs[2 + parts : 4 + parts]
    stream_ref = refs[4 + parts]
    out_refs = refs[5 + parts : 5 + parts + count]
    normed_ref = refs[5 + parts + count]
    tokens, width = query_ref.shape
    heads = GROUP // HEAD_SIZE
    rows = sum(ref.shape[1] for ref in memory_refs)
    own = (
        lax.broadcasted_iota(jnp.int32, (heads * rows, GROUP), 0) // rows
        == lax.broadcasted_iota(jnp.int32, (heads * rows, GROUP), 1) // HEAD_SIZE
    )
    total = jnp.zeros((tokens, 1), F32)

    def spread(which, cols):
        piece = jnp.concatenate([ref[which, :, cols] for ref in memory_refs], axis=0)
        return jnp.where(own, jnp.concatenate([piece] * heads, axis=0), jnp.zeros((), BF16))

    for at in range(0, width, GROUP):
        cols = slice(at, at + GROUP)
        scores = lax.dot_general(
            spread(0, cols), query_ref[:, cols], (((1,), (1,)), ((), ())), preferred_element_type=F32
        ) * HEAD_SIZE ** (-0.5)
        scores = scores.reshape(heads, rows, tokens)
        exponent = jnp.exp(scores - jnp.max(scores, axis=1, keepdims=True))
        probs = exponent / jnp.sum(exponent, axis=1, keepdims=True)
        attended = lax.dot_general(
            probs.reshape(heads * rows, tokens).astype(BF16),
            spread(1, cols),
            (((0,), (0,)), ((), ())),
            preferred_element_type=F32,
        ).astype(BF16)
        stream = residual_ref[:, cols].astype(F32) + attended.astype(F32)
        stream_ref[:, cols] = stream
        total = total + jnp.sum(stream * stream, axis=1, keepdims=True)
    scale = lax.rsqrt(total / width + 1e-06)
    for at in range(0, width, CHUNK):
        cols = slice(at, at + CHUNK)
        normed_ref[:, cols] = (stream_ref[:, cols] * scale * gain_ref[:, cols]).astype(BF16)
    slots, _ = slots_of(ids_ref)
    for k in range(count):
        pick = as_bf16(one_hot(slots, k, out_refs[k].shape[0]))
        for at in range(0, width, CHUNK):
            cols = slice(at, at + CHUNK)
            out_refs[k][:, cols] = jnp.dot(
                pick, normed_ref[:, cols], preferred_element_type=F32
            ).astype(BF16)


def expert_forward(count, *refs):
    rows_refs = refs[0:count]
    in_ref, out_ref = refs[count : count + 2]
    slope_refs = refs[count + 2 : 2 * count + 2]
    result_refs = refs[2 * count + 2 :]
    width = in_ref.shape[1]
    for k in range(count):
        value = lax.dot_general(
            rows_refs[k][...], in_ref[...], (((1,), (1,)), ((), ())), preferred_element_type=F32
        )
        square = value * value
        curve = jnp.tanh(GELU_C * (value + GELU_A * square * value))
        hidden = (0.5 * value * (1.0 + curve)).astype(BF16)
        slope_refs[k][...] = 0.5 * (1.0 + curve) + 0.5 * value * (1.0 - curve * curve) * (
            GELU_C * (1.0 + 3.0 * GELU_A * square)
        )
        for at in range(0, width, CHUNK):
            cols = slice(at, at + CHUNK)
            result_refs[k][:, cols] = jnp.dot(
                hidden, out_ref[:, cols], preferred_element_type=F32
            ).astype(BF16)


def preact_grads(count, grad_refs, slope_refs, out_ref):
    parts = []
    for k in range(count):
        back = lax.dot_general(
            grad_refs[k][...], out_ref[...], (((1,), (1,)), ((), ())), preferred_element_type=F32
        )
        parts.append((back * slope_refs[k][...]).astype(BF16))
    return jnp.concatenate(parts, axis=0)


def pack(block):
    rows, columns = block.shape
    full = columns // 128 * 128
    pieces = [block[:, at : at + 128] for at in range(0, full, 128)]
    pieces.append(
        jnp.concatenate([block[: rows // 2, full:], block[rows // 2 :, full:]], axis=1)
    )
    return jnp.concatenate(pieces, axis=0)


def unpack(packed, rows, columns):
    full = columns // 128 * 128
    last = packed[full // 128 * rows :, :]
    half = columns - full
    pieces = [packed[at * rows : (at + 1) * rows, :] for at in range(full // 128)]
    pieces.append(jnp.concatenate([last[:, :half], last[:, half:]], axis=0))
    return jnp.concatenate(pieces, axis=1)


def weight_grads_packed(count, shards, *refs):
    rows_refs, grad_refs = refs[0:count], refs[count : 2 * count]
    slope_refs = refs[2 * count : 3 * count]
    out_ref = refs[3 * count]
    keep_ref, send_ref = refs[3 * count + 1 :]
    back = preact_grads(count, grad_refs, slope_refs, out_ref)
    rows = jnp.concatenate([ref[...] for ref in rows_refs], axis=0)
    full = lax.dot_general(rows, back, (((0,), (0,)), ((), ())), preferred_element_type=F32)
    block = full.shape[0] // (2 * shards)
    core = lax.axis_index("seq")
    for shard in range(shards):
        even = pack(full[2 * shard * block : (2 * shard + 1) * block])
        odd = pack(full[(2 * shard + 1) * block : (2 * shard + 2) * block])
        keep_ref[shard] = jnp.where(core == 0, even, odd)
        send_ref[shard] = jnp.where(core == 0, odd, even).astype(BF16)


def weight_grads_whole(count, *refs):
    rows_refs, grad_refs = refs[0:count], refs[count : 2 * count]
    slope_refs = refs[2 * count : 3 * count]
    out_ref, result_ref = refs[3 * count :]
    back = preact_grads(count, grad_refs, slope_refs, out_ref)
    rows = jnp.concatenate([ref[...] for ref in rows_refs], axis=0)
    result_ref[...] = lax.dot_general(
        rows, back, (((0,), (0,)), ((), ())), preferred_element_type=F32
    )


def add_cores(shards, keep_ref, other_ref, own_ref, *send_refs):
    me = lax.axis_index("dp")
    own_ref[...] = keep_ref[me] + other_ref[me].astype(F32)
    for k in range(1, shards):
        send_refs[k - 1][...] = (keep_ref[me ^ k] + other_ref[me ^ k].astype(F32)).astype(BF16)


def add_replicas(own_ref, *refs):
    total = own_ref[...]
    for ref in refs[:-1]:
        total = total + ref[...].astype(F32)
    _, rows, columns = refs[-1].shape
    refs[-1][0] = unpack(total, rows, columns)


def combine(count, ids_ref, gates_ref, stream_ref, *refs):
    back_refs, out_ref = refs[0:count], refs[count]
    slots, first = slots_of(ids_ref)
    gates = gates_of(gates_ref, first).T
    width = stream_ref.shape[1]
    picks = [as_bf16(one_hot(slots, k, back_refs[k].shape[0])) for k in range(count)]
    for at in range(0, width, CHUNK):
        cols = slice(at, at + CHUNK)
        total = stream_ref[:, cols]
        for k in range(count):
            row = lax.dot_general(
                picks[k], back_refs[k][:, cols], (((0,), (0,)), ((), ())), preferred_element_type=F32
            )
            total = total + row * gates[:, k : k + 1]
        out_ref[:, cols] = total.astype(BF16)


def swap(value, axis, k):
    return lax.ppermute(value, axis, [(i, i ^ k) for i in range(lax.axis_size(axis))])


def per_device(
    queries, memory, residual, norm_gain, expert_ids, route_gates, weight_in, weight_out, layer_grad
):
    tokens, width = queries.shape
    hidden_width = weight_in.shape[2]
    experts, replicas, cores = (lax.axis_size(axis) for axis in ("expert", "dp", "seq"))
    capacity = (5 * tokens + 2 * experts - 1) // (2 * experts)
    capacity = (capacity + 15) // 16 * 16
    ids, gates = expert_ids.T, route_gates.T
    matrix_in, matrix_out = weight_in[0].T, weight_out[0]
    rows_shape = [shape((capacity, width), BF16)] * experts

    if cores == 2:
        memories = [memory, swap(memory, "seq", 1)]
    else:
        memories = [lax.all_gather(memory, "seq", axis=1, tiled=True)]
    grads = call(functools.partial(dispatch_grads, experts), rows_shape)(ids, gates, layer_grad)
    grads = [grads[0]] + [swap(grads[k], "expert", k) for k in range(1, experts)]
    stream, *rows = call(
        functools.partial(attend, experts, len(memories)),
        [shape((tokens, width), F32)] + rows_shape,
        [pltpu.VMEM((tokens, width), BF16)],
    )(ids, queries, *memories, residual, norm_gain[None])
    rows = [rows[0]] + [swap(rows[k], "expert", k) for k in range(1, experts)]
    outs = call(
        functools.partial(expert_forward, experts),
        [shape((capacity, hidden_width), F32)] * experts + rows_shape,
    )(*rows, matrix_in, matrix_out)
    slopes, results = outs[:experts], outs[experts:]
    results = [results[0]] + [swap(results[k], "expert", k) for k in range(1, experts)]

    block = width // (replicas * cores)
    if cores == 2 and replicas in (2, 4) and block % 32 == 0 and hidden_width % 128 == 64:
        packed = (replicas, block * hidden_width // 128, 128)
        keep, send = call(
            functools.partial(weight_grads_packed, experts, replicas),
            [shape(packed, F32), shape(packed, BF16)],
        )(*rows, *grads, *slopes, matrix_out)
        own, *sends = call(
            functools.partial(add_cores, replicas),
            [shape(packed[1:], F32)] + [shape(packed[1:], BF16)] * (replicas - 1),
        )(keep, swap(send, "seq", 1))
        received = [swap(sends[k - 1], "dp", k) for k in range(1, replicas)]
        grads_here = call(add_replicas, shape((1, block, hidden_width), F32))(own, *received)
    else:
        whole = call(
            functools.partial(weight_grads_whole, experts), shape((width, hidden_width), F32)
        )(*rows, *grads, *slopes, matrix_out)
        grads_here = lax.psum_scatter(whole, ("dp", "seq"), scatter_dimension=0, tiled=True)[None]

    layer_output = call(functools.partial(combine, experts), shape((tokens, width), BF16))(
        ids, gates, stream, *results
    )
    return layer_output, grads_here


def solution(mesh):
    rows = P(("dp", "expert", "seq"), None)
    return jax.shard_map(
        per_device,
        mesh=mesh,
        in_specs=(
            rows,
            P(None, ("dp", "expert", "seq"), None),
            rows,
            P(),
            rows,
            rows,
            P("expert", None, None),
            P("expert", None, None),
            rows,
        ),
        out_specs=(rows, P("expert", ("dp", "seq"), None)),
        check_vma=False,
    )
```

time: 153 us -> 76.7 us (0.50)
  blocking collectives: 27.9 us -> 0 us
  local copies, waits for them, and re-layouts: 27.5 us -> 7.01 us
  other arithmetic: 17.5 us -> 0 us
  starting transfers between devices: 8.28 us -> 23 us
  matrix products: 14.1 us -> 0 us
  Pallas kernels: 0 us -> 13.8 us
  between operations: 14.2 us -> 0.71 us
  waiting for transfers between devices: 42.6 us -> 31.8 us
    all_to_all x2 -> x0, waiting for transfers between devices: 34.4 us -> none  [the longest x1 18.7 us: per_device(): lax.all_to_all(expert_outputs, 'expert', split_axis=0, concat_axis=0, til...]
    ppermute x0 -> x14, waiting for transfers between devices: none -> 31.8 us  [swap(): lax.ppermute(value, axis, [(i, i ^ k) for i in range(lax.axis_size(axis))])]
    all_to_all x1 -> x0, blocking collectives: 25.8 us -> none  [per_device(): lax.all_to_all(send_rows, 'expert', split_axis=0, concat_axis=0, tiled=True)]
    ppermute x0 -> x14, starting transfers between devices: none -> 23 us  [swap(): lax.ppermute(value, axis, [(i, i ^ k) for i in range(lax.axis_size(axis))])]
    dot_general x5 -> x0, matrix products: 14.1 us -> none  [the longest x1 5.88 us: per_device(): lax.dot_general(token_rows, preact_grad, (((0,), (0,)), ((), ())), prefer...]
    pallas_call x0 -> x7, Pallas kernels: none -> 13.8 us  [the longest x1 5.08 us: per_device(): call(functools.partial(expert_forward, experts), [shape((capacity, hidden...]
    gather x3 -> x0, local copies, waits for them, and re-layouts: 8.96 us -> none  [the longest x1 3.18 us: per_device(): send_grads = jnp.where(valid_slot, pair_grads[pair_index], zero_value)]
    all_to_all x2 -> x0, starting transfers between devices: 8.24 us -> none  [the longest x1 4.35 us: per_device(): lax.all_to_all(send_grads, 'expert', split_axis=0, concat_axis=0, tiled=T...]
  transfers between devices with their start and end apart: 3 -> 14, of which waited for: 3 -> 8; matrix products, arithmetic and copies ran while one was open for 13% -> 1% of each run, Pallas kernels for 0% -> 10%
where the time goes in v1:
time: 76.7 us; the launch traced here: 76.3 us
  waiting for transfers between devices  31.8 us (41%)
  starting transfers between devices  23 us (30%)
  Pallas kernels  13.8 us (18%)
  local copies, waits for them, and re-layouts  7.01 us (9%)
    ppermute x14, waiting for transfers between devices, swap(): lax.ppermute(value, axis, [(i, i ^ k) for i in range(lax.axis_size(axis))])  31.8 us
    ppermute x14, starting transfers between devices, swap(): lax.ppermute(value, axis, [(i, i ^ k) for i in range(lax.axis_size(axis))])  23 us
    unnamed x18, local copies, waits for them, and re-layouts  6.3 us
    pallas_call x1, Pallas kernels, per_device(): call(functools.partial(expert_forward, experts), [shape((capacity, hidden...  5.08 us
    pallas_call x1, Pallas kernels, per_device(): call(functools.partial(weight_grads_packed, experts, replicas), [shape(pa...  3.47 us
    pallas_call x1, Pallas kernels, per_device(): call(functools.partial(combine, experts), shape((tokens, width), BF16))  1.9 us
    pallas_call x1, Pallas kernels, per_device(): call(functools.partial(attend, experts, len(memories)), [shape((tokens, w...  1.63 us
  transfers between devices with their start and end apart: 14, of which 8 were waited for; matrix products, arithmetic and copies ran while one was open for 1% of the time, Pallas kernels for 10%

profile of v1, /device:TPU:0, one launch (start us, length us, event | category | flops | bytes accessed | tf_op | source)
XLA Modules:
  0.0 76.3 jit_solution(9126656043293794158)
XLA Ops:
  0.6 0.0 copy-start
  0.6 0.5 collective-permute-start
  1.2 0.7 broadcast_in_dim.3.refs_5_
  1.9 0.5 collective-permute-done.refs_3_
  2.4 0.0 copy-start.2
  2.4 1.1 %copy-done.2 = bf16[128,2560]{1,0:T(8,128)(2,1)S(1)} copy-done((bf16[128,2560]{1,0:T(8,128)(2,1)S(1)}, bf16[128,2560]{1,0:T(8,128)(2,1)}, u32[]{:S(2)}) %copy-start.2) | copy-done | bytes 655384
  3.5 0.0 copy-start.3
  3.5 1.1 %copy-done.3 = bf16[128,2560]{1,0:T(8,128)(2,1)S(1)} copy-done((bf16[128,2560]{1,0:T(8,128)(2,1)S(1)}, bf16[128,2560]{1,0:T(8,128)(2,1)}, u32[]{:S(2)}) %copy-start.3) | copy-done | bytes 655384
  4.6 0.0 copy-start.5
  4.6 0.9 %copy-done.5 = bf16[2,16,2560]{2,1,0:T(8,128)(2,1)S(1)} copy-done((bf16[2,16,2560]{2,1,0:T(8,128)(2,1)S(1)}, bf16[2,16,2560]{2,1,0:T(8,128)(2,1)}, u32[]{:S(2)}) %copy-start.5) | copy-done | bytes 163864
  5.5 0.0 copy-start.6
  5.5 0.7 copy-done.6
  6.2 0.0 copy-start.8
  6.2 1.6 %shard_map.104 = (f32[128,2560]{1,0:T(8,128)S(1)}, bf16[80,2560]{1,0:T(8,128)(2,1)S(1)}, bf16[80,2560]{1,0:T(8,128)(2,1)S(1)}, bf16[80,2560]{1,0:T(8,128)(2,1)S(1)}, bf16[80,2560]{1,0:T(8,128)(2,1)S(1)}) custom-call(s32[2,128]{1,0:T(2,128)S(1)} %bitcast.9, bf16[128,2560]{1,0:T(8,128)(2,1)S(1)} %copy-done.2, bf16[2,16,2560]{2,1,0:T(8,128)(2,1)S(1)} %copy-done.5, ...), custom_call_target="tpu_custom_call" | custom-call | tf_op jit(solution)/shard_map/pallas_call | solution.py:263
  7.8 2.9 %collective-permute-start.1 = (bf16[80,2560]{1,0:T(8,128)(2,1)S(1)}, bf16[80,2560]{1,0:T(8,128)(2,1)S(1)}, u32[]{:S(2)}, u32[]{:S(2)}) collective-permute-start(bf16[80,2560]{1,0:T(8,128)(2,1)S(1)} %get-tuple-element.27), channel_id=1, source_target_pairs={{0,2},{2,0},{4,6},{6,4},{1,3},{3,1},{5,7},{7,5},{8,10},{10,8},{12,... | collective-permute-start | bytes 1228808 | tf_op jit(solution)/shard_map/ppermute | solution.py:242
  10.7 1.5 %collective-permute-start.2 = (bf16[80,2560]{1,0:T(8,128)(2,1)S(1)}, bf16[80,2560]{1,0:T(8,128)(2,1)S(1)}, u32[]{:S(2)}, u32[]{:S(2)}) collective-permute-start(bf16[80,2560]{1,0:T(8,128)(2,1)S(1)} %get-tuple-element.28), channel_id=1, source_target_pairs={{0,4},{2,6},{4,0},{6,2},{1,5},{3,7},{5,1},{7,3},{8,12},{10,14},{12... | collective-permute-start | bytes 1228808 | tf_op jit(solution)/shard_map/ppermute | solution.py:242
  12.2 0.0 collective-permute-start.3
  12.3 0.0 copy-done.8
  12.3 0.0 copy-start.4
  12.3 1.1 %copy-done.4 = bf16[128,2560]{1,0:T(8,128)(2,1)S(1)} copy-done((bf16[128,2560]{1,0:T(8,128)(2,1)S(1)}, bf16[128,2560]{1,0:T(8,128)(2,1)}, u32[]{:S(2)}) %copy-start.4) | copy-done | bytes 655384
  13.4 0.7 shard_map.107
  14.1 2.0 %collective-permute-start.7 = (bf16[80,2560]{1,0:T(8,128)(2,1)S(1)}, bf16[80,2560]{1,0:T(8,128)(2,1)S(1)}, u32[]{:S(2)}, u32[]{:S(2)}) collective-permute-start(bf16[80,2560]{1,0:T(8,128)(2,1)S(1)} %get-tuple-element.35), channel_id=1, source_target_pairs={{0,2},{2,0},{4,6},{6,4},{1,3},{3,1},{5,7},{7,5},{8,10},{10,8},{12,... | collective-permute-start | bytes 1228808 | tf_op jit(solution)/shard_map/ppermute | solution.py:242
  16.1 1.5 %collective-permute-start.8 = (bf16[80,2560]{1,0:T(8,128)(2,1)S(1)}, bf16[80,2560]{1,0:T(8,128)(2,1)S(1)}, u32[]{:S(2)}, u32[]{:S(2)}) collective-permute-start(bf16[80,2560]{1,0:T(8,128)(2,1)S(1)} %get-tuple-element.36), channel_id=1, source_target_pairs={{0,4},{2,6},{4,0},{6,2},{1,5},{3,7},{5,1},{7,3},{8,12},{10,14},{12... | collective-permute-start | bytes 1228808 | tf_op jit(solution)/shard_map/ppermute | solution.py:242
  17.6 3.4 %collective-permute-done.1.refs_1_ = bf16[80,2560]{1,0:T(8,128)(2,1)S(1)} collective-permute-done((bf16[80,2560]{1,0:T(8,128)(2,1)S(1)}, bf16[80,2560]{1,0:T(8,128)(2,1)S(1)}, u32[]{:S(2)}, u32[]{:S(2)}) %collective-permute-start.1) | collective-permute-done | bytes 409632 | tf_op jit(solution)/shard_map/ppermute | solution.py:242
  21.0 3.0 %collective-permute-start.9 = (bf16[80,2560]{1,0:T(8,128)(2,1)S(1)}, bf16[80,2560]{1,0:T(8,128)(2,1)S(1)}, u32[]{:S(2)}, u32[]{:S(2)}) collective-permute-start(bf16[80,2560]{1,0:T(8,128)(2,1)S(1)} %get-tuple-element.37), channel_id=1, source_target_pairs={{0,6},{2,4},{4,2},{6,0},{1,7},{3,5},{5,3},{7,1},{8,14},{10,12},{12... | collective-permute-start | bytes 1228808 | tf_op jit(solution)/shard_map/ppermute | solution.py:242
  24.0 7.9 %collective-permute-done.2.refs_2_ = bf16[80,2560]{1,0:T(8,128)(2,1)S(1)} collective-permute-done((bf16[80,2560]{1,0:T(8,128)(2,1)S(1)}, bf16[80,2560]{1,0:T(8,128)(2,1)S(1)}, u32[]{:S(2)}, u32[]{:S(2)}) %collective-permute-start.2) | collective-permute-done | bytes 409632 | tf_op jit(solution)/shard_map/ppermute | solution.py:242
  31.9 0.0 collective-permute-done.3.refs_3_
  31.9 0.0 copy-done
  31.9 0.0 copy-start.1
  31.9 1.4 %copy-done.1 = bf16[1,2560,320]{1,2,0:T(8,128)(2,1)S(1)} copy-done((bf16[1,2560,320]{1,2,0:T(8,128)(2,1)S(1)}, bf16[1,2560,320]{1,2,0:T(8,128)(2,1)}, u32[]{:S(2)}) %copy-start.1) | copy-done | bytes 1638424
  33.3 5.1 %shard_map.105 = (f32[80,320]{1,0:T(8,128)S(1)}, f32[80,320]{1,0:T(8,128)S(1)}, f32[80,320]{1,0:T(8,128)S(1)}, f32[80,320]{1,0:T(8,128)S(1)}, bf16[80,2560]{1,0:...) custom-call(bf16[80,2560]{1,0:T(8,128)(2,1)S(1)} %get-tuple-element.26.r, ...), custom_call_target="tpu_custom_call" | custom-call | tf_op jit(solution)/shard_map/pallas_call | solution.py:269
  38.4 0.2 collective-permute-done.7.refs_5_
  38.6 9.7 %collective-permute-done.8.refs_6_ = bf16[80,2560]{1,0:T(8,128)(2,1)S(1)} collective-permute-done((bf16[80,2560]{1,0:T(8,128)(2,1)S(1)}, bf16[80,2560]{1,0:T(8,128)(2,1)S(1)}, u32[]{:S(2)}, u32[]{:S(2)}) %collective-permute-start.8) | collective-permute-done | bytes 409632 | tf_op jit(solution)/shard_map/ppermute | solution.py:242
  48.3 0.0 collective-permute-done.9.refs_7_
  48.3 3.5 %shard_map.108 = (f32[4,800,128]{2,1,0:T(8,128)S(1)}, bf16[4,800,128]{2,1,0:T(8,128)(2,1)S(1)}) custom-call(bf16[80,2560]{1,0:T(8,128)(2,1)S(1)} %get-tuple-element.26.refs_0_, bf16[80,2560]{1,0:T(8,128)(2,1)S(1)} %collective-permute-done.1.refs_1_, bf16[80,2560]{1,0:T(8,128)(2,1)S(1)} %collective-permute-done.2.refs_2_, ...), custom_call_target="tpu_custom_call" | custom-call | tf_op jit(solution)/shard_map/pallas_call | solution.py:279
  51.8 0.0 copy-start.7
  51.8 0.1 collective-permute-start.10
  51.9 1.3 %collective-permute-start.4 = (bf16[80,2560]{1,0:T(8,128)(2,1)S(1)}, bf16[80,2560]{1,0:T(8,128)(2,1)S(1)}, u32[]{:S(2)}, u32[]{:S(2)}) collective-permute-start(bf16[80,2560]{1,0:T(8,128)(2,1)S(1)} %get-tuple-element.31), channel_id=1, source_target_pairs={{0,2},{2,0},{4,6},{6,4},{1,3},{3,1},{5,7},{7,5},{8,10},{10,8},{12,... | collective-permute-start | bytes 1228808 | tf_op jit(solution)/shard_map/ppermute | solution.py:242
  53.2 0.8 %collective-permute-start.5 = (bf16[80,2560]{1,0:T(8,128)(2,1)S(1)}, bf16[80,2560]{1,0:T(8,128)(2,1)S(1)}, u32[]{:S(2)}, u32[]{:S(2)}) collective-permute-start(bf16[80,2560]{1,0:T(8,128)(2,1)S(1)} %get-tuple-element.32), channel_id=1, source_target_pairs={{0,4},{2,6},{4,0},{6,2},{1,5},{3,7},{5,1},{7,3},{8,12},{10,14},{12... | collective-permute-start | bytes 1228808 | tf_op jit(solution)/shard_map/ppermute | solution.py:242
  54.0 1.4 %collective-permute-start.6 = (bf16[80,2560]{1,0:T(8,128)(2,1)S(1)}, bf16[80,2560]{1,0:T(8,128)(2,1)S(1)}, u32[]{:S(2)}, u32[]{:S(2)}) collective-permute-start(bf16[80,2560]{1,0:T(8,128)(2,1)S(1)} %get-tuple-element.33), channel_id=1, source_target_pairs={{0,6},{2,4},{4,2},{6,0},{1,7},{3,5},{5,3},{7,1},{8,14},{10,12},{12... | collective-permute-start | bytes 1228808 | tf_op jit(solution)/shard_map/ppermute | solution.py:242
  55.4 0.0 collective-permute-done.10.other_ref
  55.4 0.2 shard_map.109
  55.6 1.6 %collective-permute-start.11 = (bf16[800,128]{1,0:T(8,128)(2,1)S(1)}, bf16[800,128]{1,0:T(8,128)(2,1)S(1)}, u32[]{:S(2)}, u32[]{:S(2)}) collective-permute-start(bf16[800,128]{1,0:T(8,128)(2,1)S(1)} %get-tuple-element.45), channel_id=1, source_target_pairs={{0,8},{8,0},{16,24},{24,16},{1,9},{9,1},{17,25},{25,17},{2,10},{10... | collective-permute-start | bytes 614408 | tf_op jit(solution)/shard_map/ppermute | solution.py:242
  57.2 2.6 %collective-permute-start.12 = (bf16[800,128]{1,0:T(8,128)(2,1)S(1)}, bf16[800,128]{1,0:T(8,128)(2,1)S(1)}, u32[]{:S(2)}, u32[]{:S(2)}) collective-permute-start(bf16[800,128]{1,0:T(8,128)(2,1)S(1)} %get-tuple-element.46), channel_id=1, source_target_pairs={{0,16},{8,24},{16,0},{24,8},{1,17},{9,25},{17,1},{25,9},{2,18},{10... | collective-permute-start | bytes 614408 | tf_op jit(solution)/shard_map/ppermute | solution.py:242
  59.8 4.4 %collective-permute-done.4.refs_1_ = bf16[80,2560]{1,0:T(8,128)(2,1)S(1)} collective-permute-done((bf16[80,2560]{1,0:T(8,128)(2,1)S(1)}, bf16[80,2560]{1,0:T(8,128)(2,1)S(1)}, u32[]{:S(2)}, u32[]{:S(2)}) %collective-permute-start.4) | collective-permute-done | bytes 409632 | tf_op jit(solution)/shard_map/ppermute | solution.py:242
  64.2 3.6 %collective-permute-start.13 = (bf16[800,128]{1,0:T(8,128)(2,1)S(1)}, bf16[800,128]{1,0:T(8,128)(2,1)S(1)}, u32[]{:S(2)}, u32[]{:S(2)}) collective-permute-start(bf16[800,128]{1,0:T(8,128)(2,1)S(1)} %get-tuple-element.47), channel_id=1, source_target_pairs={{0,24},{8,16},{16,8},{24,0},{1,25},{9,17},{17,9},{25,1},{2,26},{10... | collective-permute-start | bytes 614408 | tf_op jit(solution)/shard_map/ppermute | solution.py:242
  67.8 4.0 %collective-permute-done.5.refs_2_ = bf16[80,2560]{1,0:T(8,128)(2,1)S(1)} collective-permute-done((bf16[80,2560]{1,0:T(8,128)(2,1)S(1)}, bf16[80,2560]{1,0:T(8,128)(2,1)S(1)}, u32[]{:S(2)}, u32[]{:S(2)}) %collective-permute-start.5) | collective-permute-done | bytes 409632 | tf_op jit(solution)/shard_map/ppermute | solution.py:242
  71.8 1.7 %collective-permute-done.6.refs_3_ = bf16[80,2560]{1,0:T(8,128)(2,1)S(1)} collective-permute-done((bf16[80,2560]{1,0:T(8,128)(2,1)S(1)}, bf16[80,2560]{1,0:T(8,128)(2,1)S(1)}, u32[]{:S(2)}, u32[]{:S(2)}) %collective-permute-start.6) | collective-permute-done | bytes 409632 | tf_op jit(solution)/shard_map/ppermute | solution.py:242
  73.5 0.0 copy-done.7
  73.5 1.9 %shard_map.106 = bf16[128,2560]{1,0:T(8,128)(2,1)} custom-call(s32[2,128]{1,0:T(2,128)S(1)} %bitcast.11, f32[2,128]{1,0:T(2,128)S(1)} %bitcast.13, f32[128,2560]{1,0:T(8,128)S(1)} %get-tuple-element.25.stream_ref, bf16[80,2560]{1,0:T(8,128)(2,1)S(1)} %get-tuple-element.30.refs_0_, bf16[80,2560]{1,0:T(8,128)(2,1)S(1)} %collective-permute-done.4.refs_1_, ...), custom_call_target="tpu_custom_call" | custom-call | tf_op jit(solution)/shard_map/pallas_call | solution.py:295
  75.4 0.0 collective-permute-done.11.refs_0_
  75.4 0.0 collective-permute-done.12.refs_1_
  75.4 0.0 collective-permute-done.13.refs_2_
  75.4 0.9 %shard_map.110 = f32[1,320,320]{2,1,0:T(8,128)} custom-call(f32[800,128]{1,0:T(8,128)S(1)} %get-tuple-element.44.own_ref, bf16[800,128]{1,0:T(8,128)(2,1)S(1)} %collective-permute-done.11.refs_0_, bf16[800,128]{1,0:T(8,128)(2,1)S(1)} %collective-permute-done.12.refs_1_, bf16[800,128]{1,0:T(8,128)(2,1)S(1)} %collective-permute-done.13.refs_2_), custom_call_target="tpu_custom_call" | custom-call | tf_op jit(solution)/shard_map/pallas_call | solution.py:288
Async XLA Ops:
  0.6 31.2 %copy-start = (bf16[1,320,2560]{2,1,0:T(8,128)(2,1)S(1)}, bf16[1,320,2560]{2,1,0:T(8,128)(2,1)}, u32[]{:S(2)}) copy-start(bf16[1,320,2560]{2,1,0:T(8,128)(2,1)} %param.16) | copy-start | bytes 4915204
  0.6 1.8 %collective-permute-start = (bf16[2,16,2560]{2,1,0:T(8,128)(2,1)}, bf16[2,16,2560]{2,1,0:T(8,128)(2,1)S(1)}, u32[]{:S(2)}, u32[]{:S(2)}) collective-permute-start(bf16[2,16,2560]{2,1,0:T(8,128)(2,1)} %refs_2_.1), channel_id=1, source_target_pairs={{0,1},{1,0},{2,3},{3,2},{4,5},{5,4},{6,7},{7,6},{8,9},{9,8},{10,11... | collective-permute-start | bytes 491528 | tf_op jit(solution)/shard_map/ppermute | solution.py:242
  2.4 1.1 %copy-start.2 = (bf16[128,2560]{1,0:T(8,128)(2,1)S(1)}, bf16[128,2560]{1,0:T(8,128)(2,1)}, u32[]{:S(2)}) copy-start(bf16[128,2560]{1,0:T(8,128)(2,1)} %refs_1_.1) | copy-start | bytes 1966084
  3.5 1.1 %copy-start.3 = (bf16[128,2560]{1,0:T(8,128)(2,1)S(1)}, bf16[128,2560]{1,0:T(8,128)(2,1)}, u32[]{:S(2)}) copy-start(bf16[128,2560]{1,0:T(8,128)(2,1)} %refs_4_.1) | copy-start | bytes 1966084
  4.6 0.9 %copy-start.5 = (bf16[2,16,2560]{2,1,0:T(8,128)(2,1)S(1)}, bf16[2,16,2560]{2,1,0:T(8,128)(2,1)}, u32[]{:S(2)}) copy-start(bf16[2,16,2560]{2,1,0:T(8,128)(2,1)} %refs_2_.1) | copy-start | bytes 491524
  5.5 0.7 copy-start.6
  6.2 6.1 %copy-start.8 = (f32[128,2]{0,1:T(2,128)S(1)}, f32[128,2]{0,1:T(2,128)}, u32[]{:S(2)}) copy-start(f32[128,2]{0,1:T(2,128)} %param.14) | copy-start | bytes 3076
  7.8 13.2 %collective-permute-start.1 = (bf16[80,2560]{1,0:T(8,128)(2,1)S(1)}, bf16[80,2560]{1,0:T(8,128)(2,1)S(1)}, u32[]{:S(2)}, u32[]{:S(2)}) collective-permute-start(bf16[80,2560]{1,0:T(8,128)(2,1)S(1)} %get-tuple-element.27), channel_id=1, source_target_pairs={{0,2},{2,0},{4,6},{6,4},{1,3},{3,1},{5,7},{7,5},{8,10},{10,8},{12,... | collective-permute-start | bytes 1228808 | tf_op jit(solution)/shard_map/ppermute | solution.py:242
  10.7 21.1 %collective-permute-start.2 = (bf16[80,2560]{1,0:T(8,128)(2,1)S(1)}, bf16[80,2560]{1,0:T(8,128)(2,1)S(1)}, u32[]{:S(2)}, u32[]{:S(2)}) collective-permute-start(bf16[80,2560]{1,0:T(8,128)(2,1)S(1)} %get-tuple-element.28), channel_id=1, source_target_pairs={{0,4},{2,6},{4,0},{6,2},{1,5},{3,7},{5,1},{7,3},{8,12},{10,14},{12... | collective-permute-start | bytes 1228808 | tf_op jit(solution)/shard_map/ppermute | solution.py:242
  12.2 19.6 %collective-permute-start.3 = (bf16[80,2560]{1,0:T(8,128)(2,1)S(1)}, bf16[80,2560]{1,0:T(8,128)(2,1)S(1)}, u32[]{:S(2)}, u32[]{:S(2)}) collective-permute-start(bf16[80,2560]{1,0:T(8,128)(2,1)S(1)} %get-tuple-element.29), channel_id=1, source_target_pairs={{0,6},{2,4},{4,2},{6,0},{1,7},{3,5},{5,3},{7,1},{8,14},{10,12},{12... | collective-permute-start | bytes 1228808 | tf_op jit(solution)/shard_map/ppermute | solution.py:242
  12.3 1.1 %copy-start.4 = (bf16[128,2560]{1,0:T(8,128)(2,1)S(1)}, bf16[128,2560]{1,0:T(8,128)(2,1)}, u32[]{:S(2)}) copy-start(bf16[128,2560]{1,0:T(8,128)(2,1)} %grad_ref.1) | copy-start | bytes 1966084
  14.1 24.5 %collective-permute-start.7 = (bf16[80,2560]{1,0:T(8,128)(2,1)S(1)}, bf16[80,2560]{1,0:T(8,128)(2,1)S(1)}, u32[]{:S(2)}, u32[]{:S(2)}) collective-permute-start(bf16[80,2560]{1,0:T(8,128)(2,1)S(1)} %get-tuple-element.35), channel_id=1, source_target_pairs={{0,2},{2,0},{4,6},{6,4},{1,3},{3,1},{5,7},{7,5},{8,10},{10,8},{12,... | collective-permute-start | bytes 1228808 | tf_op jit(solution)/shard_map/ppermute | solution.py:242
  16.1 32.2 %collective-permute-start.8 = (bf16[80,2560]{1,0:T(8,128)(2,1)S(1)}, bf16[80,2560]{1,0:T(8,128)(2,1)S(1)}, u32[]{:S(2)}, u32[]{:S(2)}) collective-permute-start(bf16[80,2560]{1,0:T(8,128)(2,1)S(1)} %get-tuple-element.36), channel_id=1, source_target_pairs={{0,4},{2,6},{4,0},{6,2},{1,5},{3,7},{5,1},{7,3},{8,12},{10,14},{12... | collective-permute-start | bytes 1228808 | tf_op jit(solution)/shard_map/ppermute | solution.py:242
  21.0 27.3 %collective-permute-start.9 = (bf16[80,2560]{1,0:T(8,128)(2,1)S(1)}, bf16[80,2560]{1,0:T(8,128)(2,1)S(1)}, u32[]{:S(2)}, u32[]{:S(2)}) collective-permute-start(bf16[80,2560]{1,0:T(8,128)(2,1)S(1)} %get-tuple-element.37), channel_id=1, source_target_pairs={{0,6},{2,4},{4,2},{6,0},{1,7},{3,5},{5,3},{7,1},{8,14},{10,12},{12... | collective-permute-start | bytes 1228808 | tf_op jit(solution)/shard_map/ppermute | solution.py:242
  31.9 1.4 %copy-start.1 = (bf16[1,2560,320]{1,2,0:T(8,128)(2,1)S(1)}, bf16[1,2560,320]{1,2,0:T(8,128)(2,1)}, u32[]{:S(2)}) copy-start(bf16[1,2560,320]{1,2,0:T(8,128)(2,1)} %param.15) | copy-start | bytes 4915204
  51.8 21.7 %copy-start.7 = (s32[128,2]{0,1:T(2,128)S(1)}, s32[128,2]{0,1:T(2,128)}, u32[]{:S(2)}) copy-start(s32[128,2]{0,1:T(2,128)} %param.13) | copy-start | bytes 3076
  51.8 3.6 %collective-permute-start.10 = (bf16[4,800,128]{2,1,0:T(8,128)(2,1)S(1)}, bf16[4,800,128]{2,1,0:T(8,128)(2,1)S(1)}, u32[]{:S(2)}, u32[]{:S(2)}) collective-permute-start(bf16[4,800,128]{2,1,0:T(8,128)(2,1)S(1)} %get-tuple-element.43), channel_id=1, source_target_pairs={{0,1},{1,0},{2,3},{3,2},{4,5},{5,4},{6,7},{7,6},{8,9},{9,8},{10,11... | collective-permute-start | bytes 2457608 | tf_op jit(solution)/shard_map/ppermute | solution.py:242
  51.9 12.3 %collective-permute-start.4 = (bf16[80,2560]{1,0:T(8,128)(2,1)S(1)}, bf16[80,2560]{1,0:T(8,128)(2,1)S(1)}, u32[]{:S(2)}, u32[]{:S(2)}) collective-permute-start(bf16[80,2560]{1,0:T(8,128)(2,1)S(1)} %get-tuple-element.31), channel_id=1, source_target_pairs={{0,2},{2,0},{4,6},{6,4},{1,3},{3,1},{5,7},{7,5},{8,10},{10,8},{12,... | collective-permute-start | bytes 1228808 | tf_op jit(solution)/shard_map/ppermute | solution.py:242
  53.2 18.6 %collective-permute-start.5 = (bf16[80,2560]{1,0:T(8,128)(2,1)S(1)}, bf16[80,2560]{1,0:T(8,128)(2,1)S(1)}, u32[]{:S(2)}, u32[]{:S(2)}) collective-permute-start(bf16[80,2560]{1,0:T(8,128)(2,1)S(1)} %get-tuple-element.32), channel_id=1, source_target_pairs={{0,4},{2,6},{4,0},{6,2},{1,5},{3,7},{5,1},{7,3},{8,12},{10,14},{12... | collective-permute-start | bytes 1228808 | tf_op jit(solution)/shard_map/ppermute | solution.py:242
  54.0 19.5 %collective-permute-start.6 = (bf16[80,2560]{1,0:T(8,128)(2,1)S(1)}, bf16[80,2560]{1,0:T(8,128)(2,1)S(1)}, u32[]{:S(2)}, u32[]{:S(2)}) collective-permute-start(bf16[80,2560]{1,0:T(8,128)(2,1)S(1)} %get-tuple-element.33), channel_id=1, source_target_pairs={{0,6},{2,4},{4,2},{6,0},{1,7},{3,5},{5,3},{7,1},{8,14},{10,12},{12... | collective-permute-start | bytes 1228808 | tf_op jit(solution)/shard_map/ppermute | solution.py:242
  55.6 19.8 %collective-permute-start.11 = (bf16[800,128]{1,0:T(8,128)(2,1)S(1)}, bf16[800,128]{1,0:T(8,128)(2,1)S(1)}, u32[]{:S(2)}, u32[]{:S(2)}) collective-permute-start(bf16[800,128]{1,0:T(8,128)(2,1)S(1)} %get-tuple-element.45), channel_id=1, source_target_pairs={{0,8},{8,0},{16,24},{24,16},{1,9},{9,1},{17,25},{25,17},{2,10},{10... | collective-permute-start | bytes 614408 | tf_op jit(solution)/shard_map/ppermute | solution.py:242
  57.2 18.2 %collective-permute-start.12 = (bf16[800,128]{1,0:T(8,128)(2,1)S(1)}, bf16[800,128]{1,0:T(8,128)(2,1)S(1)}, u32[]{:S(2)}, u32[]{:S(2)}) collective-permute-start(bf16[800,128]{1,0:T(8,128)(2,1)S(1)} %get-tuple-element.46), channel_id=1, source_target_pairs={{0,16},{8,24},{16,0},{24,8},{1,17},{9,25},{17,1},{25,9},{2,18},{10... | collective-permute-start | bytes 614408 | tf_op jit(solution)/shard_map/ppermute | solution.py:242
  64.2 11.2 %collective-permute-start.13 = (bf16[800,128]{1,0:T(8,128)(2,1)S(1)}, bf16[800,128]{1,0:T(8,128)(2,1)S(1)}, u32[]{:S(2)}, u32[]{:S(2)}) collective-permute-start(bf16[800,128]{1,0:T(8,128)(2,1)S(1)} %get-tuple-element.47), channel_id=1, source_target_pairs={{0,24},{8,16},{16,8},{24,0},{1,25},{9,17},{17,9},{25,1},{2,26},{10... | collective-permute-start | bytes 614408 | tf_op jit(solution)/shard_map/ppermute | solution.py:242

commit v2 on v1

v2 whole, which is shorter than its diff:
```python
import functools

import jax
import jax.numpy as jnp
from jax import lax
from jax.experimental import pallas as pl
from jax.experimental.pallas import tpu as pltpu
from jax.sharding import PartitionSpec as P

HEAD_SIZE = 64
GROUP = 256
CHUNK = 512
VMEM_LIMIT = 24 * 1024 * 1024
GELU_C = 0.7978845608028654
GELU_A = 0.044715
BF16 = jnp.bfloat16
F32 = jnp.float32


def params():
    return pltpu.CompilerParams(vmem_limit_bytes=VMEM_LIMIT)


def call(kernel, out_shapes, scratch=(), inputs=None):
    specs = {} if inputs is None else {"in_specs": [pl.BlockSpec(memory_space=at) for at in inputs]}
    return pl.pallas_call(
        kernel,
        out_shape=out_shapes,
        scratch_shapes=list(scratch),
        compiler_params=params(),
        **specs,
    )


def shape(dims, dtype):
    return jax.ShapeDtypeStruct(dims, dtype)


def one_hot(slots, k, capacity):
    tokens = slots.shape[1]
    return lax.broadcasted_iota(jnp.int32, (capacity, tokens), 0) == slots[k : k + 1, :]


def as_bf16(mask):
    return jnp.where(mask, 1.0, 0.0).astype(BF16)


def start_columns(source, target, sems):
    copies = []
    for at in range(0, target.shape[1], CHUNK):
        cols = pl.ds(at, CHUNK)
        copies.append(
            pltpu.make_async_copy(source.at[:, cols], target.at[:, cols], sems.at[at // CHUNK])
        )
        copies[-1].start()
    return copies


def dispatch_grads(count, ids_ref, gates_ref, grad_hbm, *refs):
    out_refs = refs[:count]
    slots_ref, table_ref, grad_ref, sems = refs[count:]
    width = grad_ref.shape[1]
    copies = start_columns(grad_hbm, grad_ref, sems)
    slots, first = slots_from(ids_ref[...])
    slots_ref[...] = slots
    gates = jnp.where(first, gates_ref[0:1, :], gates_ref[1:2, :])
    table_ref[...] = gates
    masks = [one_hot(slots, k, out_refs[k].shape[0]) for k in range(count)]
    picks = [as_bf16(mask) for mask in masks]
    scales = [
        jnp.sum(jnp.where(masks[k], gates[k : k + 1, :], 0.0), axis=1, keepdims=True)
        for k in range(count)
    ]
    for at in range(0, width, CHUNK):
        cols = slice(at, at + CHUNK)
        copies[at // CHUNK].wait()
        for k in range(count):
            rows = jnp.dot(picks[k], grad_ref[:, cols], preferred_element_type=F32)
            out_refs[k][:, cols] = (rows * scales[k]).astype(BF16)


def attend(parts, *refs):
    query_hbm, residual_hbm, gain_hbm, own_hbm = refs[0:4]
    other_refs = refs[4 : 3 + parts]
    stream_ref, left_ref, right_ref = refs[3 + parts : 6 + parts]
    query_ref, residual_ref, gain_ref, own_ref = refs[6 + parts : 10 + parts]
    query_sems, residual_sems, gain_sem, own_sem = refs[10 + parts :]
    tokens, width = query_ref.shape
    own_copy = pltpu.make_async_copy(own_hbm, own_ref, own_sem)
    own_copy.start()
    query_copies = start_columns(query_hbm, query_ref, query_sems)
    residual_copies = start_columns(residual_hbm, residual_ref, residual_sems)
    gain_copy = pltpu.make_async_copy(gain_hbm, gain_ref, gain_sem)
    gain_copy.start()
    memory_refs = (own_ref,) + tuple(other_refs)
    heads = GROUP // HEAD_SIZE
    rows = sum(ref.shape[1] for ref in memory_refs)
    own = (
        lax.broadcasted_iota(jnp.int32, (heads * rows, GROUP), 0) // rows
        == lax.broadcasted_iota(jnp.int32, (heads * rows, GROUP), 1) // HEAD_SIZE
    )
    total = jnp.zeros((tokens, 1), F32)

    def spread(which, cols):
        piece = jnp.concatenate([ref[which, :, cols] for ref in memory_refs], axis=0)
        return jnp.where(own, jnp.concatenate([piece] * heads, axis=0), jnp.zeros((), BF16))

    own_copy.wait()
    for at in range(0, width, GROUP):
        cols = slice(at, at + GROUP)
        if at % CHUNK == 0:
            query_copies[at // CHUNK].wait()
            residual_copies[at // CHUNK].wait()
        scores = lax.dot_general(
            spread(0, cols), query_ref[:, cols], (((1,), (1,)), ((), ())), preferred_element_type=F32
        ) * HEAD_SIZE ** (-0.5)
        scores = scores.reshape(heads, rows, tokens)
        exponent = jnp.exp(scores - jnp.max(scores, axis=1, keepdims=True))
        probs = exponent / jnp.sum(exponent, axis=1, keepdims=True)
        attended = lax.dot_general(
            probs.reshape(heads * rows, tokens).astype(BF16),
            spread(1, cols),
            (((0,), (0,)), ((), ())),
            preferred_element_type=F32,
        ).astype(BF16)
        stream = residual_ref[:, cols].astype(F32) + attended.astype(F32)
        stream_ref[:, cols] = stream
        total = total + jnp.sum(stream * stream, axis=1, keepdims=True)
    gain_copy.wait()
    scale = lax.rsqrt(total / width + 1e-06)
    half = width // 2
    for at in range(0, width, GROUP):
        cols = slice(at, at + GROUP)
        gain = gain_ref[cols].reshape(1, GROUP)
        piece = (stream_ref[:, cols] * scale * gain).astype(BF16)
        if at < half:
            left_ref[:, cols] = piece
        else:
            right_ref[:, at - half : at - half + GROUP] = piece


def slots_from(ids):
    tokens = ids.shape[1]
    me = lax.axis_index("expert")
    expert = lax.broadcasted_iota(jnp.int32, (8, tokens), 0) ^ me
    first = ids[0:1, :] == expert
    chosen = first | (ids[1:2, :] == expert)
    earlier = lax.broadcasted_iota(jnp.int32, (tokens, tokens), 0) < lax.broadcasted_iota(
        jnp.int32, (tokens, tokens), 1
    )
    count = jnp.dot(as_bf16(chosen), as_bf16(earlier), preferred_element_type=F32)
    return jnp.where(chosen, count.astype(jnp.int32), -1), first


def split_grads(ids_hbm, gates_hbm, grad_hbm, left_ref, right_ref, ids_ref, gates_ref, sems):
    tokens, half = grad_hbm.shape[0], left_ref.shape[1]
    copies = [
        pltpu.make_async_copy(ids_hbm, ids_ref, sems.at[0]),
        pltpu.make_async_copy(gates_hbm, gates_ref, sems.at[1]),
    ]
    for side, target in enumerate((left_ref, right_ref)):
        for part in range(2):
            rows = pl.ds(part * (tokens // 2), tokens // 2)
            copies.append(
                pltpu.make_async_copy(
                    grad_hbm.at[rows, pl.ds(side * half, half)],
                    target.at[rows, :],
                    sems.at[2 + 2 * side + part],
                )
            )
    for copy in copies:
        copy.start()
    copies[0].wait()
    copies[1].wait()
    gates = gates_ref[...]
    high = gates.astype(BF16).astype(F32)
    middle = (gates - high).astype(BF16).astype(F32)
    low = gates - high - middle
    notes = jnp.concatenate(
        [ids_ref[...].astype(F32), high, middle, low, jnp.zeros((8, tokens), F32)], axis=0
    ).astype(BF16)
    for target in (left_ref, right_ref):
        target[tokens:, :] = jnp.zeros((16, half), BF16)
        target[tokens:, 0:tokens] = notes
    for copy in copies[2:]:
        copy.wait()


def notes_of(ref):
    tokens = ref.shape[0] - 16
    notes = ref[tokens:, 0:tokens].astype(F32)
    slots, first = slots_from(notes[0:2].astype(jnp.int32))
    gates = notes[2:4] + notes[4:6] + notes[6:8]
    return slots, jnp.where(first, gates[0:1, :], gates[1:2, :])


def relay(ref, slots, gates, k, out_ref, place):
    tokens = slots.shape[1]
    capacity = out_ref.shape[0] // 2
    mask = one_hot(slots, k, capacity)
    pick = as_bf16(mask)
    if gates is not None:
        gate = jnp.sum(jnp.where(mask, gates[k : k + 1, :], 0.0), axis=1, keepdims=True)
    for at in range(0, ref.shape[1], GROUP):
        cols = slice(at, at + GROUP)
        rows = jnp.dot(pick, ref[0:tokens, cols], preferred_element_type=F32)
        if gates is not None:
            rows = rows * gate
        out_ref[place * capacity : (place + 1) * capacity, cols] = rows.astype(BF16)


def relay_grads(left_ref, right_ref, x_ref, y_ref, *refs):
    pass_left, pass_right, here_left, here_right, slots_ref, gates_ref = refs
    own, own_gates = notes_of(left_ref)
    by_x, x_gates = notes_of(x_ref)
    by_y, y_gates = notes_of(y_ref)
    slots_ref[0:8, :], slots_ref[8:16, :], slots_ref[16:24, :] = own, by_x, by_y
    gates_ref[...] = own_gates
    relay(left_ref, own, own_gates, 2, pass_left, 0)
    relay(x_ref, by_x, x_gates, 2, pass_left, 1)
    relay(right_ref, own, own_gates, 1, pass_right, 0)
    relay(y_ref, by_y, y_gates, 1, pass_right, 1)
    relay(left_ref, own, own_gates, 0, here_left, 0)
    relay(x_ref, by_x, x_gates, 0, here_left, 1)
    relay(right_ref, own, own_gates, 0, here_right, 0)
    relay(y_ref, by_y, y_gates, 0, here_right, 1)


def relay_rows(left_ref, right_ref, x_ref, y_ref, slots_ref, *refs):
    pass_left, pass_right, here_left, here_right = refs
    own, by_x, by_y = slots_ref[0:8, :], slots_ref[8:16, :], slots_ref[16:24, :]
    relay(left_ref, own, None, 2, pass_left, 0)
    relay(x_ref, by_x, None, 2, pass_left, 1)
    relay(right_ref, own, None, 1, pass_right, 0)
    relay(y_ref, by_y, None, 1, pass_right, 1)
    relay(left_ref, own, None, 0, here_left, 0)
    relay(x_ref, by_x, None, 0, here_left, 1)
    relay(right_ref, own, None, 0, here_right, 0)
    relay(y_ref, by_y, None, 0, here_right, 1)


def narrow(left_refs, right_refs, matrix_ref):
    half = matrix_ref.shape[1] // 2

    def product(ref, at):
        return lax.dot_general(
            ref[...], matrix_ref[:, at : at + half], (((1,), (1,)), ((), ())), preferred_element_type=F32
        )

    left = [product(ref, 0) for ref in left_refs]
    right = [product(ref, half) for ref in right_refs]
    size = left[0].shape[0] // 2
    low, high = slice(0, size), slice(size, 2 * size)
    return [
        left[0][low] + right[0][low],
        left[0][high] + right[1][low],
        left[1][low] + right[0][high],
        left[1][high] + right[1][high],
    ]


def back_products(*refs):
    parts = narrow(refs[0:2], refs[2:4], refs[4])
    refs[5][...] = jnp.concatenate(parts, axis=0)


def activate(value):
    square = value * value
    curve = jnp.tanh(GELU_C * (value + GELU_A * square * value))
    hidden = (0.5 * value * (1.0 + curve)).astype(BF16)
    slope = 0.5 * (1.0 + curve) + 0.5 * value * (1.0 - curve * curve) * (
        GELU_C * (1.0 + 3.0 * GELU_A * square)
    )
    return hidden, slope


def experts_of_four(*refs):
    in_ref, out_ref = refs[4:6]
    result_refs, slope_ref = refs[6:10], refs[10]
    hidden, slope = activate(jnp.concatenate(narrow(refs[0:2], refs[2:4], in_ref), axis=0))
    slope_ref[...] = slope
    size = result_refs[0].shape[0]
    for at in range(0, out_ref.shape[1], CHUNK):
        cols = slice(at, at + CHUNK)
        rows = jnp.dot(hidden, out_ref[:, cols], preferred_element_type=F32).astype(BF16)
        for k in range(4):
            result_refs[k][:, cols] = rows[k * size : (k + 1) * size]


def gradient_halves(left_refs, right_refs, back_ref, slope_ref):
    grads = (back_ref[...] * slope_ref[...]).astype(BF16)
    size = grads.shape[0] // 4
    swapped = jnp.concatenate(
        [grads[k * size : (k + 1) * size] for k in (0, 2, 1, 3)], axis=0
    )
    halves = []
    for refs, part in ((left_refs, grads), (right_refs, swapped)):
        rows = jnp.concatenate([ref[...] for ref in refs], axis=0)
        halves.append(
            lax.dot_general(rows, part, (((0,), (0,)), ((), ())), preferred_element_type=F32)
        )
    return halves


def four_packed(shards, *refs):
    keep_ref, send_ref = refs[6:]
    halves = gradient_halves(refs[0:2], refs[2:4], refs[4], refs[5])
    block = halves[0].shape[0] // shards
    core = lax.axis_index("seq")
    for shard in range(shards):
        full = halves[2 * shard // shards]
        at = (2 * shard) % shards * block
        even = pack(full[at : at + block])
        odd = pack(full[at + block : at + 2 * block])
        keep_ref[shard] = jnp.where(core == 0, even, odd)
        send_ref[shard] = jnp.where(core == 0, odd, even).astype(BF16)


def four_whole(*refs):
    halves = gradient_halves(refs[0:2], refs[2:4], refs[4], refs[5])
    half = halves[0].shape[0]
    refs[6][0:half, :] = halves[0]
    refs[6][half:, :] = halves[1]


def dispatch_rows(count, slots_ref, left_ref, right_ref, *out_refs):
    half = left_ref.shape[1]
    slots = slots_ref[...]
    for k in range(count):
        pick = as_bf16(one_hot(slots, k, out_refs[k].shape[0]))
        for at in range(0, half, GROUP):
            cols = slice(at, at + GROUP)
            there = slice(half + at, half + at + GROUP)
            out_refs[k][:, cols] = jnp.dot(
                pick, left_ref[:, cols], preferred_element_type=F32
            ).astype(BF16)
            out_refs[k][:, there] = jnp.dot(
                pick, right_ref[:, cols], preferred_element_type=F32
            ).astype(BF16)


def forward(rows_ref, in_ref, out_ref, result_ref):
    hidden, slope = activate(
        lax.dot_general(
            rows_ref[...], in_ref[...], (((1,), (1,)), ((), ())), preferred_element_type=F32
        )
    )
    for at in range(0, out_ref.shape[1], CHUNK):
        cols = slice(at, at + CHUNK)
        result_ref[:, cols] = jnp.dot(
            hidden, out_ref[:, cols], preferred_element_type=F32
        ).astype(BF16)
    return slope


def hidden_grad(grad_ref, out_ref):
    return lax.dot_general(
        grad_ref[...], out_ref[...], (((1,), (1,)), ((), ())), preferred_element_type=F32
    )


def expert_first(count, *refs):
    rows_refs, grad_refs = refs[0:count], refs[count : 2 * count + 1]
    in_ref, out_ref = refs[2 * count + 1 : 2 * count + 3]
    result_refs = refs[2 * count + 3 : 3 * count + 3]
    back_refs, last_ref = refs[3 * count + 3 : 4 * count + 3], refs[4 * count + 3]
    for k in range(count):
        slope = forward(rows_refs[k], in_ref, out_ref, result_refs[k])
        back_refs[k][...] = (hidden_grad(grad_refs[k], out_ref) * slope).astype(BF16)
    last_ref[...] = hidden_grad(grad_refs[count], out_ref)


def expert_last(rows_ref, back_ref, in_ref, out_ref, result_ref, grad_ref):
    slope = forward(rows_ref, in_ref, out_ref, result_ref)
    grad_ref[...] = (back_ref[...] * slope).astype(BF16)


def sum_of_products(rows_refs, grad_refs):
    rows = jnp.concatenate([ref[...] for ref in rows_refs], axis=0)
    grads = jnp.concatenate([ref[...] for ref in grad_refs], axis=0)
    return lax.dot_general(rows, grads, (((0,), (0,)), ((), ())), preferred_element_type=F32)


def pack(block):
    rows, columns = block.shape
    full = columns // 128 * 128
    pieces = [block[:, at : at + 128] for at in range(0, full, 128)]
    pieces.append(
        jnp.concatenate([block[: rows // 2, full:], block[rows // 2 :, full:]], axis=1)
    )
    return jnp.concatenate(pieces, axis=0)


def unpack(packed, rows, columns):
    full = columns // 128 * 128
    last = packed[full // 128 * rows :, :]
    half = columns - full
    pieces = [packed[at * rows : (at + 1) * rows, :] for at in range(full // 128)]
    pieces.append(jnp.concatenate([last[:, :half], last[:, half:]], axis=0))
    return jnp.concatenate(pieces, axis=1)


def weight_grads_whole(count, *refs):
    refs[2 * count][...] = sum_of_products(refs[0:count], refs[count : 2 * count])


def add_cores(shards, keep_ref, other_ref, own_ref, *send_refs):
    me = lax.axis_index("dp")
    own_ref[...] = keep_ref[me] + other_ref[me].astype(F32)
    for k in range(1, shards):
        send_refs[k - 1][...] = (keep_ref[me ^ k] + other_ref[me ^ k].astype(F32)).astype(BF16)


def add_replicas(own_ref, *refs):
    total = own_ref[...]
    for ref in refs[:-1]:
        total = total + ref[...].astype(F32)
    _, rows, columns = refs[-1].shape
    refs[-1][0] = unpack(total, rows, columns)


def combine(count, slots_ref, gates_ref, stream_ref, *refs):
    back_refs, out_ref = refs[0:count], refs[count]
    slots = slots_ref[0:8, :]
    gates = gates_ref[...].T
    width = stream_ref.shape[1]
    picks = [as_bf16(one_hot(slots, k, back_refs[k].shape[0])) for k in range(count)]
    for at in range(0, width, CHUNK):
        cols = slice(at, at + CHUNK)
        total = stream_ref[:, cols]
        for k in range(count):
            row = lax.dot_general(
                picks[k], back_refs[k][:, cols], (((0,), (0,)), ((), ())), preferred_element_type=F32
            )
            total = total + row * gates[:, k : k + 1]
        out_ref[:, cols] = total.astype(BF16)


def swap(value, axis, k):
    return lax.ppermute(value, axis, [(i, i ^ k) for i in range(lax.axis_size(axis))])


def per_device(
    queries, memory, residual, norm_gain, expert_ids, route_gates, weight_in, weight_out, layer_grad
):
    tokens, width = queries.shape
    hidden_width = weight_in.shape[2]
    experts, replicas, cores = (lax.axis_size(axis) for axis in ("expert", "dp", "seq"))
    capacity = (5 * tokens + 2 * experts - 1) // (2 * experts)
    capacity = (capacity + 15) // 16 * 16
    half = width // 2
    in_hbm = functools.partial(pltpu.with_memory_space_constraint, memory_space=pltpu.HBM)
    ids, gates = in_hbm(expert_ids.T), in_hbm(route_gates.T)
    layer_grad, queries, residual = in_hbm(layer_grad), in_hbm(queries), in_hbm(residual)
    matrix_in, matrix_out = weight_in[0].T, weight_out[0]
    table = shape((8, tokens), F32)
    vmem, hbm = pltpu.VMEM, pltpu.HBM

    if cores == 2:
        memories = [swap(memory, "seq", 1)]
        own_memory = in_hbm(memory)
    else:
        memories = []
        own_memory = in_hbm(lax.all_gather(memory, "seq", axis=1, tiled=True))
    parts = 1 + len(memories)
    dma = pltpu.SemaphoreType.DMA
    attend_call = call(
        functools.partial(attend, parts),
        [shape((tokens, width), F32)] + [shape((tokens, half), BF16)] * 2,
        [vmem((tokens, width), BF16)] * 2
        + [vmem((width,), F32), vmem(own_memory.shape, BF16)]
        + [dma((width // CHUNK,))] * 2
        + [dma, dma],
        [hbm] * 4 + [vmem] * len(memories),
    )
    attend_inputs = (queries, residual, in_hbm(norm_gain), own_memory, *memories)

    if experts == 4:
        with_notes = shape((tokens + 16, half), BF16)
        pairs = shape((2 * capacity, half), BF16)
        narrow_shape = shape((4 * capacity, hidden_width), F32)
        left_grad, right_grad = call(
            split_grads,
            [with_notes] * 2,
            [vmem((2, tokens), jnp.int32), vmem((2, tokens), F32), dma((6,))],
            [hbm] * 3,
        )(ids, gates, layer_grad)
        x_grad, y_grad = swap(left_grad, "expert", 1), swap(right_grad, "expert", 2)
        stream, left, right = attend_call(*attend_inputs)
        x_rows, y_rows = swap(left, "expert", 1), swap(right, "expert", 2)
        pass_left, pass_right, here_left, here_right, slots, gates = call(
            relay_grads, [pairs] * 4 + [shape((24, tokens), jnp.int32), table]
        )(left_grad, right_grad, x_grad, y_grad)
        grads = (
            here_left,
            swap(pass_left, "expert", 2),
            here_right,
            swap(pass_right, "expert", 1),
        )
        pass_left, pass_right, here_left, here_right = call(relay_rows, [pairs] * 4)(
            left, right, x_rows, y_rows, slots
        )
        rows = (
            here_left,
            swap(pass_left, "expert", 2),
            here_right,
            swap(pass_right, "expert", 1),
        )
        back = call(back_products, narrow_shape)(*grads, matrix_out)
        *results, slope = call(
            experts_of_four, [shape((capacity, width), BF16)] * 4 + [narrow_shape]
        )(*rows, matrix_in, matrix_out)
        products = (*rows, back, slope)
        whole_call = four_whole
    else:
        rows_shape = [shape((capacity, width), BF16)] * experts
        *grads, slots, gates = call(
            functools.partial(dispatch_grads, experts),
            rows_shape + [shape((8, tokens), jnp.int32), table],
            [vmem((tokens, width), BF16), dma((width // CHUNK,))],
            [vmem, vmem, hbm],
        )(expert_ids.T, route_gates.T, layer_grad)
        grads = [grads[0]] + [swap(grads[k], "expert", k) for k in range(1, experts)]
        stream, left, right = attend_call(*attend_inputs)
        rows = call(functools.partial(dispatch_rows, experts), rows_shape)(slots, left, right)
        rows = [rows[0]] + [swap(rows[k], "expert", k) for k in range(1, experts)]
        last = experts - 1
        back_shape = shape((capacity, hidden_width), BF16)
        outs = call(
            functools.partial(expert_first, last),
            rows_shape[:last] + [back_shape] * last + [shape((capacity, hidden_width), F32)],
        )(*rows[:last], *grads, matrix_in, matrix_out)
        result, back = call(expert_last, [rows_shape[0], back_shape])(
            rows[last], outs[2 * last], matrix_in, matrix_out
        )
        results = list(outs[:last]) + [result]
        products = (*rows, *outs[last : 2 * last], back)
        whole_call = functools.partial(weight_grads_whole, experts)
    results = [results[0]] + [swap(results[k], "expert", k) for k in range(1, experts)]

    block = width // (replicas * cores)
    if experts == 4 and cores == 2 and replicas == 4 and block % 32 == 0 and hidden_width % 128 == 64:
        packed = (replicas, block * hidden_width // 128, 128)
        keep, send = call(
            functools.partial(four_packed, replicas), [shape(packed, F32), shape(packed, BF16)]
        )(*products)
        own, *sends = call(
            functools.partial(add_cores, replicas),
            [shape(packed[1:], F32)] + [shape(packed[1:], BF16)] * (replicas - 1),
        )(keep, swap(send, "seq", 1))
        received = [swap(sends[k - 1], "dp", k) for k in range(1, replicas)]
        grads_here = call(add_replicas, shape((1, block, hidden_width), F32))(own, *received)
    else:
        whole = call(whole_call, shape((width, hidden_width), F32))(*products)
        grads_here = lax.psum_scatter(whole, ("dp", "seq"), scatter_dimension=0, tiled=True)[None]

    layer_output = call(functools.partial(combine, experts), shape((tokens, width), BF16))(
        slots, gates, stream, *results
    )
    return layer_output, grads_here


def solution(mesh):
    rows = P(("dp", "expert", "seq"), None)
    return jax.shard_map(
        per_device,
        mesh=mesh,
        in_specs=(
            rows,
            P(None, ("dp", "expert", "seq"), None),
            rows,
            P(),
            rows,
            rows,
            P("expert", None, None),
            P("expert", None, None),
            rows,
        ),
        out_specs=(rows, P("expert", ("dp", "seq"), None)),
        check_vma=False,
    )
```

time: 76.7 us -> 69 us (0.90)
  local copies, waits for them, and re-layouts: 7.01 us -> 0.01 us
  starting transfers between devices: 23 us -> 21 us
  Pallas kernels: 13.8 us -> 15.1 us
    unnamed x18 -> x4, local copies, waits for them, and re-layouts: 6.3 us -> 0.01 us
    ppermute x14 -> x16, starting transfers between devices: 23 us -> 21 us  [swap(): lax.ppermute(value, axis, [(i, i ^ k) for i in range(lax.axis_size(axis))])]
    pallas_call x4 -> x7, Pallas kernels: 10.9 us -> 12.2 us  [the longest x1 4.38 us: per_device(): stream, left, right = attend_call(*attend_inputs)]
    ppermute x14 -> x16, waiting for transfers between devices: 31.8 us -> 31.8 us  [swap(): lax.ppermute(value, axis, [(i, i ^ k) for i in range(lax.axis_size(axis))])]
  transfers between devices with their start and end apart: 14 -> 16, of which waited for: 8 -> 9; matrix products, arithmetic and copies ran while one was open for 1% -> 0% of each run, Pallas kernels for 10% -> 15%
where the time goes in v2:
time: 69 us; the launch traced here: 68.6 us
  waiting for transfers between devices  31.8 us (46%)
  starting transfers between devices  21 us (30%)
  Pallas kernels  15.1 us (22%)
  between operations  0.73 us (1%)
    ppermute x16, waiting for transfers between devices, swap(): lax.ppermute(value, axis, [(i, i ^ k) for i in range(lax.axis_size(axis))])  31.8 us
    ppermute x16, starting transfers between devices, swap(): lax.ppermute(value, axis, [(i, i ^ k) for i in range(lax.axis_size(axis))])  21 us
    pallas_call x1, Pallas kernels, per_device(): stream, left, right = attend_call(*attend_inputs)  4.38 us
    pallas_call x1, Pallas kernels, per_device(): call(experts_of_four, [shape((capacity, width), BF16)] * 4 + [narrow_shape])  2.51 us
    pallas_call x1, Pallas kernels, per_device(): call(functools.partial(combine, experts), shape((tokens, width), BF16))  1.77 us
    pallas_call x1, Pallas kernels, per_device(): call(functools.partial(four_packed, replicas), [shape(packed, F32), shape...  1.48 us
  transfers between devices with their start and end apart: 16, of which 9 were waited for; matrix products, arithmetic and copies ran while one was open for 0% of the time, Pallas kernels for 15%

profile of v2, /device:TPU:0, one launch (start us, length us, event | category | flops | bytes accessed | tf_op | source)
XLA Modules:
  0.0 68.6 jit_solution(1590412087924169415)
XLA Ops:
  0.6 0.5 collective-permute-start.2
  1.1 1.2 %shard_map.104 = (bf16[144,1280]{1,0:T(8,128)(2,1)S(1)}, bf16[144,1280]{1,0:T(8,128)(2,1)S(1)}) custom-call(s32[2,128]{1,0:T(2,128)} %bitcast.9, f32[2,128]{1,0:T(2,128)} %bitcast.10, bf16[128,2560]{1,0:T(8,128)(2,1)} %grad_hbm.1), custom_call_target="tpu_custom_call" | custom-call | tf_op jit(solution)/shard_map/pallas_call | solution.py:482
  2.4 2.6 %collective-permute-start = (bf16[144,1280]{1,0:T(8,128)(2,1)S(1)}, bf16[144,1280]{1,0:T(8,128)(2,1)S(1)}, u32[]{:S(2)}, u32[]{:S(2)}) collective-permute-start(bf16[144,1280]{1,0:T(8,128)(2,1)S(1)} %get-tuple-element.28.left_ref), channel_id=1, source_target_pairs={{0,2},{2,0},{4,6},{6,4},{1,3},{3,1},{5,7},{7,5},{8,10},{10,8},{12,... | collective-permute-start | bytes 1105928 | tf_op jit(solution)/shard_map/ppermute | solution.py:440
  5.0 1.5 %collective-permute-start.1 = (bf16[144,1280]{1,0:T(8,128)(2,1)S(1)}, bf16[144,1280]{1,0:T(8,128)(2,1)S(1)}, u32[]{:S(2)}, u32[]{:S(2)}) collective-permute-start(bf16[144,1280]{1,0:T(8,128)(2,1)S(1)} %get-tuple-element.29.right_ref), channel_id=1, source_target_pairs={{0,4},{2,6},{4,0},{6,2},{1,5},{3,7},{5,1},{7,3},{8,12},{10,14},{12... | collective-permute-start | bytes 1105928 | tf_op jit(solution)/shard_map/ppermute | solution.py:440
  6.5 0.0 collective-permute-done.2.refs_4_
  6.5 4.4 %shard_map.106 = (f32[128,2560]{1,0:T(8,128)S(1)}, bf16[128,1280]{1,0:T(8,128)(2,1)S(1)}, bf16[128,1280]{1,0:T(8,128)(2,1)S(1)}) custom-call(bf16[128,2560]{1,0:T(8,128)(2,1)} %refs_0_.1, bf16[128,2560]{1,0:T(8,128)(2,1)} %refs_1_.1, f32[2560]{0:T(1024)} %refs_2_.1, bf16[2,16,2560]{2,1,0:T(8,128)(2,1)} %refs_3_.1, ...), custom_call_target="tpu_custom_call" | custom-call | tf_op jit(solution)/shard_map/pallas_call | solution.py:489
  10.9 0.0 copy-start
  10.9 0.6 collective-permute-start.3
  11.5 0.1 collective-permute-start.4
  11.5 2.9 %collective-permute-done.x_ref = bf16[144,1280]{1,0:T(8,128)(2,1)S(1)} collective-permute-done((bf16[144,1280]{1,0:T(8,128)(2,1)S(1)}, bf16[144,1280]{1,0:T(8,128)(2,1)S(1)}, u32[]{:S(2)}, u32[]{:S(2)}) %collective-permute-start) | collective-permute-done | bytes 368672 | tf_op jit(solution)/shard_map/ppermute | solution.py:440
  14.4 2.0 %collective-permute-done.1.y_ref = bf16[144,1280]{1,0:T(8,128)(2,1)S(1)} collective-permute-done((bf16[144,1280]{1,0:T(8,128)(2,1)S(1)}, bf16[144,1280]{1,0:T(8,128)(2,1)S(1)}, u32[]{:S(2)}, u32[]{:S(2)}) %collective-permute-start.1) | collective-permute-done | bytes 368672 | tf_op jit(solution)/shard_map/ppermute | solution.py:440
  16.4 0.7 %shard_map.105 = (bf16[160,1280]{1,0:T(8,128)(2,1)S(1)}, bf16[160,1280]{1,0:T(8,128)(2,1)S(1)}, bf16[160,1280]{1,0:T(8,128)(2,1)S(1)}, bf16[160,1280]{1,0:T(8,12...) custom-call(bf16[144,1280]{1,0:T(8,128)(2,1)S(1)} %get-tuple-element.28.left_ref, ...), custom_call_target="tpu_custom_call" | custom-call | tf_op jit(solution)/shard_map/pallas_call | solution.py:491
  17.1 1.6 %collective-permute-start.10 = (bf16[160,1280]{1,0:T(8,128)(2,1)S(1)}, bf16[160,1280]{1,0:T(8,128)(2,1)S(1)}, u32[]{:S(2)}, u32[]{:S(2)}) collective-permute-start(bf16[160,1280]{1,0:T(8,128)(2,1)S(1)} %get-tuple-element.44), channel_id=1, source_target_pairs={{0,4},{2,6},{4,0},{6,2},{1,5},{3,7},{5,1},{7,3},{8,12},{10,14},{12... | collective-permute-start | bytes 1228808 | tf_op jit(solution)/shard_map/ppermute | solution.py:440
  18.7 0.5 collective-permute-start.11
  19.2 2.4 %collective-permute-done.3.x_ref = bf16[128,1280]{1,0:T(8,128)(2,1)S(1)} collective-permute-done((bf16[128,1280]{1,0:T(8,128)(2,1)S(1)}, bf16[128,1280]{1,0:T(8,128)(2,1)S(1)}, u32[]{:S(2)}, u32[]{:S(2)}) %collective-permute-start.3) | collective-permute-done | bytes 327712 | tf_op jit(solution)/shard_map/ppermute | solution.py:440
  21.6 1.8 %collective-permute-done.4.y_ref = bf16[128,1280]{1,0:T(8,128)(2,1)S(1)} collective-permute-done((bf16[128,1280]{1,0:T(8,128)(2,1)S(1)}, bf16[128,1280]{1,0:T(8,128)(2,1)S(1)}, u32[]{:S(2)}, u32[]{:S(2)}) %collective-permute-start.4) | collective-permute-done | bytes 327712 | tf_op jit(solution)/shard_map/ppermute | solution.py:440
  23.4 0.6 shard_map.107
  24.0 1.6 %collective-permute-start.5 = (bf16[160,1280]{1,0:T(8,128)(2,1)S(1)}, bf16[160,1280]{1,0:T(8,128)(2,1)S(1)}, u32[]{:S(2)}, u32[]{:S(2)}) collective-permute-start(bf16[160,1280]{1,0:T(8,128)(2,1)S(1)} %get-tuple-element.36), channel_id=1, source_target_pairs={{0,4},{2,6},{4,0},{6,2},{1,5},{3,7},{5,1},{7,3},{8,12},{10,14},{12... | collective-permute-start | bytes 1228808 | tf_op jit(solution)/shard_map/ppermute | solution.py:440
  25.6 0.5 collective-permute-start.6
  26.1 6.1 %collective-permute-done.10.refs_1_ = bf16[160,1280]{1,0:T(8,128)(2,1)S(1)} collective-permute-done((bf16[160,1280]{1,0:T(8,128)(2,1)S(1)}, bf16[160,1280]{1,0:T(8,128)(2,1)S(1)}, u32[]{:S(2)}, u32[]{:S(2)}) %collective-permute-start.10) | collective-permute-done | bytes 409632 | tf_op jit(solution)/shard_map/ppermute | solution.py:440
  32.2 0.0 collective-permute-done.11.refs_3_
  32.2 0.0 copy-done
  32.2 0.0 copy-start.1
  32.2 1.3 %shard_map.110.refs_4_ = f32[320,320]{1,0:T(8,128)S(1)} custom-call(bf16[160,1280]{1,0:T(8,128)(2,1)S(1)} %get-tuple-element.43.refs_0_, bf16[160,1280]{1,0:T(8,128)(2,1)S(1)} %collective-permute-done.10.refs_1_, bf16[160,1280]{1,0:T(8,128)(2,1)S(1)} %get-tuple-element.45.refs_2_, bf16[160,1280]{1,0:T(8,128)(2,1)S(1)} %collective-permute-done.11.refs_3_, ...), custom_call_target="tpu_custom_call" | custom-call | tf_op jit(solution)/shard_map/pallas_call | solution.py:509
  33.5 6.7 %collective-permute-done.5.refs_1_ = bf16[160,1280]{1,0:T(8,128)(2,1)S(1)} collective-permute-done((bf16[160,1280]{1,0:T(8,128)(2,1)S(1)}, bf16[160,1280]{1,0:T(8,128)(2,1)S(1)}, u32[]{:S(2)}, u32[]{:S(2)}) %collective-permute-start.5) | collective-permute-done | bytes 409632 | tf_op jit(solution)/shard_map/ppermute | solution.py:440
  40.2 0.0 collective-permute-done.6.refs_3_
  40.2 0.0 copy-done.1
  40.2 2.5 %shard_map.108 = (bf16[80,2560]{1,0:T(8,128)(2,1)S(1)}, bf16[80,2560]{1,0:T(8,128)(2,1)S(1)}, bf16[80,2560]{1,0:T(8,128)(2,1)S(1)}, bf16[80,2560]{1,0:T(8,128)(2,1)S(1)}, f32[320,320]{1,0:T(8,128)S(1)}) custom-call(bf16[160,1280]{1,0:T(8,128)(2,1)S(1)} %get-tuple-element.35.refs_0_, bf16[160,1280]{1,0:T(8,128)(2,1)S(1)} %collective-permute-done.5.refs_1_, ...), custom_call_target="tpu_custom_call" | custom-call | tf_op jit(solution)/shard_map/pallas_call | solution.py:510
  42.8 1.5 %shard_map.111 = (f32[4,800,128]{2,1,0:T(8,128)S(1)}, bf16[4,800,128]{2,1,0:T(8,128)(2,1)S(1)}) custom-call(bf16[160,1280]{1,0:T(8,128)(2,1)S(1)} %get-tuple-element.35.refs_0_, bf16[160,1280]{1,0:T(8,128)(2,1)S(1)} %collective-permute-done.5.refs_1_, bf16[160,1280]{1,0:T(8,128)(2,1)S(1)} %get-tuple-element.37.refs_2_, ...), custom_call_target="tpu_custom_call" | custom-call | tf_op jit(solution)/shard_map/pallas_call | solution.py:544
  44.3 0.1 collective-permute-start.12
  44.3 0.4 collective-permute-start.7
  44.8 1.7 %collective-permute-start.8 = (bf16[80,2560]{1,0:T(8,128)(2,1)S(1)}, bf16[80,2560]{1,0:T(8,128)(2,1)S(1)}, u32[]{:S(2)}, u32[]{:S(2)}) collective-permute-start(bf16[80,2560]{1,0:T(8,128)(2,1)S(1)} %get-tuple-element.41), channel_id=1, source_target_pairs={{0,4},{2,6},{4,0},{6,2},{1,5},{3,7},{5,1},{7,3},{8,12},{10,14},{12... | collective-permute-start | bytes 1228808 | tf_op jit(solution)/shard_map/ppermute | solution.py:440
  46.5 1.4 %collective-permute-start.9 = (bf16[80,2560]{1,0:T(8,128)(2,1)S(1)}, bf16[80,2560]{1,0:T(8,128)(2,1)S(1)}, u32[]{:S(2)}, u32[]{:S(2)}) collective-permute-start(bf16[80,2560]{1,0:T(8,128)(2,1)S(1)} %get-tuple-element.42), channel_id=1, source_target_pairs={{0,6},{2,4},{4,2},{6,0},{1,7},{3,5},{5,3},{7,1},{8,14},{10,12},{12... | collective-permute-start | bytes 1228808 | tf_op jit(solution)/shard_map/ppermute | solution.py:440
  47.9 0.0 collective-permute-done.12.other_ref
  47.9 0.2 shard_map.112
  48.1 1.6 %collective-permute-start.13 = (bf16[800,128]{1,0:T(8,128)(2,1)S(1)}, bf16[800,128]{1,0:T(8,128)(2,1)S(1)}, u32[]{:S(2)}, u32[]{:S(2)}) collective-permute-start(bf16[800,128]{1,0:T(8,128)(2,1)S(1)} %get-tuple-element.51), channel_id=1, source_target_pairs={{0,8},{8,0},{16,24},{24,16},{1,9},{9,1},{17,25},{25,17},{2,10},{10... | collective-permute-start | bytes 614408 | tf_op jit(solution)/shard_map/ppermute | solution.py:440
  49.7 2.6 %collective-permute-start.14 = (bf16[800,128]{1,0:T(8,128)(2,1)S(1)}, bf16[800,128]{1,0:T(8,128)(2,1)S(1)}, u32[]{:S(2)}, u32[]{:S(2)}) collective-permute-start(bf16[800,128]{1,0:T(8,128)(2,1)S(1)} %get-tuple-element.52), channel_id=1, source_target_pairs={{0,16},{8,24},{16,0},{24,8},{1,17},{9,25},{17,1},{25,9},{2,18},{10... | collective-permute-start | bytes 614408 | tf_op jit(solution)/shard_map/ppermute | solution.py:440
  52.3 4.4 %collective-permute-done.7.refs_1_ = bf16[80,2560]{1,0:T(8,128)(2,1)S(1)} collective-permute-done((bf16[80,2560]{1,0:T(8,128)(2,1)S(1)}, bf16[80,2560]{1,0:T(8,128)(2,1)S(1)}, u32[]{:S(2)}, u32[]{:S(2)}) %collective-permute-start.7) | collective-permute-done | bytes 409632 | tf_op jit(solution)/shard_map/ppermute | solution.py:440
  56.7 3.6 %collective-permute-start.15 = (bf16[800,128]{1,0:T(8,128)(2,1)S(1)}, bf16[800,128]{1,0:T(8,128)(2,1)S(1)}, u32[]{:S(2)}, u32[]{:S(2)}) collective-permute-start(bf16[800,128]{1,0:T(8,128)(2,1)S(1)} %get-tuple-element.53), channel_id=1, source_target_pairs={{0,24},{8,16},{16,8},{24,0},{1,25},{9,17},{17,9},{25,1},{2,26},{10... | collective-permute-start | bytes 614408 | tf_op jit(solution)/shard_map/ppermute | solution.py:440
  60.3 4.0 %collective-permute-done.8.refs_2_ = bf16[80,2560]{1,0:T(8,128)(2,1)S(1)} collective-permute-done((bf16[80,2560]{1,0:T(8,128)(2,1)S(1)}, bf16[80,2560]{1,0:T(8,128)(2,1)S(1)}, u32[]{:S(2)}, u32[]{:S(2)}) %collective-permute-start.8) | collective-permute-done | bytes 409632 | tf_op jit(solution)/shard_map/ppermute | solution.py:440
  64.3 1.6 %collective-permute-done.9.refs_3_ = bf16[80,2560]{1,0:T(8,128)(2,1)S(1)} collective-permute-done((bf16[80,2560]{1,0:T(8,128)(2,1)S(1)}, bf16[80,2560]{1,0:T(8,128)(2,1)S(1)}, u32[]{:S(2)}, u32[]{:S(2)}) %collective-permute-start.9) | collective-permute-done | bytes 409632 | tf_op jit(solution)/shard_map/ppermute | solution.py:440
  65.9 1.8 %shard_map.109 = bf16[128,2560]{1,0:T(8,128)(2,1)} custom-call(s32[24,128]{1,0:T(8,128)S(1)} %get-tuple-element.30.slots_ref, f32[8,128]{1,0:T(8,128)S(1)} %get-tuple-element.31.gates_ref, f32[128,2560]{1,0:T(8,128)S(1)} %get-tuple-element.32.stream_ref, bf16[80,2560]{1,0:T(8,128)(2,1)S(1)} %get-tuple-element.39.refs_0_, ...), custom_call_target="tpu_custom_call" | custom-call | tf_op jit(solution)/shard_map/pallas_call | solution.py:557
  67.7 0.0 collective-permute-done.13.refs_0_
  67.7 0.0 collective-permute-done.14.refs_1_
  67.7 0.0 collective-permute-done.15.refs_2_
  67.7 0.9 %shard_map.113 = f32[1,320,320]{2,1,0:T(8,128)} custom-call(f32[800,128]{1,0:T(8,128)S(1)} %get-tuple-element.50.own_ref, bf16[800,128]{1,0:T(8,128)(2,1)S(1)} %collective-permute-done.13.refs_0_, bf16[800,128]{1,0:T(8,128)(2,1)S(1)} %collective-permute-done.14.refs_1_, bf16[800,128]{1,0:T(8,128)(2,1)S(1)} %collective-permute-done.15.refs_2_), custom_call_target="tpu_custom_call" | custom-call | tf_op jit(solution)/shard_map/pallas_call | solution.py:552
Async XLA Ops:
  0.6 5.9 %collective-permute-start.2 = (bf16[2,16,2560]{2,1,0:T(8,128)(2,1)}, bf16[2,16,2560]{2,1,0:T(8,128)(2,1)S(1)}, u32[]{:S(2)}, u32[]{:S(2)}) collective-permute-start(bf16[2,16,2560]{2,1,0:T(8,128)(2,1)} %refs_3_.1), channel_id=1, source_target_pairs={{0,1},{1,0},{2,3},{3,2},{4,5},{5,4},{6,7},{7,6},{8,9},{9,8},{10,11... | collective-permute-start | bytes 491528 | tf_op jit(solution)/shard_map/ppermute | solution.py:440
  2.4 12.0 %collective-permute-start = (bf16[144,1280]{1,0:T(8,128)(2,1)S(1)}, bf16[144,1280]{1,0:T(8,128)(2,1)S(1)}, u32[]{:S(2)}, u32[]{:S(2)}) collective-permute-start(bf16[144,1280]{1,0:T(8,128)(2,1)S(1)} %get-tuple-element.28.left_ref), channel_id=1, source_target_pairs={{0,2},{2,0},{4,6},{6,4},{1,3},{3,1},{5,7},{7,5},{8,10},{10,8},{12,... | collective-permute-start | bytes 1105928 | tf_op jit(solution)/shard_map/ppermute | solution.py:440
  5.0 11.4 %collective-permute-start.1 = (bf16[144,1280]{1,0:T(8,128)(2,1)S(1)}, bf16[144,1280]{1,0:T(8,128)(2,1)S(1)}, u32[]{:S(2)}, u32[]{:S(2)}) collective-permute-start(bf16[144,1280]{1,0:T(8,128)(2,1)S(1)} %get-tuple-element.29.right_ref), channel_id=1, source_target_pairs={{0,4},{2,6},{4,0},{6,2},{1,5},{3,7},{5,1},{7,3},{8,12},{10,14},{12... | collective-permute-start | bytes 1105928 | tf_op jit(solution)/shard_map/ppermute | solution.py:440
  10.9 21.3 %copy-start = (bf16[1,320,2560]{2,1,0:T(8,128)(2,1)S(1)}, bf16[1,320,2560]{2,1,0:T(8,128)(2,1)}, u32[]{:S(2)}) copy-start(bf16[1,320,2560]{2,1,0:T(8,128)(2,1)} %param.16) | copy-start | bytes 4915204
  10.9 10.7 %collective-permute-start.3 = (bf16[128,1280]{1,0:T(8,128)(2,1)S(1)}, bf16[128,1280]{1,0:T(8,128)(2,1)S(1)}, u32[]{:S(2)}, u32[]{:S(2)}) collective-permute-start(bf16[128,1280]{1,0:T(8,128)(2,1)S(1)} %get-tuple-element.33.left_ref), channel_id=1, source_target_pairs={{0,2},{2,0},{4,6},{6,4},{1,3},{3,1},{5,7},{7,5},{8,10},{10,8},{12,... | collective-permute-start | bytes 983048 | tf_op jit(solution)/shard_map/ppermute | solution.py:440
  11.5 11.9 %collective-permute-start.4 = (bf16[128,1280]{1,0:T(8,128)(2,1)S(1)}, bf16[128,1280]{1,0:T(8,128)(2,1)S(1)}, u32[]{:S(2)}, u32[]{:S(2)}) collective-permute-start(bf16[128,1280]{1,0:T(8,128)(2,1)S(1)} %get-tuple-element.34.right_ref), channel_id=1, source_target_pairs={{0,4},{2,6},{4,0},{6,2},{1,5},{3,7},{5,1},{7,3},{8,12},{10,14},{12... | collective-permute-start | bytes 983048 | tf_op jit(solution)/shard_map/ppermute | solution.py:440
  17.1 15.1 %collective-permute-start.10 = (bf16[160,1280]{1,0:T(8,128)(2,1)S(1)}, bf16[160,1280]{1,0:T(8,128)(2,1)S(1)}, u32[]{:S(2)}, u32[]{:S(2)}) collective-permute-start(bf16[160,1280]{1,0:T(8,128)(2,1)S(1)} %get-tuple-element.44), channel_id=1, source_target_pairs={{0,4},{2,6},{4,0},{6,2},{1,5},{3,7},{5,1},{7,3},{8,12},{10,14},{12... | collective-permute-start | bytes 1228808 | tf_op jit(solution)/shard_map/ppermute | solution.py:440
  18.7 13.5 %collective-permute-start.11 = (bf16[160,1280]{1,0:T(8,128)(2,1)S(1)}, bf16[160,1280]{1,0:T(8,128)(2,1)S(1)}, u32[]{:S(2)}, u32[]{:S(2)}) collective-permute-start(bf16[160,1280]{1,0:T(8,128)(2,1)S(1)} %get-tuple-element.46), channel_id=1, source_target_pairs={{0,2},{2,0},{4,6},{6,4},{1,3},{3,1},{5,7},{7,5},{8,10},{10,8},{12,... | collective-permute-start | bytes 1228808 | tf_op jit(solution)/shard_map/ppermute | solution.py:440
  24.0 16.2 %collective-permute-start.5 = (bf16[160,1280]{1,0:T(8,128)(2,1)S(1)}, bf16[160,1280]{1,0:T(8,128)(2,1)S(1)}, u32[]{:S(2)}, u32[]{:S(2)}) collective-permute-start(bf16[160,1280]{1,0:T(8,128)(2,1)S(1)} %get-tuple-element.36), channel_id=1, source_target_pairs={{0,4},{2,6},{4,0},{6,2},{1,5},{3,7},{5,1},{7,3},{8,12},{10,14},{12... | collective-permute-start | bytes 1228808 | tf_op jit(solution)/shard_map/ppermute | solution.py:440
  25.6 14.7 %collective-permute-start.6 = (bf16[160,1280]{1,0:T(8,128)(2,1)S(1)}, bf16[160,1280]{1,0:T(8,128)(2,1)S(1)}, u32[]{:S(2)}, u32[]{:S(2)}) collective-permute-start(bf16[160,1280]{1,0:T(8,128)(2,1)S(1)} %get-tuple-element.38), channel_id=1, source_target_pairs={{0,2},{2,0},{4,6},{6,4},{1,3},{3,1},{5,7},{7,5},{8,10},{10,8},{12,... | collective-permute-start | bytes 1228808 | tf_op jit(solution)/shard_map/ppermute | solution.py:440
  32.2 8.1 %copy-start.1 = (bf16[1,2560,320]{1,2,0:T(8,128)(2,1)S(1)}, bf16[1,2560,320]{1,2,0:T(8,128)(2,1)}, u32[]{:S(2)}) copy-start(bf16[1,2560,320]{1,2,0:T(8,128)(2,1)} %param.15) | copy-start | bytes 4915204
  44.3 3.6 %collective-permute-start.12 = (bf16[4,800,128]{2,1,0:T(8,128)(2,1)S(1)}, bf16[4,800,128]{2,1,0:T(8,128)(2,1)S(1)}, u32[]{:S(2)}, u32[]{:S(2)}) collective-permute-start(bf16[4,800,128]{2,1,0:T(8,128)(2,1)S(1)} %get-tuple-element.49), channel_id=1, source_target_pairs={{0,1},{1,0},{2,3},{3,2},{4,5},{5,4},{6,7},{7,6},{8,9},{9,8},{10,11... | collective-permute-start | bytes 2457608 | tf_op jit(solution)/shard_map/ppermute | solution.py:440
  44.3 12.3 %collective-permute-start.7 = (bf16[80,2560]{1,0:T(8,128)(2,1)S(1)}, bf16[80,2560]{1,0:T(8,128)(2,1)S(1)}, u32[]{:S(2)}, u32[]{:S(2)}) collective-permute-start(bf16[80,2560]{1,0:T(8,128)(2,1)S(1)} %get-tuple-element.40), channel_id=1, source_target_pairs={{0,2},{2,0},{4,6},{6,4},{1,3},{3,1},{5,7},{7,5},{8,10},{10,8},{12,... | collective-permute-start | bytes 1228808 | tf_op jit(solution)/shard_map/ppermute | solution.py:440
  44.8 19.6 %collective-permute-start.8 = (bf16[80,2560]{1,0:T(8,128)(2,1)S(1)}, bf16[80,2560]{1,0:T(8,128)(2,1)S(1)}, u32[]{:S(2)}, u32[]{:S(2)}) collective-permute-start(bf16[80,2560]{1,0:T(8,128)(2,1)S(1)} %get-tuple-element.41), channel_id=1, source_target_pairs={{0,4},{2,6},{4,0},{6,2},{1,5},{3,7},{5,1},{7,3},{8,12},{10,14},{12... | collective-permute-start | bytes 1228808 | tf_op jit(solution)/shard_map/ppermute | solution.py:440
  46.5 19.5 %collective-permute-start.9 = (bf16[80,2560]{1,0:T(8,128)(2,1)S(1)}, bf16[80,2560]{1,0:T(8,128)(2,1)S(1)}, u32[]{:S(2)}, u32[]{:S(2)}) collective-permute-start(bf16[80,2560]{1,0:T(8,128)(2,1)S(1)} %get-tuple-element.42), channel_id=1, source_target_pairs={{0,6},{2,4},{4,2},{6,0},{1,7},{3,5},{5,3},{7,1},{8,14},{10,12},{12... | collective-permute-start | bytes 1228808 | tf_op jit(solution)/shard_map/ppermute | solution.py:440
  48.1 19.7 %collective-permute-start.13 = (bf16[800,128]{1,0:T(8,128)(2,1)S(1)}, bf16[800,128]{1,0:T(8,128)(2,1)S(1)}, u32[]{:S(2)}, u32[]{:S(2)}) collective-permute-start(bf16[800,128]{1,0:T(8,128)(2,1)S(1)} %get-tuple-element.51), channel_id=1, source_target_pairs={{0,8},{8,0},{16,24},{24,16},{1,9},{9,1},{17,25},{25,17},{2,10},{10... | collective-permute-start | bytes 614408 | tf_op jit(solution)/shard_map/ppermute | solution.py:440
  49.7 18.0 %collective-permute-start.14 = (bf16[800,128]{1,0:T(8,128)(2,1)S(1)}, bf16[800,128]{1,0:T(8,128)(2,1)S(1)}, u32[]{:S(2)}, u32[]{:S(2)}) collective-permute-start(bf16[800,128]{1,0:T(8,128)(2,1)S(1)} %get-tuple-element.52), channel_id=1, source_target_pairs={{0,16},{8,24},{16,0},{24,8},{1,17},{9,25},{17,1},{25,9},{2,18},{10... | collective-permute-start | bytes 614408 | tf_op jit(solution)/shard_map/ppermute | solution.py:440
  56.7 11.1 %collective-permute-start.15 = (bf16[800,128]{1,0:T(8,128)(2,1)S(1)}, bf16[800,128]{1,0:T(8,128)(2,1)S(1)}, u32[]{:S(2)}, u32[]{:S(2)}) collective-permute-start(bf16[800,128]{1,0:T(8,128)(2,1)S(1)} %get-tuple-element.53), channel_id=1, source_target_pairs={{0,24},{8,16},{16,8},{24,0},{1,25},{9,17},{17,9},{25,1},{2,26},{10... | collective-permute-start | bytes 614408 | tf_op jit(solution)/shard_map/ppermute | solution.py:440

commit v3 on v2

v3 whole, which is shorter than its diff:
```python
import functools

import jax
import jax.numpy as jnp
from jax import lax
from jax.experimental import pallas as pl
from jax.experimental.pallas import tpu as pltpu
from jax.sharding import PartitionSpec as P

HEAD_SIZE = 64
GROUP = 256
CHUNK = 512
VMEM_LIMIT = 24 * 1024 * 1024
GELU_C = 0.7978845608028654
GELU_A = 0.044715
BF16 = jnp.bfloat16
F32 = jnp.float32


def params():
    return pltpu.CompilerParams(vmem_limit_bytes=VMEM_LIMIT)


def call(kernel, out_shapes, scratch=(), inputs=None):
    specs = {} if inputs is None else {"in_specs": [pl.BlockSpec(memory_space=at) for at in inputs]}
    return pl.pallas_call(
        kernel,
        out_shape=out_shapes,
        scratch_shapes=list(scratch),
        compiler_params=params(),
        **specs,
    )


def shape(dims, dtype):
    return jax.ShapeDtypeStruct(dims, dtype)


def one_hot(slots, k, capacity):
    tokens = slots.shape[1]
    return lax.broadcasted_iota(jnp.int32, (capacity, tokens), 0) == slots[k : k + 1, :]


def as_bf16(mask):
    return jnp.where(mask, 1.0, 0.0).astype(BF16)


def start_columns(source, target, sems):
    copies = []
    for at in range(0, target.shape[1], CHUNK):
        cols = pl.ds(at, CHUNK)
        copies.append(
            pltpu.make_async_copy(source.at[:, cols], target.at[:, cols], sems.at[at // CHUNK])
        )
        copies[-1].start()
    return copies


def dispatch_grads(count, ids_ref, gates_ref, grad_hbm, *refs):
    out_refs = refs[:count]
    slots_ref, table_ref, grad_ref, sems = refs[count:]
    width = grad_ref.shape[1]
    copies = start_columns(grad_hbm, grad_ref, sems)
    slots, first = slots_from(ids_ref[...])
    slots_ref[...] = slots
    gates = jnp.where(first, gates_ref[0:1, :], gates_ref[1:2, :])
    table_ref[...] = gates
    masks = [one_hot(slots, k, out_refs[k].shape[0]) for k in range(count)]
    picks = [as_bf16(mask) for mask in masks]
    scales = [
        jnp.sum(jnp.where(masks[k], gates[k : k + 1, :], 0.0), axis=1, keepdims=True)
        for k in range(count)
    ]
    for at in range(0, width, CHUNK):
        cols = slice(at, at + CHUNK)
        copies[at // CHUNK].wait()
        for k in range(count):
            rows = jnp.dot(picks[k], grad_ref[:, cols], preferred_element_type=F32)
            out_refs[k][:, cols] = (rows * scales[k]).astype(BF16)


def attend(parts, hops, slots_ref, *refs):
    query_hbm, residual_hbm, gain_hbm = refs[0:3]
    memory_refs = refs[3 : 3 + parts]
    stream_ref, left_ref, right_ref = refs[3 + parts : 6 + parts]
    query_ref, residual_ref, gain_ref = refs[6 + parts : 9 + parts]
    query_sems, residual_sems, gain_sem = refs[9 + parts :]
    tokens, width = query_ref.shape
    query_copies = start_columns(query_hbm, query_ref, query_sems)
    residual_copies = start_columns(residual_hbm, residual_ref, residual_sems)
    gain_copy = pltpu.make_async_copy(gain_hbm, gain_ref, gain_sem)
    gain_copy.start()
    heads = GROUP // HEAD_SIZE
    rows = sum(ref.shape[1] for ref in memory_refs)
    own = (
        lax.broadcasted_iota(jnp.int32, (heads * rows, GROUP), 0) // rows
        == lax.broadcasted_iota(jnp.int32, (heads * rows, GROUP), 1) // HEAD_SIZE
    )
    total = jnp.zeros((tokens, 1), F32)

    def spread(which, cols):
        piece = jnp.concatenate([ref[which, :, cols] for ref in memory_refs], axis=0)
        return jnp.where(own, jnp.concatenate([piece] * heads, axis=0), jnp.zeros((), BF16))

    for at in range(0, width, GROUP):
        cols = slice(at, at + GROUP)
        if at % CHUNK == 0:
            query_copies[at // CHUNK].wait()
            residual_copies[at // CHUNK].wait()
        scores = lax.dot_general(
            spread(0, cols), query_ref[:, cols], (((1,), (1,)), ((), ())), preferred_element_type=F32
        ) * HEAD_SIZE ** (-0.5)
        scores = scores.reshape(heads, rows, tokens)
        exponent = jnp.exp(scores - jnp.max(scores, axis=1, keepdims=True))
        probs = exponent / jnp.sum(exponent, axis=1, keepdims=True)
        attended = lax.dot_general(
            probs.reshape(heads * rows, tokens).astype(BF16),
            spread(1, cols),
            (((0,), (0,)), ((), ())),
            preferred_element_type=F32,
        ).astype(BF16)
        stream = residual_ref[:, cols].astype(F32) + attended.astype(F32)
        stream_ref[:, cols] = stream
        total = total + jnp.sum(stream * stream, axis=1, keepdims=True)
    gain_copy.wait()
    scale = lax.rsqrt(total / width + 1e-06)
    half = width // 2
    for at in range(0, width, GROUP):
        cols = slice(at, at + GROUP)
        gain = gain_ref[cols].reshape(1, GROUP)
        piece = (stream_ref[:, cols] * scale * gain).astype(BF16)
        if at < half:
            left_ref[0:tokens, cols] = piece
        else:
            right_ref[0:tokens, at - half : at - half + GROUP] = piece
    if hops:
        slots = slots_ref[...]
        relay(right_ref, slots, None, 1, left_ref, slice(tokens, None))
        relay(left_ref, slots, None, 2, right_ref, slice(tokens, None))


def slots_from(ids):
    tokens = ids.shape[1]
    me = lax.axis_index("expert")
    expert = lax.broadcasted_iota(jnp.int32, (8, tokens), 0) ^ me
    first = ids[0:1, :] == expert
    chosen = first | (ids[1:2, :] == expert)
    earlier = lax.broadcasted_iota(jnp.int32, (tokens, tokens), 0) < lax.broadcasted_iota(
        jnp.int32, (tokens, tokens), 1
    )
    count = jnp.dot(as_bf16(chosen), as_bf16(earlier), preferred_element_type=F32)
    return jnp.where(chosen, count.astype(jnp.int32), -1), first


def split_grads(ids_hbm, gates_hbm, grad_hbm, memory_hbm, *refs):
    left_ref, right_ref, slots_ref, table_ref, memory_ref, ids_ref, gates_ref, sems = refs
    tokens, half = grad_hbm.shape[0], left_ref.shape[1]
    copies = [
        pltpu.make_async_copy(ids_hbm, ids_ref, sems.at[0]),
        pltpu.make_async_copy(gates_hbm, gates_ref, sems.at[1]),
        pltpu.make_async_copy(memory_hbm, memory_ref, sems.at[6]),
    ]
    for side, target in enumerate((left_ref, right_ref)):
        for part in range(2):
            rows = pl.ds(part * (tokens // 2), tokens // 2)
            copies.append(
                pltpu.make_async_copy(
                    grad_hbm.at[rows, pl.ds(side * half, half)],
                    target.at[rows, :],
                    sems.at[2 + 2 * side + part],
                )
            )
    for copy in copies:
        copy.start()
    copies[0].wait()
    copies[1].wait()
    gates = gates_ref[...]
    high = gates.astype(BF16).astype(F32)
    middle = (gates - high).astype(BF16).astype(F32)
    low = gates - high - middle
    notes = jnp.concatenate(
        [ids_ref[...].astype(F32), high, middle, low, jnp.zeros((8, tokens), F32)], axis=0
    ).astype(BF16)
    for target in (left_ref, right_ref):
        target[tokens : tokens + 16, :] = jnp.zeros((16, half), BF16)
        target[tokens : tokens + 16, 0:tokens] = notes
    slots, first = slots_from(ids_ref[...])
    table = jnp.where(first, gates[0:1, :], gates[1:2, :])
    slots_ref[...], table_ref[...] = slots, table
    for copy in copies[2:]:
        copy.wait()
    relay(right_ref, slots, table, 1, left_ref, slice(tokens + 16, None))
    relay(left_ref, slots, table, 2, right_ref, slice(tokens + 16, None))


def notes_of(ref, tokens):
    notes = ref[tokens : tokens + 16, 0:tokens].astype(F32)
    slots, first = slots_from(notes[0:2].astype(jnp.int32))
    gates = notes[2:4] + notes[4:6] + notes[6:8]
    return slots, jnp.where(first, gates[0:1, :], gates[1:2, :])


def relay(ref, slots, gates, k, out_ref, place, shift=0):
    tokens = slots.shape[1]
    rows_at = range(*place.indices(out_ref.shape[0]))
    mask = one_hot(slots, k, len(rows_at))
    pick = as_bf16(mask)
    if gates is not None:
        gate = jnp.sum(jnp.where(mask, gates[k : k + 1, :], 0.0), axis=1, keepdims=True)
    for at in range(0, ref.shape[1], GROUP):
        rows = jnp.dot(pick, ref[0:tokens, at : at + GROUP], preferred_element_type=F32)
        if gates is not None:
            rows = rows * gate
        out_ref[place, shift + at : shift + at + GROUP] = rows.astype(BF16)


def gather_near(own, by_x, by_y, blocks, direct, near_ref):
    (own_slots, own_gates), (x_slots, x_gates), (y_slots, y_gates) = own, by_x, by_y
    left_ref, right_ref, x_ref, y_ref = blocks
    capacity, half = near_ref.shape[0] // 3, left_ref.shape[1]
    here, at_x, at_y = (slice(k * capacity, (k + 1) * capacity) for k in range(3))
    relay(left_ref, own_slots, own_gates, 0, near_ref, here)
    relay(right_ref, own_slots, own_gates, 0, near_ref, here, half)
    relay(x_ref, x_slots, x_gates, 0, near_ref, at_x)
    near_ref[at_x, half:] = x_ref[direct, :]
    near_ref[at_y, 0:half] = y_ref[direct, :]
    relay(y_ref, y_slots, y_gates, 0, near_ref, at_y, half)


def relay_grads(left_ref, right_ref, x_ref, y_ref, slots_ref, table_ref, *refs):
    pass_left, pass_right, near_ref, others_ref = refs
    tokens = slots_ref.shape[1]
    x_notes, y_notes = notes_of(x_ref, tokens), notes_of(y_ref, tokens)
    others_ref[0:8, :], others_ref[8:16, :] = x_notes[0], y_notes[0]
    relay(x_ref, *x_notes, 2, pass_left, slice(None))
    relay(y_ref, *y_notes, 1, pass_right, slice(None))
    blocks = (left_ref, right_ref, x_ref, y_ref)
    own = (slots_ref[...], table_ref[...])
    gather_near(own, x_notes, y_notes, blocks, slice(tokens + 16, None), near_ref)


def relay_rows(left_ref, right_ref, x_ref, y_ref, slots_ref, others_ref, *refs):
    pass_left, pass_right, near_ref = refs
    by_x, by_y = (others_ref[0:8, :], None), (others_ref[8:16, :], None)
    relay(x_ref, *by_x, 2, pass_left, slice(None))
    relay(y_ref, *by_y, 1, pass_right, slice(None))
    blocks = (left_ref, right_ref, x_ref, y_ref)
    direct = slice(slots_ref.shape[1], None)
    gather_near((slots_ref[...], None), by_x, by_y, blocks, direct, near_ref)


def activate(value):
    square = value * value
    curve = jnp.tanh(GELU_C * (value + GELU_A * square * value))
    hidden = (0.5 * value * (1.0 + curve)).astype(BF16)
    slope = 0.5 * (1.0 + curve) + 0.5 * value * (1.0 - curve * curve) * (
        GELU_C * (1.0 + 3.0 * GELU_A * square)
    )
    return hidden, slope


def narrow(left_ref, right_ref, matrix_ref):
    half = left_ref.shape[1]
    return sum(
        lax.dot_general(
            ref[...], matrix_ref[:, at : at + half], (((1,), (1,)), ((), ())), preferred_element_type=F32
        )
        for ref, at in ((left_ref, 0), (right_ref, half))
    )


def back_products(near_ref, left_ref, right_ref, out_ref, near_back_ref, far_back_ref):
    near_back_ref[...] = hidden_grad(near_ref, out_ref)
    far_back_ref[...] = narrow(left_ref, right_ref, out_ref)


def experts_near(near_ref, back_ref, in_ref, out_ref, *refs):
    result_refs, grad_ref = refs[0:3], refs[3]
    hidden, slope = activate(hidden_grad(near_ref, in_ref))
    grad_ref[...] = (back_ref[...] * slope).astype(BF16)
    size = result_refs[0].shape[0]
    for at in range(0, out_ref.shape[1], CHUNK):
        cols = slice(at, at + CHUNK)
        rows = jnp.dot(hidden, out_ref[:, cols], preferred_element_type=F32).astype(BF16)
        for k in range(3):
            result_refs[k][:, cols] = rows[k * size : (k + 1) * size]


def weight_grads_near(near_ref, grad_ref, total_ref):
    total_ref[...] = lax.dot_general(
        near_ref[...], grad_ref[...], (((0,), (0,)), ((), ())), preferred_element_type=F32
    )


def finish_far(shards, *refs):
    left_ref, right_ref, back_ref, in_ref, total_ref = refs[0:5]
    hidden_ref, keep_ref, send_ref = refs[5:]

    hidden, slope = activate(narrow(left_ref, right_ref, in_ref))
    hidden_ref[...] = hidden
    grads = (back_ref[...] * slope).astype(BF16)
    halves = [
        lax.dot_general(ref[...], grads, (((0,), (0,)), ((), ())), preferred_element_type=F32)
        for ref in (left_ref, right_ref)
    ]
    block = total_ref.shape[0] // (2 * shards)
    core = lax.axis_index("seq")
    for shard in range(shards):
        full = halves[2 * shard // shards]
        at, there = (2 * shard) % shards * block, 2 * shard * block
        even = pack(full[at : at + block] + total_ref[there : there + block, :])
        odd = pack(
            full[at + block : at + 2 * block] + total_ref[there + block : there + 2 * block, :]
        )
        keep_ref[shard] = jnp.where(core == 0, even, odd)
        send_ref[shard] = jnp.where(core == 0, odd, even).astype(BF16)


def widen(hidden_ref, out_ref, result_ref):
    for at in range(0, out_ref.shape[1], CHUNK):
        cols = slice(at, at + CHUNK)
        result_ref[:, cols] = jnp.dot(
            hidden_ref[...], out_ref[:, cols], preferred_element_type=F32
        ).astype(BF16)


def dispatch_rows(count, slots_ref, left_ref, right_ref, *out_refs):
    half = left_ref.shape[1]
    slots = slots_ref[...]
    for k in range(count):
        pick = as_bf16(one_hot(slots, k, out_refs[k].shape[0]))
        for at in range(0, half, GROUP):
            cols = slice(at, at + GROUP)
            there = slice(half + at, half + at + GROUP)
            out_refs[k][:, cols] = jnp.dot(
                pick, left_ref[:, cols], preferred_element_type=F32
            ).astype(BF16)
            out_refs[k][:, there] = jnp.dot(
                pick, right_ref[:, cols], preferred_element_type=F32
            ).astype(BF16)


def forward(rows_ref, in_ref, out_ref, result_ref):
    hidden, slope = activate(
        lax.dot_general(
            rows_ref[...], in_ref[...], (((1,), (1,)), ((), ())), preferred_element_type=F32
        )
    )
    for at in range(0, out_ref.shape[1], CHUNK):
        cols = slice(at, at + CHUNK)
        result_ref[:, cols] = jnp.dot(
            hidden, out_ref[:, cols], preferred_element_type=F32
        ).astype(BF16)
    return slope


def hidden_grad(grad_ref, out_ref):
    return lax.dot_general(
        grad_ref[...], out_ref[...], (((1,), (1,)), ((), ())), preferred_element_type=F32
    )


def expert_first(count, *refs):
    rows_refs, grad_refs = refs[0:count], refs[count : 2 * count + 1]
    in_ref, out_ref = refs[2 * count + 1 : 2 * count + 3]
    result_refs = refs[2 * count + 3 : 3 * count + 3]
    back_refs, last_ref = refs[3 * count + 3 : 4 * count + 3], refs[4 * count + 3]
    for k in range(count):
        slope = forward(rows_refs[k], in_ref, out_ref, result_refs[k])
        back_refs[k][...] = (hidden_grad(grad_refs[k], out_ref) * slope).astype(BF16)
    last_ref[...] = hidden_grad(grad_refs[count], out_ref)


def expert_last(rows_ref, back_ref, in_ref, out_ref, result_ref, grad_ref):
    slope = forward(rows_ref, in_ref, out_ref, result_ref)
    grad_ref[...] = (back_ref[...] * slope).astype(BF16)


def sum_of_products(rows_refs, grad_refs):
    rows = jnp.concatenate([ref[...] for ref in rows_refs], axis=0)
    grads = jnp.concatenate([ref[...] for ref in grad_refs], axis=0)
    return lax.dot_general(rows, grads, (((0,), (0,)), ((), ())), preferred_element_type=F32)


def pack(block):
    rows, columns = block.shape
    full = columns // 128 * 128
    pieces = [block[:, at : at + 128] for at in range(0, full, 128)]
    pieces.append(
        jnp.concatenate([block[: rows // 2, full:], block[rows // 2 :, full:]], axis=1)
    )
    return jnp.concatenate(pieces, axis=0)


def unpack(packed, rows, columns):
    full = columns // 128 * 128
    last = packed[full // 128 * rows :, :]
    half = columns - full
    pieces = [packed[at * rows : (at + 1) * rows, :] for at in range(full // 128)]
    pieces.append(jnp.concatenate([last[:, :half], last[:, half:]], axis=0))
    return jnp.concatenate(pieces, axis=1)


def weight_grads_whole(count, *refs):
    refs[2 * count][...] = sum_of_products(refs[0:count], refs[count : 2 * count])


def add_cores(keep_ref, other_ref, own_ref, *sum_refs):
    me = lax.axis_index("dp")
    own_ref[...] = keep_ref[me] + other_ref[me].astype(F32)
    for k, sum_ref in enumerate(sum_refs):
        sum_ref[...] = (keep_ref[me ^ (3 - k)] + other_ref[me ^ (3 - k)].astype(F32)).astype(BF16)


def combine_here(slots_ref, gates_ref, stream_ref, here_ref, total_ref):
    mix_into(slots_ref, gates_ref, (0,), stream_ref, (here_ref,), total_ref)


def finish(*refs):
    slots_ref, gates_ref, base_ref, x_ref, y_ref, far_ref = refs[0:6]
    out_hbm, sum_hbm, out_ref, sum_ref, sems, sum_sem = refs[10:]
    total = refs[6][...]
    for ref in refs[7:10]:
        total = total + ref[...].astype(F32)
    _, rows, columns = sum_ref.shape
    sum_ref[0] = unpack(total, rows, columns)
    copies = [pltpu.make_async_copy(sum_ref, sum_hbm, sum_sem)]
    copies[0].start()

    def send(cols):
        at = cols.start
        copy = pltpu.make_async_copy(
            out_ref.at[:, pl.ds(at, CHUNK)], out_hbm.at[:, pl.ds(at, CHUNK)], sems.at[at // CHUNK]
        )
        copy.start()
        copies.append(copy)

    mix_into(
        slots_ref, gates_ref, (1, 2, 3), base_ref, (x_ref, y_ref, far_ref), out_ref, send
    )
    for copy in copies:
        copy.wait()


def mix_into(slots_ref, gates_ref, sources, base_ref, result_refs, out_ref, after=None):
    slots = slots_ref[...]
    gates = gates_ref[...].T
    picks = [as_bf16(one_hot(slots, k, ref.shape[0])) for k, ref in zip(sources, result_refs)]
    for at in range(0, base_ref.shape[1], CHUNK):
        cols = slice(at, at + CHUNK)
        total = base_ref[:, cols]
        for k, pick, ref in zip(sources, picks, result_refs):
            row = lax.dot_general(
                pick, ref[:, cols], (((0,), (0,)), ((), ())), preferred_element_type=F32
            )
            total = total + row * gates[:, k : k + 1]
        out_ref[:, cols] = total.astype(out_ref.dtype)
        if after is not None:
            after(cols)


def combine(count, slots_ref, gates_ref, stream_ref, *refs):
    mix_into(slots_ref, gates_ref, range(count), stream_ref, refs[0:count], refs[count])


def swap(value, axis, k):
    return lax.ppermute(value, axis, [(i, i ^ k) for i in range(lax.axis_size(axis))])


def per_device(
    queries, memory, residual, norm_gain, expert_ids, route_gates, weight_in, weight_out, layer_grad
):
    tokens, width = queries.shape
    hidden_width = weight_in.shape[2]
    experts, replicas, cores = (lax.axis_size(axis) for axis in ("expert", "dp", "seq"))
    capacity = (5 * tokens + 2 * experts - 1) // (2 * experts)
    capacity = (capacity + 15) // 16 * 16
    half = width // 2
    in_hbm = functools.partial(pltpu.with_memory_space_constraint, memory_space=pltpu.HBM)
    ids, gates = in_hbm(expert_ids.T), in_hbm(route_gates.T)
    layer_grad, queries, residual = in_hbm(layer_grad), in_hbm(queries), in_hbm(residual)
    matrix_in, matrix_out = weight_in[0].T, weight_out[0]
    table = shape((8, tokens), F32)
    vmem, hbm = pltpu.VMEM, pltpu.HBM

    own_memory = in_hbm(memory) if cores == 2 else lax.all_gather(memory, "seq", axis=1, tiled=True)
    parts = cores if cores == 2 else 1
    dma = pltpu.SemaphoreType.DMA
    block = width // (replicas * cores)
    hops = experts == 4 and cores == 2 and replicas == 4 and block % 32 == 0
    hops = hops and hidden_width % 128 == 64
    extra = capacity if hops else 0
    attend_call = call(
        functools.partial(attend, parts, hops),
        [shape((tokens, width), F32)] + [shape((tokens + extra, half), BF16)] * 2,
        [vmem((tokens, width), BF16)] * 2
        + [vmem((width,), F32)]
        + [dma((width // CHUNK,))] * 2
        + [dma],
        [vmem] + [hbm] * 3 + [vmem] * parts,
    )
    attend_inputs = (queries, residual, in_hbm(norm_gain))
    integers = shape((8, tokens), jnp.int32)

    if hops:
        first_hop = shape((tokens + 16 + capacity, half), BF16)
        second_hop = shape((capacity, half), BF16)
        near = shape((3 * capacity, width), BF16)
        near_narrow = (3 * capacity, hidden_width)
        left, right, slots, gates, own_memory = call(
            split_grads,
            [first_hop] * 2 + [integers, table, shape(memory.shape, BF16)],
            [vmem((2, tokens), jnp.int32), vmem((2, tokens), F32), dma((7,))],
            [hbm] * 4,
        )(ids, gates, layer_grad, own_memory)
        by_x, by_y = swap(left, "expert", 1), swap(right, "expert", 2)
        stream, left_rows, right_rows = attend_call(
            slots, *attend_inputs, own_memory, swap(own_memory, "seq", 1)
        )
        rows_x, rows_y = swap(left_rows, "expert", 1), swap(right_rows, "expert", 2)
        pass_left, pass_right, near_grads, others = call(
            relay_grads, [second_hop] * 2 + [near, shape((16, tokens), jnp.int32)]
        )(left, right, by_x, by_y, slots, gates)
        far_grads = (swap(pass_left, "expert", 2), swap(pass_right, "expert", 1))
        pass_left, pass_right, near_rows = call(relay_rows, [second_hop] * 2 + [near])(
            left_rows, right_rows, rows_x, rows_y, slots, others
        )
        far_rows = (swap(pass_left, "expert", 2), swap(pass_right, "expert", 1))
        back, far_back = call(
            back_products, [shape(near_narrow, F32), shape((capacity, hidden_width), F32)]
        )(near_grads, *far_grads, matrix_out)
        result_shape = shape((capacity, width), BF16)
        *results, near_pre = call(experts_near, [result_shape] * 3 + [shape(near_narrow, BF16)])(
            near_rows, back, matrix_in, matrix_out
        )
        total = call(weight_grads_near, shape((width, hidden_width), F32))(near_rows, near_pre)
        packed = (replicas, block * hidden_width // 128, 128)
        hidden, keep, send = call(
            functools.partial(finish_far, replicas),
            [shape((capacity, hidden_width), BF16), shape(packed, F32), shape(packed, BF16)],
        )(*far_rows, far_back, matrix_in, total)
        here, from_x, from_y = [results[0]] + [swap(results[k], "expert", k) for k in (1, 2)]
        far = swap(call(widen, result_shape)(hidden, matrix_out), "expert", 3)
        one = shape(packed[1:], BF16)
        own, *sums = call(add_cores, [shape(packed[1:], F32), one, one, one])(
            keep, swap(send, "seq", 1)
        )
        received = [swap(part, "dp", 3 - k) for k, part in enumerate(sums)]
        base = call(combine_here, shape((tokens, width), F32))(slots, gates, stream, here)
        grads_shape = (1, block, hidden_width)
        layer_output, grads_here = pl.pallas_call(
            finish,
            out_shape=[shape((tokens, width), BF16), shape(grads_shape, F32)],
            in_specs=[pl.BlockSpec(memory_space=vmem)] * 10,
            out_specs=[pl.BlockSpec(memory_space=hbm)] * 2,
            scratch_shapes=[
                vmem((tokens, width), BF16),
                vmem(grads_shape, F32),
                dma((width // CHUNK,)),
                dma,
            ],
            compiler_params=params(),
        )(slots, gates, base, from_x, from_y, far, own, *received)
    else:
        rows_shape = [shape((capacity, width), BF16)] * experts
        *grads, slots, gates = call(
            functools.partial(dispatch_grads, experts),
            rows_shape + [integers, table],
            [vmem((tokens, width), BF16), dma((width // CHUNK,))],
            [vmem, vmem, hbm],
        )(expert_ids.T, route_gates.T, layer_grad)
        grads = [grads[0]] + [swap(grads[k], "expert", k) for k in range(1, experts)]
        memories = [own_memory] if cores != 2 else [own_memory, swap(own_memory, "seq", 1)]
        stream, left, right = attend_call(slots, *attend_inputs, *memories)
        rows = call(functools.partial(dispatch_rows, experts), rows_shape)(slots, left, right)
        rows = [rows[0]] + [swap(rows[k], "expert", k) for k in range(1, experts)]
        last = experts - 1
        back_shape = shape((capacity, hidden_width), BF16)
        outs = call(
            functools.partial(expert_first, last),
            rows_shape[:last] + [back_shape] * last + [shape((capacity, hidden_width), F32)],
        )(*rows[:last], *grads, matrix_in, matrix_out)
        result, back = call(expert_last, [rows_shape[0], back_shape])(
            rows[last], outs[2 * last], matrix_in, matrix_out
        )
        results = list(outs[:last]) + [result]
        whole = call(
            functools.partial(weight_grads_whole, experts), shape((width, hidden_width), F32)
        )(*rows, *outs[last : 2 * last], back)
        grads_here = lax.psum_scatter(whole, ("dp", "seq"), scatter_dimension=0, tiled=True)[None]
        results = [results[0]] + [swap(results[k], "expert", k) for k in range(1, experts)]
        layer_output = call(functools.partial(combine, experts), shape((tokens, width), BF16))(
            slots, gates, stream, *results
        )
    return layer_output, grads_here


def solution(mesh):
    rows = P(("dp", "expert", "seq"), None)
    return jax.shard_map(
        per_device,
        mesh=mesh,
        in_specs=(
            rows,
            P(None, ("dp", "expert", "seq"), None),
            rows,
            P(),
            rows,
            rows,
            P("expert", None, None),
            P("expert", None, None),
            rows,
        ),
        out_specs=(rows, P("expert", ("dp", "seq"), None)),
        check_vma=False,
    )
```

time: 69 us -> 69.8 us (1.012)
  waiting for transfers between devices: 31.8 us -> 34.4 us
  starting transfers between devices: 21 us -> 19.2 us
    ppermute x16, waiting for transfers between devices: 31.8 us -> 34.4 us  [swap(): lax.ppermute(value, axis, [(i, i ^ k) for i in range(lax.axis_size(axis))])]
    ppermute x16, starting transfers between devices: 21 us -> 19.2 us  [swap(): lax.ppermute(value, axis, [(i, i ^ k) for i in range(lax.axis_size(axis))])]
    pallas_call x10 -> x12, Pallas kernels: 15.1 us -> 15.1 us  [the longest x1 4.2 us: per_device(): attend_call(slots, *attend_inputs, own_memory, swap(own_memory, 'seq', 1))]
where the time goes in v3:
time: 69.8 us; the launch traced here: 69.6 us
  waiting for transfers between devices  34.4 us (49%)
  starting transfers between devices  19.2 us (28%)
  Pallas kernels  15.1 us (22%)
  between operations  0.75 us (1%)
    ppermute x16, waiting for transfers between devices, swap(): lax.ppermute(value, axis, [(i, i ^ k) for i in range(lax.axis_size(axis))])  34.4 us
    ppermute x16, starting transfers between devices, swap(): lax.ppermute(value, axis, [(i, i ^ k) for i in range(lax.axis_size(axis))])  19.2 us
    pallas_call x1, Pallas kernels, per_device(): attend_call(slots, *attend_inputs, own_memory, swap(own_memory, 'seq', 1))  4.2 us
    pallas_call x1, Pallas kernels, per_device(): call(functools.partial(finish_far, replicas), [shape((capacity, hidden_wi...  1.75 us
    pallas_call x1, Pallas kernels, per_device(): call(experts_near, [result_shape] * 3 + [shape(near_narrow, BF16)])  1.71 us
    pallas_call x1, Pallas kernels, per_device(): pl.pallas_call(finish, out_shape=[shape((tokens, width), BF16), shape(gra...  1.67 us
    pallas_call x1, Pallas kernels, per_device(): call(split_grads, [first_hop] * 2 + [integers, table, shape(memory.shape,...  1.59 us
  transfers between devices with their start and end apart: 16, of which 9 were waited for; matrix products, arithmetic and copies ran while one was open for 0% of the time, Pallas kernels for 15%

profile of v3, /device:TPU:0, one launch (start us, length us, event | category | flops | bytes accessed | tf_op | source)
XLA Modules:
  0.0 69.6 jit_solution(5064688243374178067)
XLA Ops:
  0.6 1.6 %shard_map.104 = (bf16[224,1280]{1,0:T(8,128)(2,1)S(1)}, bf16[224,1280]{1,0:T(8,128)(2,1)S(1)}, s32[8,128]{1,0:T(8,128)S(1)}, f32[8,128]{1,0:T(8,128)S(1)}, bf16[2,16,2560]{2,1,0:T(8,128)(2,1)S(1)}) custom-call(s32[2,128]{1,0:T(2,128)} %bitcast.11, f32[2,128]{1,0:T(2,128)} %bitcast.12, bf16[128,2560]{1,0:T(8,128)(2,1)} %grad_hbm.1, ...), custom_call_target="tpu_custom_call" | custom-call | tf_op jit(solution)/shard_map/pallas_call | solution.py:510
  2.2 0.5 collective-permute-start
  2.7 2.6 %collective-permute-start.3 = (bf16[224,1280]{1,0:T(8,128)(2,1)S(1)}, bf16[224,1280]{1,0:T(8,128)(2,1)S(1)}, u32[]{:S(2)}, u32[]{:S(2)}) collective-permute-start(bf16[224,1280]{1,0:T(8,128)(2,1)S(1)} %get-tuple-element.36.left_ref), channel_id=1, source_target_pairs={{0,2},{2,0},{4,6},{6,4},{1,3},{3,1},{5,7},{7,5},{8,10},{10,8},{12,... | collective-permute-start | bytes 1720328 | tf_op jit(solution)/shard_map/ppermute | solution.py:467
  5.3 1.5 %collective-permute-start.4 = (bf16[224,1280]{1,0:T(8,128)(2,1)S(1)}, bf16[224,1280]{1,0:T(8,128)(2,1)S(1)}, u32[]{:S(2)}, u32[]{:S(2)}) collective-permute-start(bf16[224,1280]{1,0:T(8,128)(2,1)S(1)} %get-tuple-element.37.right_ref), channel_id=1, source_target_pairs={{0,4},{2,6},{4,0},{6,2},{1,5},{3,7},{5,1},{7,3},{8,12},{10,14},{12... | collective-permute-start | bytes 1720328 | tf_op jit(solution)/shard_map/ppermute | solution.py:467
  6.8 0.0 collective-permute-done.refs_4_
  6.8 4.2 %shard_map.105 = (f32[128,2560]{1,0:T(8,128)S(1)}, bf16[208,1280]{1,0:T(8,128)(2,1)S(1)}, bf16[208,1280]{1,0:T(8,128)(2,1)S(1)}) custom-call(s32[8,128]{1,0:T(8,128)S(1)} %get-tuple-element.30.slots_ref.refs_0_, bf16[128,2560]{1,0:T(8,128)(2,1)} %refs_0_.1, bf16[128,2560]{1,0:T(8,128)(2,1)} %refs_1_.1, f32[2560]{0:T(1024)} %refs_2_.1, ...), custom_call_target="tpu_custom_call" | custom-call | tf_op jit(solution)/shard_map/pallas_call | solution.py:517
  11.0 0.6 collective-permute-start.1
  11.7 0.8 %collective-permute-start.2 = (bf16[208,1280]{1,0:T(8,128)(2,1)S(1)}, bf16[208,1280]{1,0:T(8,128)(2,1)S(1)}, u32[]{:S(2)}, u32[]{:S(2)}) collective-permute-start(bf16[208,1280]{1,0:T(8,128)(2,1)S(1)} %get-tuple-element.35.right_ref), channel_id=1, source_target_pairs={{0,4},{2,6},{4,0},{6,2},{1,5},{3,7},{5,1},{7,3},{8,12},{10,14},{12... | collective-permute-start | bytes 1597448 | tf_op jit(solution)/shard_map/ppermute | solution.py:467
  12.4 6.7 %collective-permute-done.3.x_ref = bf16[224,1280]{1,0:T(8,128)(2,1)S(1)} collective-permute-done((bf16[224,1280]{1,0:T(8,128)(2,1)S(1)}, bf16[224,1280]{1,0:T(8,128)(2,1)S(1)}, u32[]{:S(2)}, u32[]{:S(2)}) %collective-permute-start.3) | collective-permute-done | bytes 573472 | tf_op jit(solution)/shard_map/ppermute | solution.py:467
  19.1 2.0 %collective-permute-done.4.y_ref = bf16[224,1280]{1,0:T(8,128)(2,1)S(1)} collective-permute-done((bf16[224,1280]{1,0:T(8,128)(2,1)S(1)}, bf16[224,1280]{1,0:T(8,128)(2,1)S(1)}, u32[]{:S(2)}, u32[]{:S(2)}) %collective-permute-start.4) | collective-permute-done | bytes 573472 | tf_op jit(solution)/shard_map/ppermute | solution.py:467
  21.1 0.6 shard_map.106
  21.8 0.0 copy-start
  21.8 1.6 %collective-permute-start.5 = (bf16[80,1280]{1,0:T(8,128)(2,1)S(1)}, bf16[80,1280]{1,0:T(8,128)(2,1)S(1)}, u32[]{:S(2)}, u32[]{:S(2)}) collective-permute-start(bf16[80,1280]{1,0:T(8,128)(2,1)S(1)} %get-tuple-element.41), channel_id=1, source_target_pairs={{0,4},{2,6},{4,0},{6,2},{1,5},{3,7},{5,1},{7,3},{8,12},{10,14},{12... | collective-permute-start | bytes 614408 | tf_op jit(solution)/shard_map/ppermute | solution.py:467
  23.4 0.5 collective-permute-start.6
  23.9 6.7 %collective-permute-done.1.x_ref = bf16[208,1280]{1,0:T(8,128)(2,1)S(1)} collective-permute-done((bf16[208,1280]{1,0:T(8,128)(2,1)S(1)}, bf16[208,1280]{1,0:T(8,128)(2,1)S(1)}, u32[]{:S(2)}, u32[]{:S(2)}) %collective-permute-start.1) | collective-permute-done | bytes 532512 | tf_op jit(solution)/shard_map/ppermute | solution.py:467
  30.6 2.0 %collective-permute-done.2.y_ref = bf16[208,1280]{1,0:T(8,128)(2,1)S(1)} collective-permute-done((bf16[208,1280]{1,0:T(8,128)(2,1)S(1)}, bf16[208,1280]{1,0:T(8,128)(2,1)S(1)}, u32[]{:S(2)}, u32[]{:S(2)}) %collective-permute-start.2) | collective-permute-done | bytes 532512 | tf_op jit(solution)/shard_map/ppermute | solution.py:467
  32.5 0.5 shard_map.107
  33.0 1.6 %collective-permute-start.9 = (bf16[80,1280]{1,0:T(8,128)(2,1)S(1)}, bf16[80,1280]{1,0:T(8,128)(2,1)S(1)}, u32[]{:S(2)}, u32[]{:S(2)}) collective-permute-start(bf16[80,1280]{1,0:T(8,128)(2,1)S(1)} %get-tuple-element.47), channel_id=1, source_target_pairs={{0,4},{2,6},{4,0},{6,2},{1,5},{3,7},{5,1},{7,3},{8,12},{10,14},{12... | collective-permute-start | bytes 614408 | tf_op jit(solution)/shard_map/ppermute | solution.py:467
  34.6 0.5 collective-permute-start.10
  35.2 1.8 %collective-permute-done.5.left_ref = bf16[80,1280]{1,0:T(8,128)(2,1)S(1)} collective-permute-done((bf16[80,1280]{1,0:T(8,128)(2,1)S(1)}, bf16[80,1280]{1,0:T(8,128)(2,1)S(1)}, u32[]{:S(2)}, u32[]{:S(2)}) %collective-permute-start.5) | collective-permute-done | bytes 204832 | tf_op jit(solution)/shard_map/ppermute | solution.py:467
  36.9 0.0 collective-permute-done.6.right_ref
  36.9 0.0 copy-done
  36.9 0.0 copy-start.1
  36.9 1.2 %shard_map.108 = (f32[240,320]{1,0:T(8,128)S(1)}, f32[80,320]{1,0:T(8,128)S(1)}) custom-call(bf16[240,2560]{1,0:T(8,128)(2,1)S(1)} %get-tuple-element.40.near_ref, bf16[80,1280]{1,0:T(8,128)(2,1)S(1)} %collective-permute-done.5.left_ref, bf16[80,1280]{1,0:T(8,128)(2,1)S(1)} %collective-permute-done.6.right_ref, bf16[320,2560]{1,0:T(8,128)(2,1)S(1)} %bitcast.6), custom_call_target="tpu_custom_call" | custom-call | tf_op jit(solution)/shard_map/pallas_call | solution.py:529
  38.2 0.2 copy-done.1
  38.4 1.7 %shard_map.109 = (bf16[80,2560]{1,0:T(8,128)(2,1)S(1)}, bf16[80,2560]{1,0:T(8,128)(2,1)S(1)}, bf16[80,2560]{1,0:T(8,128)(2,1)S(1)}, bf16[240,320]{1,0:T(8,128)(2,1)S(1)}) custom-call(bf16[240,2560]{1,0:T(8,128)(2,1)S(1)} %get-tuple-element.39.near_ref, f32[240,320]{1,0:T(8,128)S(1)} %get-tuple-element.43.back_ref, bf16[320,2560]{1,0:T(8,128)(2,1)S(1)} %bitcast.9, ...), custom_call_target="tpu_custom_call" | custom-call | tf_op jit(solution)/shard_map/pallas_call | solution.py:533
  40.1 0.9 %shard_map.111.refs_4_ = f32[2560,320]{1,0:T(8,128)S(1)} custom-call(bf16[240,2560]{1,0:T(8,128)(2,1)S(1)} %get-tuple-element.39.near_ref, bf16[240,320]{1,0:T(8,128)(2,1)S(1)} %get-tuple-element.50.grad_ref), custom_call_target="tpu_custom_call" | custom-call | tf_op jit(solution)/shard_map/pallas_call | solution.py:536
  41.0 0.0 collective-permute-done.9.refs_0_
  41.0 0.0 collective-permute-done.10.refs_1_
  41.0 1.8 %shard_map.112 = (bf16[80,320]{1,0:T(8,128)(2,1)S(1)}, f32[4,800,128]{2,1,0:T(8,128)S(1)}, bf16[4,800,128]{2,1,0:T(8,128)(2,1)S(1)}) custom-call(bf16[80,1280]{1,0:T(8,128)(2,1)S(1)} %collective-permute-done.9.refs_0_, bf16[80,1280]{1,0:T(8,128)(2,1)S(1)} %collective-permute-done.10.refs_1_, f32[80,320]{1,0:T(8,128)S(1)} %get-tuple-element.49.refs_2_, ...), custom_call_target="tpu_custom_call" | custom-call | tf_op jit(solution)/shard_map/pallas_call | solution.py:538
  42.8 0.1 collective-permute-start.12
  42.8 0.1 collective-permute-start.7
  43.0 2.0 %collective-permute-start.8 = (bf16[80,2560]{1,0:T(8,128)(2,1)S(1)}, bf16[80,2560]{1,0:T(8,128)(2,1)S(1)}, u32[]{:S(2)}, u32[]{:S(2)}) collective-permute-start(bf16[80,2560]{1,0:T(8,128)(2,1)S(1)} %get-tuple-element.46), channel_id=1, source_target_pairs={{0,4},{2,6},{4,0},{6,2},{1,5},{3,7},{5,1},{7,3},{8,12},{10,14},{12... | collective-permute-start | bytes 1228808 | tf_op jit(solution)/shard_map/ppermute | solution.py:467
  45.0 0.5 shard_map.113
  45.5 1.5 %collective-permute-start.11 = (bf16[80,2560]{1,0:T(8,128)(2,1)S(1)}, bf16[80,2560]{1,0:T(8,128)(2,1)S(1)}, u32[]{:S(2)}, u32[]{:S(2)}) collective-permute-start(bf16[80,2560]{1,0:T(8,128)(2,1)S(1)} %shard_map.113), channel_id=1, source_target_pairs={{0,6},{2,4},{4,2},{6,0},{1,7},{3,5},{5,3},{7,1},{8,14},{10,12},{12... | collective-permute-start | bytes 1228808 | tf_op jit(solution)/shard_map/ppermute | solution.py:467
  46.9 0.0 collective-permute-done.12.other_ref
  46.9 0.2 shard_map.114
  47.1 3.7 %collective-permute-start.13 = (bf16[800,128]{1,0:T(8,128)(2,1)S(1)}, bf16[800,128]{1,0:T(8,128)(2,1)S(1)}, u32[]{:S(2)}, u32[]{:S(2)}) collective-permute-start(bf16[800,128]{1,0:T(8,128)(2,1)S(1)} %get-tuple-element.55), channel_id=1, source_target_pairs={{0,24},{8,16},{16,8},{24,0},{1,25},{9,17},{17,9},{25,1},{2,26},{10... | collective-permute-start | bytes 614408 | tf_op jit(solution)/shard_map/ppermute | solution.py:467
  50.8 0.0 collective-permute-start.14
  50.8 4.4 %collective-permute-done.7.refs_3_ = bf16[80,2560]{1,0:T(8,128)(2,1)S(1)} collective-permute-done((bf16[80,2560]{1,0:T(8,128)(2,1)S(1)}, bf16[80,2560]{1,0:T(8,128)(2,1)S(1)}, u32[]{:S(2)}, u32[]{:S(2)}) %collective-permute-start.7) | collective-permute-done | bytes 409632 | tf_op jit(solution)/shard_map/ppermute | solution.py:467
  55.2 1.6 %collective-permute-start.15 = (bf16[800,128]{1,0:T(8,128)(2,1)S(1)}, bf16[800,128]{1,0:T(8,128)(2,1)S(1)}, u32[]{:S(2)}, u32[]{:S(2)}) collective-permute-start(bf16[800,128]{1,0:T(8,128)(2,1)S(1)} %get-tuple-element.57), channel_id=1, source_target_pairs={{0,8},{8,0},{16,24},{24,16},{1,9},{9,1},{17,25},{25,17},{2,10},{10... | collective-permute-start | bytes 614408 | tf_op jit(solution)/shard_map/ppermute | solution.py:467
  56.8 0.4 shard_map.110.refs_2_
  57.1 5.7 %collective-permute-done.8.refs_4_ = bf16[80,2560]{1,0:T(8,128)(2,1)S(1)} collective-permute-done((bf16[80,2560]{1,0:T(8,128)(2,1)S(1)}, bf16[80,2560]{1,0:T(8,128)(2,1)S(1)}, u32[]{:S(2)}, u32[]{:S(2)}) %collective-permute-start.8) | collective-permute-done | bytes 409632 | tf_op jit(solution)/shard_map/ppermute | solution.py:467
  62.8 1.6 %collective-permute-done.11.refs_5_ = bf16[80,2560]{1,0:T(8,128)(2,1)S(1)} collective-permute-done((bf16[80,2560]{1,0:T(8,128)(2,1)S(1)}, bf16[80,2560]{1,0:T(8,128)(2,1)S(1)}, u32[]{:S(2)}, u32[]{:S(2)}) %collective-permute-start.11) | collective-permute-done | bytes 409632 | tf_op jit(solution)/shard_map/ppermute | solution.py:467
  64.5 0.0 collective-permute-done.13.refs_7_
  64.5 3.5 %collective-permute-done.14.refs_8_ = bf16[800,128]{1,0:T(8,128)(2,1)S(1)} collective-permute-done((bf16[800,128]{1,0:T(8,128)(2,1)S(1)}, bf16[800,128]{1,0:T(8,128)(2,1)S(1)}, u32[]{:S(2)}, u32[]{:S(2)}) %collective-permute-start.14) | collective-permute-done | bytes 204832 | tf_op jit(solution)/shard_map/ppermute | solution.py:467
  68.0 0.0 collective-permute-done.15.refs_9_
  68.0 1.7 %shard_map.115 = (bf16[128,2560]{1,0:T(8,128)(2,1)}, f32[1,320,320]{2,1,0:T(8,128)}) custom-call(s32[8,128]{1,0:T(8,128)S(1)} %get-tuple-element.30.slots_ref.refs_0_, f32[8,128]{1,0:T(8,128)S(1)} %get-tuple-element.31.table_ref.gates_ref.refs_1_, f32[128,2560]{1,0:T(8,128)S(1)} %shard_map.110.refs_2_, bf16[80,2560]{1,0:T(8,128)(2,1)S(1)} %collective-permute-done.7.refs_3_, ...), custom_call_target="tpu_custom_call" | custom-call | tf_op jit(solution)/shard_map/pallas_call | solution.py:551
Async XLA Ops:
  2.2 4.6 %collective-permute-start = (bf16[2,16,2560]{2,1,0:T(8,128)(2,1)S(1)}, bf16[2,16,2560]{2,1,0:T(8,128)(2,1)S(1)}, u32[]{:S(2)}, u32[]{:S(2)}) collective-permute-start(bf16[2,16,2560]{2,1,0:T(8,128)(2,1)S(1)} %get-tuple-element.32.refs_3_), channel_id=1, source_target_pairs={{0,1},{1,0},{2,3},{3,2},{4,5},{5,4},{6,7},{7,6},{8,9},{9,8},{10,11... | collective-permute-start | bytes 491528 | tf_op jit(solution)/shard_map/ppermute | solution.py:467
  2.7 16.4 %collective-permute-start.3 = (bf16[224,1280]{1,0:T(8,128)(2,1)S(1)}, bf16[224,1280]{1,0:T(8,128)(2,1)S(1)}, u32[]{:S(2)}, u32[]{:S(2)}) collective-permute-start(bf16[224,1280]{1,0:T(8,128)(2,1)S(1)} %get-tuple-element.36.left_ref), channel_id=1, source_target_pairs={{0,2},{2,0},{4,6},{6,4},{1,3},{3,1},{5,7},{7,5},{8,10},{10,8},{12,... | collective-permute-start | bytes 1720328 | tf_op jit(solution)/shard_map/ppermute | solution.py:467
  5.3 15.8 %collective-permute-start.4 = (bf16[224,1280]{1,0:T(8,128)(2,1)S(1)}, bf16[224,1280]{1,0:T(8,128)(2,1)S(1)}, u32[]{:S(2)}, u32[]{:S(2)}) collective-permute-start(bf16[224,1280]{1,0:T(8,128)(2,1)S(1)} %get-tuple-element.37.right_ref), channel_id=1, source_target_pairs={{0,4},{2,6},{4,0},{6,2},{1,5},{3,7},{5,1},{7,3},{8,12},{10,14},{12... | collective-permute-start | bytes 1720328 | tf_op jit(solution)/shard_map/ppermute | solution.py:467
  11.0 19.5 %collective-permute-start.1 = (bf16[208,1280]{1,0:T(8,128)(2,1)S(1)}, bf16[208,1280]{1,0:T(8,128)(2,1)S(1)}, u32[]{:S(2)}, u32[]{:S(2)}) collective-permute-start(bf16[208,1280]{1,0:T(8,128)(2,1)S(1)} %get-tuple-element.34.left_ref), channel_id=1, source_target_pairs={{0,2},{2,0},{4,6},{6,4},{1,3},{3,1},{5,7},{7,5},{8,10},{10,8},{12,... | collective-permute-start | bytes 1597448 | tf_op jit(solution)/shard_map/ppermute | solution.py:467
  11.7 20.9 %collective-permute-start.2 = (bf16[208,1280]{1,0:T(8,128)(2,1)S(1)}, bf16[208,1280]{1,0:T(8,128)(2,1)S(1)}, u32[]{:S(2)}, u32[]{:S(2)}) collective-permute-start(bf16[208,1280]{1,0:T(8,128)(2,1)S(1)} %get-tuple-element.35.right_ref), channel_id=1, source_target_pairs={{0,4},{2,6},{4,0},{6,2},{1,5},{3,7},{5,1},{7,3},{8,12},{10,14},{12... | collective-permute-start | bytes 1597448 | tf_op jit(solution)/shard_map/ppermute | solution.py:467
  21.8 15.2 %copy-start = (bf16[1,320,2560]{2,1,0:T(8,128)(2,1)S(1)}, bf16[1,320,2560]{2,1,0:T(8,128)(2,1)}, u32[]{:S(2)}) copy-start(bf16[1,320,2560]{2,1,0:T(8,128)(2,1)} %param.16) | copy-start | bytes 4915204
  21.8 15.2 %collective-permute-start.5 = (bf16[80,1280]{1,0:T(8,128)(2,1)S(1)}, bf16[80,1280]{1,0:T(8,128)(2,1)S(1)}, u32[]{:S(2)}, u32[]{:S(2)}) collective-permute-start(bf16[80,1280]{1,0:T(8,128)(2,1)S(1)} %get-tuple-element.41), channel_id=1, source_target_pairs={{0,4},{2,6},{4,0},{6,2},{1,5},{3,7},{5,1},{7,3},{8,12},{10,14},{12... | collective-permute-start | bytes 614408 | tf_op jit(solution)/shard_map/ppermute | solution.py:467
  23.4 13.6 %collective-permute-start.6 = (bf16[80,1280]{1,0:T(8,128)(2,1)S(1)}, bf16[80,1280]{1,0:T(8,128)(2,1)S(1)}, u32[]{:S(2)}, u32[]{:S(2)}) collective-permute-start(bf16[80,1280]{1,0:T(8,128)(2,1)S(1)} %get-tuple-element.42), channel_id=1, source_target_pairs={{0,2},{2,0},{4,6},{6,4},{1,3},{3,1},{5,7},{7,5},{8,10},{10,8},{12,... | collective-permute-start | bytes 614408 | tf_op jit(solution)/shard_map/ppermute | solution.py:467
  33.0 7.9 %collective-permute-start.9 = (bf16[80,1280]{1,0:T(8,128)(2,1)S(1)}, bf16[80,1280]{1,0:T(8,128)(2,1)S(1)}, u32[]{:S(2)}, u32[]{:S(2)}) collective-permute-start(bf16[80,1280]{1,0:T(8,128)(2,1)S(1)} %get-tuple-element.47), channel_id=1, source_target_pairs={{0,4},{2,6},{4,0},{6,2},{1,5},{3,7},{5,1},{7,3},{8,12},{10,14},{12... | collective-permute-start | bytes 614408 | tf_op jit(solution)/shard_map/ppermute | solution.py:467
  34.6 6.4 %collective-permute-start.10 = (bf16[80,1280]{1,0:T(8,128)(2,1)S(1)}, bf16[80,1280]{1,0:T(8,128)(2,1)S(1)}, u32[]{:S(2)}, u32[]{:S(2)}) collective-permute-start(bf16[80,1280]{1,0:T(8,128)(2,1)S(1)} %get-tuple-element.48), channel_id=1, source_target_pairs={{0,2},{2,0},{4,6},{6,4},{1,3},{3,1},{5,7},{7,5},{8,10},{10,8},{12,... | collective-permute-start | bytes 614408 | tf_op jit(solution)/shard_map/ppermute | solution.py:467
  36.9 1.4 %copy-start.1 = (bf16[1,2560,320]{1,2,0:T(8,128)(2,1)S(1)}, bf16[1,2560,320]{1,2,0:T(8,128)(2,1)}, u32[]{:S(2)}) copy-start(bf16[1,2560,320]{1,2,0:T(8,128)(2,1)} %param.15) | copy-start | bytes 4915204
  42.8 4.2 %collective-permute-start.12 = (bf16[4,800,128]{2,1,0:T(8,128)(2,1)S(1)}, bf16[4,800,128]{2,1,0:T(8,128)(2,1)S(1)}, u32[]{:S(2)}, u32[]{:S(2)}) collective-permute-start(bf16[4,800,128]{2,1,0:T(8,128)(2,1)S(1)} %get-tuple-element.53), channel_id=1, source_target_pairs={{0,1},{1,0},{2,3},{3,2},{4,5},{5,4},{6,7},{7,6},{8,9},{9,8},{10,11... | collective-permute-start | bytes 2457608 | tf_op jit(solution)/shard_map/ppermute | solution.py:467
  42.8 12.3 %collective-permute-start.7 = (bf16[80,2560]{1,0:T(8,128)(2,1)S(1)}, bf16[80,2560]{1,0:T(8,128)(2,1)S(1)}, u32[]{:S(2)}, u32[]{:S(2)}) collective-permute-start(bf16[80,2560]{1,0:T(8,128)(2,1)S(1)} %get-tuple-element.45), channel_id=1, source_target_pairs={{0,2},{2,0},{4,6},{6,4},{1,3},{3,1},{5,7},{7,5},{8,10},{10,8},{12,... | collective-permute-start | bytes 1228808 | tf_op jit(solution)/shard_map/ppermute | solution.py:467
  43.0 19.9 %collective-permute-start.8 = (bf16[80,2560]{1,0:T(8,128)(2,1)S(1)}, bf16[80,2560]{1,0:T(8,128)(2,1)S(1)}, u32[]{:S(2)}, u32[]{:S(2)}) collective-permute-start(bf16[80,2560]{1,0:T(8,128)(2,1)S(1)} %get-tuple-element.46), channel_id=1, source_target_pairs={{0,4},{2,6},{4,0},{6,2},{1,5},{3,7},{5,1},{7,3},{8,12},{10,14},{12... | collective-permute-start | bytes 1228808 | tf_op jit(solution)/shard_map/ppermute | solution.py:467
  45.5 19.0 %collective-permute-start.11 = (bf16[80,2560]{1,0:T(8,128)(2,1)S(1)}, bf16[80,2560]{1,0:T(8,128)(2,1)S(1)}, u32[]{:S(2)}, u32[]{:S(2)}) collective-permute-start(bf16[80,2560]{1,0:T(8,128)(2,1)S(1)} %shard_map.113), channel_id=1, source_target_pairs={{0,6},{2,4},{4,2},{6,0},{1,7},{3,5},{5,3},{7,1},{8,14},{10,12},{12... | collective-permute-start | bytes 1228808 | tf_op jit(solution)/shard_map/ppermute | solution.py:467
  47.1 17.4 %collective-permute-start.13 = (bf16[800,128]{1,0:T(8,128)(2,1)S(1)}, bf16[800,128]{1,0:T(8,128)(2,1)S(1)}, u32[]{:S(2)}, u32[]{:S(2)}) collective-permute-start(bf16[800,128]{1,0:T(8,128)(2,1)S(1)} %get-tuple-element.55), channel_id=1, source_target_pairs={{0,24},{8,16},{16,8},{24,0},{1,25},{9,17},{17,9},{25,1},{2,26},{10... | collective-permute-start | bytes 614408 | tf_op jit(solution)/shard_map/ppermute | solution.py:467
  50.8 17.2 %collective-permute-start.14 = (bf16[800,128]{1,0:T(8,128)(2,1)S(1)}, bf16[800,128]{1,0:T(8,128)(2,1)S(1)}, u32[]{:S(2)}, u32[]{:S(2)}) collective-permute-start(bf16[800,128]{1,0:T(8,128)(2,1)S(1)} %get-tuple-element.56), channel_id=1, source_target_pairs={{0,16},{8,24},{16,0},{24,8},{1,17},{9,25},{17,1},{25,9},{2,18},{10... | collective-permute-start | bytes 614408 | tf_op jit(solution)/shard_map/ppermute | solution.py:467
  55.2 12.8 %collective-permute-start.15 = (bf16[800,128]{1,0:T(8,128)(2,1)S(1)}, bf16[800,128]{1,0:T(8,128)(2,1)S(1)}, u32[]{:S(2)}, u32[]{:S(2)}) collective-permute-start(bf16[800,128]{1,0:T(8,128)(2,1)S(1)} %get-tuple-element.57), channel_id=1, source_target_pairs={{0,8},{8,0},{16,24},{24,16},{1,9},{9,1},{17,25},{25,17},{2,10},{10... | collective-permute-start | bytes 614408 | tf_op jit(solution)/shard_map/ppermute | solution.py:467

commit v4 on v3

--- a/solution.py
+++ b/solution.py
@@ -80,16 +80,19 @@
 
 
 def attend(parts, hops, slots_ref, *refs):
-    query_hbm, residual_hbm, gain_hbm = refs[0:3]
-    memory_refs = refs[3 : 3 + parts]
+    query_hbm, residual_hbm, gain_hbm, own_hbm = refs[0:4]
+    other_refs = refs[4 : 3 + parts]
     stream_ref, left_ref, right_ref = refs[3 + parts : 6 + parts]
-    query_ref, residual_ref, gain_ref = refs[6 + parts : 9 + parts]
-    query_sems, residual_sems, gain_sem = refs[9 + parts :]
+    query_ref, residual_ref, gain_ref, own_ref = refs[6 + parts : 10 + parts]
+    query_sems, residual_sems, gain_sem, own_sem = refs[10 + parts :]
     tokens, width = query_ref.shape
+    own_copy = pltpu.make_async_copy(own_hbm, own_ref, own_sem)
+    own_copy.start()
     query_copies = start_columns(query_hbm, query_ref, query_sems)
     residual_copies = start_columns(residual_hbm, residual_ref, residual_sems)
     gain_copy = pltpu.make_async_copy(gain_hbm, gain_ref, gain_sem)
     gain_copy.start()
+    memory_refs = (own_ref,) + tuple(other_refs)
     heads = GROUP // HEAD_SIZE
     rows = sum(ref.shape[1] for ref in memory_refs)
     own = (
@@ -102,6 +105,7 @@
         piece = jnp.concatenate([ref[which, :, cols] for ref in memory_refs], axis=0)
         return jnp.where(own, jnp.concatenate([piece] * heads, axis=0), jnp.zeros((), BF16))
 
+    own_copy.wait()
     for at in range(0, width, GROUP):
         cols = slice(at, at + GROUP)
         if at % CHUNK == 0:
@@ -152,13 +156,12 @@
     return jnp.where(chosen, count.astype(jnp.int32), -1), first
 
 
-def split_grads(ids_hbm, gates_hbm, grad_hbm, memory_hbm, *refs):
-    left_ref, right_ref, slots_ref, table_ref, memory_ref, ids_ref, gates_ref, sems = refs
+def split_grads(ids_hbm, gates_hbm, grad_hbm, left_ref, right_ref, slots_ref, table_ref, *scratch):
+    ids_ref, gates_ref, sems = scratch
     tokens, half = grad_hbm.shape[0], left_ref.shape[1]
     copies = [
         pltpu.make_async_copy(ids_hbm, ids_ref, sems.at[0]),
         pltpu.make_async_copy(gates_hbm, gates_ref, sems.at[1]),
-        pltpu.make_async_copy(memory_hbm, memory_ref, sems.at[6]),
     ]
     for side, target in enumerate((left_ref, right_ref)):
         for part in range(2):
@@ -259,19 +262,8 @@
     return hidden, slope
 
 
-def narrow(left_ref, right_ref, matrix_ref):
-    half = left_ref.shape[1]
-    return sum(
-        lax.dot_general(
-            ref[...], matrix_ref[:, at : at + half], (((1,), (1,)), ((), ())), preferred_element_type=F32
-        )
-        for ref, at in ((left_ref, 0), (right_ref, half))
-    )
-
-
-def back_products(near_ref, left_ref, right_ref, out_ref, near_back_ref, far_back_ref):
-    near_back_ref[...] = hidden_grad(near_ref, out_ref)
-    far_back_ref[...] = narrow(left_ref, right_ref, out_ref)
+def back_near(near_ref, out_ref, back_ref):
+    back_ref[...] = hidden_grad(near_ref, out_ref)
 
 
 def experts_near(near_ref, back_ref, in_ref, out_ref, *refs):
@@ -293,12 +285,22 @@
 
 
 def finish_far(shards, *refs):
-    left_ref, right_ref, back_ref, in_ref, total_ref = refs[0:5]
-    hidden_ref, keep_ref, send_ref = refs[5:]
+    left_ref, right_ref, grad_left, grad_right, in_ref, out_ref, total_ref = refs[0:7]
+    hidden_ref, keep_ref, send_ref = refs[7:]
+    half = left_ref.shape[1]
+
+    def narrow(left, right, matrix_ref):
+        return sum(
+            lax.dot_general(
+                ref[...], matrix_ref[:, at : at + half], (((1,), (1,)), ((), ())),
+                preferred_element_type=F32,
+            )
+            for ref, at in ((left, 0), (right, half))
+        )
 
     hidden, slope = activate(narrow(left_ref, right_ref, in_ref))
     hidden_ref[...] = hidden
-    grads = (back_ref[...] * slope).astype(BF16)
+    grads = (narrow(grad_left, grad_right, out_ref) * slope).astype(BF16)
     halves = [
         lax.dot_general(ref[...], grads, (((0,), (0,)), ((), ())), preferred_element_type=F32)
         for ref in (left_ref, right_ref)
@@ -405,62 +407,36 @@
     refs[2 * count][...] = sum_of_products(refs[0:count], refs[count : 2 * count])
 
 
-def add_cores(keep_ref, other_ref, own_ref, *sum_refs):
+def add_cores(shards, keep_ref, other_ref, own_ref, *send_refs):
     me = lax.axis_index("dp")
     own_ref[...] = keep_ref[me] + other_ref[me].astype(F32)
-    for k, sum_ref in enumerate(sum_refs):
-        sum_ref[...] = (keep_ref[me ^ (3 - k)] + other_ref[me ^ (3 - k)].astype(F32)).astype(BF16)
-
-
-def combine_here(slots_ref, gates_ref, stream_ref, here_ref, total_ref):
-    mix_into(slots_ref, gates_ref, (0,), stream_ref, (here_ref,), total_ref)
-
-
-def finish(*refs):
-    slots_ref, gates_ref, base_ref, x_ref, y_ref, far_ref = refs[0:6]
-    out_hbm, sum_hbm, out_ref, sum_ref, sems, sum_sem = refs[10:]
-    total = refs[6][...]
-    for ref in refs[7:10]:
+    for k in range(1, shards):
+        send_refs[k - 1][...] = (keep_ref[me ^ k] + other_ref[me ^ k].astype(F32)).astype(BF16)
+
+
+def add_replicas(own_ref, *refs):
+    total = own_ref[...]
+    for ref in refs[:-1]:
         total = total + ref[...].astype(F32)
-    _, rows, columns = sum_ref.shape
-    sum_ref[0] = unpack(total, rows, columns)
-    copies = [pltpu.make_async_copy(sum_ref, sum_hbm, sum_sem)]
-    copies[0].start()
-
-    def send(cols):
-        at = cols.start
-        copy = pltpu.make_async_copy(
-            out_ref.at[:, pl.ds(at, CHUNK)], out_hbm.at[:, pl.ds(at, CHUNK)], sems.at[at // CHUNK]
-        )
-        copy.start()
-        copies.append(copy)
-
-    mix_into(
-        slots_ref, gates_ref, (1, 2, 3), base_ref, (x_ref, y_ref, far_ref), out_ref, send
-    )
-    for copy in copies:
-        copy.wait()
-
-
-def mix_into(slots_ref, gates_ref, sources, base_ref, result_refs, out_ref, after=None):
+    _, rows, columns = refs[-1].shape
+    refs[-1][0] = unpack(total, rows, columns)
+
+
+def combine(count, slots_ref, gates_ref, stream_ref, *refs):
+    back_refs, out_ref = refs[0:count], refs[count]
     slots = slots_ref[...]
     gates = gates_ref[...].T
-    picks = [as_bf16(one_hot(slots, k, ref.shape[0])) for k, ref in zip(sources, result_refs)]
-    for at in range(0, base_ref.shape[1], CHUNK):
+    width = stream_ref.shape[1]
+    picks = [as_bf16(one_hot(slots, k, back_refs[k].shape[0])) for k in range(count)]
+    for at in range(0, width, CHUNK):
         cols = slice(at, at + CHUNK)
-        total = base_ref[:, cols]
-        for k, pick, ref in zip(sources, picks, result_refs):
+        total = stream_ref[:, cols]
+        for k in range(count):
             row = lax.dot_general(
-                pick, ref[:, cols], (((0,), (0,)), ((), ())), preferred_element_type=F32
+                picks[k], back_refs[k][:, cols], (((0,), (0,)), ((), ())), preferred_element_type=F32
             )
             total = total + row * gates[:, k : k + 1]
-        out_ref[:, cols] = total.astype(out_ref.dtype)
-        if after is not None:
-            after(cols)
-
-
-def combine(count, slots_ref, gates_ref, stream_ref, *refs):
-    mix_into(slots_ref, gates_ref, range(count), stream_ref, refs[0:count], refs[count])
+        out_ref[:, cols] = total.astype(BF16)
 
 
 def swap(value, axis, k):
@@ -483,8 +459,13 @@
     table = shape((8, tokens), F32)
     vmem, hbm = pltpu.VMEM, pltpu.HBM
 
-    own_memory = in_hbm(memory) if cores == 2 else lax.all_gather(memory, "seq", axis=1, tiled=True)
-    parts = cores if cores == 2 else 1
+    if cores == 2:
+        memories = [swap(memory, "seq", 1)]
+        own_memory = in_hbm(memory)
+    else:
+        memories = []
+        own_memory = in_hbm(lax.all_gather(memory, "seq", axis=1, tiled=True))
+    parts = 1 + len(memories)
     dma = pltpu.SemaphoreType.DMA
     block = width // (replicas * cores)
     hops = experts == 4 and cores == 2 and replicas == 4 and block % 32 == 0
@@ -494,12 +475,12 @@
         functools.partial(attend, parts, hops),
         [shape((tokens, width), F32)] + [shape((tokens + extra, half), BF16)] * 2,
         [vmem((tokens, width), BF16)] * 2
-        + [vmem((width,), F32)]
+        + [vmem((width,), F32), vmem(own_memory.shape, BF16)]
         + [dma((width // CHUNK,))] * 2
-        + [dma],
-        [vmem] + [hbm] * 3 + [vmem] * parts,
-    )
-    attend_inputs = (queries, residual, in_hbm(norm_gain))
+        + [dma, dma],
+        [vmem] + [hbm] * 4 + [vmem] * len(memories),
+    )
+    attend_inputs = (queries, residual, in_hbm(norm_gain), own_memory, *memories)
     integers = shape((8, tokens), jnp.int32)
 
     if hops:
@@ -507,16 +488,14 @@
         second_hop = shape((capacity, half), BF16)
         near = shape((3 * capacity, width), BF16)
         near_narrow = (3 * capacity, hidden_width)
-        left, right, slots, gates, own_memory = call(
+        left, right, slots, gates = call(
             split_grads,
-            [first_hop] * 2 + [integers, table, shape(memory.shape, BF16)],
-            [vmem((2, tokens), jnp.int32), vmem((2, tokens), F32), dma((7,))],
-            [hbm] * 4,
-        )(ids, gates, layer_grad, own_memory)
+            [first_hop] * 2 + [integers, table],
+            [vmem((2, tokens), jnp.int32), vmem((2, tokens), F32), dma((6,))],
+            [hbm] * 3,
+        )(ids, gates, layer_grad)
         by_x, by_y = swap(left, "expert", 1), swap(right, "expert", 2)
-        stream, left_rows, right_rows = attend_call(
-            slots, *attend_inputs, own_memory, swap(own_memory, "seq", 1)
-        )
+        stream, left_rows, right_rows = attend_call(slots, *attend_inputs)
         rows_x, rows_y = swap(left_rows, "expert", 1), swap(right_rows, "expert", 2)
         pass_left, pass_right, near_grads, others = call(
             relay_grads, [second_hop] * 2 + [near, shape((16, tokens), jnp.int32)]
@@ -526,9 +505,7 @@
             left_rows, right_rows, rows_x, rows_y, slots, others
         )
         far_rows = (swap(pass_left, "expert", 2), swap(pass_right, "expert", 1))
-        back, far_back = call(
-            back_products, [shape(near_narrow, F32), shape((capacity, hidden_width), F32)]
-        )(near_grads, *far_grads, matrix_out)
+        back = call(back_near, shape(near_narrow, F32))(near_grads, matrix_out)
         result_shape = shape((capacity, width), BF16)
         *results, near_pre = call(experts_near, [result_shape] * 3 + [shape(near_narrow, BF16)])(
             near_rows, back, matrix_in, matrix_out
@@ -538,29 +515,14 @@
         hidden, keep, send = call(
             functools.partial(finish_far, replicas),
             [shape((capacity, hidden_width), BF16), shape(packed, F32), shape(packed, BF16)],
-        )(*far_rows, far_back, matrix_in, total)
-        here, from_x, from_y = [results[0]] + [swap(results[k], "expert", k) for k in (1, 2)]
-        far = swap(call(widen, result_shape)(hidden, matrix_out), "expert", 3)
-        one = shape(packed[1:], BF16)
-        own, *sums = call(add_cores, [shape(packed[1:], F32), one, one, one])(
-            keep, swap(send, "seq", 1)
-        )
-        received = [swap(part, "dp", 3 - k) for k, part in enumerate(sums)]
-        base = call(combine_here, shape((tokens, width), F32))(slots, gates, stream, here)
-        grads_shape = (1, block, hidden_width)
-        layer_output, grads_here = pl.pallas_call(
-            finish,
-            out_shape=[shape((tokens, width), BF16), shape(grads_shape, F32)],
-            in_specs=[pl.BlockSpec(memory_space=vmem)] * 10,
-            out_specs=[pl.BlockSpec(memory_space=hbm)] * 2,
-            scratch_shapes=[
-                vmem((tokens, width), BF16),
-                vmem(grads_shape, F32),
-                dma((width // CHUNK,)),
-                dma,
-            ],
-            compiler_params=params(),
-        )(slots, gates, base, from_x, from_y, far, own, *received)
+        )(*far_rows, *far_grads, matrix_in, matrix_out, total)
+        results.append(call(widen, result_shape)(hidden, matrix_out))
+        own, *sends = call(
+            functools.partial(add_cores, replicas),
+            [shape(packed[1:], F32)] + [shape(packed[1:], BF16)] * (replicas - 1),
+        )(keep, swap(send, "seq", 1))
+        received = [swap(sends[k - 1], "dp", k) for k in range(1, replicas)]
+        grads_here = call(add_replicas, shape((1, block, hidden_width), F32))(own, *received)
     else:
         rows_shape = [shape((capacity, width), BF16)] * experts
         *grads, slots, gates = call(
@@ -570,8 +532,7 @@
             [vmem, vmem, hbm],
         )(expert_ids.T, route_gates.T, layer_grad)
         grads = [grads[0]] + [swap(grads[k], "expert", k) for k in range(1, experts)]
-        memories = [own_memory] if cores != 2 else [own_memory, swap(own_memory, "seq", 1)]
-        stream, left, right = attend_call(slots, *attend_inputs, *memories)
+        stream, left, right = attend_call(slots, *attend_inputs)
         rows = call(functools.partial(dispatch_rows, experts), rows_shape)(slots, left, right)
         rows = [rows[0]] + [swap(rows[k], "expert", k) for k in range(1, experts)]
         last = experts - 1
@@ -588,10 +549,11 @@
             functools.partial(weight_grads_whole, experts), shape((width, hidden_width), F32)
         )(*rows, *outs[last : 2 * last], back)
         grads_here = lax.psum_scatter(whole, ("dp", "seq"), scatter_dimension=0, tiled=True)[None]
-        results = [results[0]] + [swap(results[k], "expert", k) for k in range(1, experts)]
-        layer_output = call(functools.partial(combine, experts), shape((tokens, width), BF16))(
-            slots, gates, stream, *results
-        )
+    results = [results[0]] + [swap(results[k], "expert", k) for k in range(1, experts)]
+
+    layer_output = call(functools.partial(combine, experts), shape((tokens, width), BF16))(
+        slots, gates, stream, *results
+    )
     return layer_output, grads_here
 
 

time: 69.8 us -> 67.9 us (0.973)
  waiting for transfers between devices: 34.4 us -> 29.2 us
  starting transfers between devices: 19.2 us -> 21 us
  Pallas kernels: 15.1 us -> 16.1 us
    ppermute x16, waiting for transfers between devices: 34.4 us -> 29.2 us  [swap(): lax.ppermute(value, axis, [(i, i ^ k) for i in range(lax.axis_size(axis))])]
    ppermute x16, starting transfers between devices: 19.2 us -> 21 us  [swap(): lax.ppermute(value, axis, [(i, i ^ k) for i in range(lax.axis_size(axis))])]
  transfers between devices with their start and end apart: 16 -> 16, of which waited for: 9 -> 8; matrix products, arithmetic and copies ran while one was open for 0% -> 0% of each run, Pallas kernels for 15% -> 20%
where the time goes in v4:
time: 67.9 us; the launch traced here: 67.1 us
  waiting for transfers between devices  29.2 us (43%)
  starting transfers between devices  21 us (31%)
  Pallas kernels  16.1 us (24%)
  between operations  0.76 us (1%)
    ppermute x16, waiting for transfers between devices, swap(): lax.ppermute(value, axis, [(i, i ^ k) for i in range(lax.axis_size(axis))])  29.2 us
    ppermute x16, starting transfers between devices, swap(): lax.ppermute(value, axis, [(i, i ^ k) for i in range(lax.axis_size(axis))])  21 us
    pallas_call x1, Pallas kernels, per_device(): stream, left_rows, right_rows = attend_call(slots, *attend_inputs)  4.59 us
    pallas_call x1, Pallas kernels, per_device(): call(functools.partial(finish_far, replicas), [shape((capacity, hidden_wi...  2.12 us
    pallas_call x1, Pallas kernels, per_device(): call(functools.partial(combine, experts), shape((tokens, width), BF16))  1.81 us
    pallas_call x1, Pallas kernels, per_device(): call(experts_near, [result_shape] * 3 + [shape(near_narrow, BF16)])  1.71 us
    pallas_call x1, Pallas kernels, per_device(): call(split_grads, [first_hop] * 2 + [integers, table], [vmem((2, tokens),...  1.5 us
  transfers between devices with their start and end apart: 16, of which 8 were waited for; matrix products, arithmetic and copies ran while one was open for 0% of the time, Pallas kernels for 20%

profile of v4, /device:TPU:0, one launch (start us, length us, event | category | flops | bytes accessed | tf_op | source)
XLA Modules:
  0.0 67.1 jit_solution(11360499545653805618)
XLA Ops:
  0.6 0.5 collective-permute-start
  1.1 1.5 %shard_map.104 = (bf16[224,1280]{1,0:T(8,128)(2,1)S(1)}, bf16[224,1280]{1,0:T(8,128)(2,1)S(1)}, s32[8,128]{1,0:T(8,128)S(1)}, f32[8,128]{1,0:T(8,128)S(1)}) custom-call(s32[2,128]{1,0:T(2,128)} %bitcast.12, f32[2,128]{1,0:T(2,128)} %bitcast.13, bf16[128,2560]{1,0:T(8,128)(2,1)} %grad_hbm.1), custom_call_target="tpu_custom_call" | custom-call | tf_op jit(solution)/shard_map/pallas_call | solution.py:491
  2.7 2.6 %collective-permute-start.3 = (bf16[224,1280]{1,0:T(8,128)(2,1)S(1)}, bf16[224,1280]{1,0:T(8,128)(2,1)S(1)}, u32[]{:S(2)}, u32[]{:S(2)}) collective-permute-start(bf16[224,1280]{1,0:T(8,128)(2,1)S(1)} %get-tuple-element.32.left_ref), channel_id=1, source_target_pairs={{0,2},{2,0},{4,6},{6,4},{1,3},{3,1},{5,7},{7,5},{8,10},{10,8},{12,... | collective-permute-start | bytes 1720328 | tf_op jit(solution)/shard_map/ppermute | solution.py:443
  5.2 1.5 %collective-permute-start.4 = (bf16[224,1280]{1,0:T(8,128)(2,1)S(1)}, bf16[224,1280]{1,0:T(8,128)(2,1)S(1)}, u32[]{:S(2)}, u32[]{:S(2)}) collective-permute-start(bf16[224,1280]{1,0:T(8,128)(2,1)S(1)} %get-tuple-element.33.right_ref), channel_id=1, source_target_pairs={{0,4},{2,6},{4,0},{6,2},{1,5},{3,7},{5,1},{7,3},{8,12},{10,14},{12... | collective-permute-start | bytes 1720328 | tf_op jit(solution)/shard_map/ppermute | solution.py:443
  6.7 0.0 collective-permute-done.refs_4_
  6.7 4.6 %shard_map.105 = (f32[128,2560]{1,0:T(8,128)S(1)}, bf16[208,1280]{1,0:T(8,128)(2,1)S(1)}, bf16[208,1280]{1,0:T(8,128)(2,1)S(1)}) custom-call(s32[8,128]{1,0:T(8,128)S(1)} %get-tuple-element.27.slots_ref, bf16[128,2560]{1,0:T(8,128)(2,1)} %refs_0_.1, bf16[128,2560]{1,0:T(8,128)(2,1)} %refs_1_.1, f32[2560]{0:T(1024)} %refs_2_.1, bf16[2,16,2560]{2,1,0:T(8,128)(2,1)} %refs_3_.1, ...), custom_call_target="tpu_custom_call" | custom-call | tf_op jit(solution)/shard_map/pallas_call | solution.py:498
  11.3 0.6 collective-permute-start.1
  11.9 0.1 collective-permute-start.2
  12.0 7.1 %collective-permute-done.3.x_ref = bf16[224,1280]{1,0:T(8,128)(2,1)S(1)} collective-permute-done((bf16[224,1280]{1,0:T(8,128)(2,1)S(1)}, bf16[224,1280]{1,0:T(8,128)(2,1)S(1)}, u32[]{:S(2)}, u32[]{:S(2)}) %collective-permute-start.3) | collective-permute-done | bytes 573472 | tf_op jit(solution)/shard_map/ppermute | solution.py:443
  19.1 2.0 %collective-permute-done.4.y_ref = bf16[224,1280]{1,0:T(8,128)(2,1)S(1)} collective-permute-done((bf16[224,1280]{1,0:T(8,128)(2,1)S(1)}, bf16[224,1280]{1,0:T(8,128)(2,1)S(1)}, u32[]{:S(2)}, u32[]{:S(2)}) %collective-permute-start.4) | collective-permute-done | bytes 573472 | tf_op jit(solution)/shard_map/ppermute | solution.py:443
  21.0 0.6 shard_map.106
  21.6 0.0 copy-start
  21.7 1.6 %collective-permute-start.9 = (bf16[80,1280]{1,0:T(8,128)(2,1)S(1)}, bf16[80,1280]{1,0:T(8,128)(2,1)S(1)}, u32[]{:S(2)}, u32[]{:S(2)}) collective-permute-start(bf16[80,1280]{1,0:T(8,128)(2,1)S(1)} %get-tuple-element.42), channel_id=1, source_target_pairs={{0,4},{2,6},{4,0},{6,2},{1,5},{3,7},{5,1},{7,3},{8,12},{10,14},{12... | collective-permute-start | bytes 614408 | tf_op jit(solution)/shard_map/ppermute | solution.py:443
  23.2 0.5 collective-permute-start.10
  23.8 6.7 %collective-permute-done.1.x_ref = bf16[208,1280]{1,0:T(8,128)(2,1)S(1)} collective-permute-done((bf16[208,1280]{1,0:T(8,128)(2,1)S(1)}, bf16[208,1280]{1,0:T(8,128)(2,1)S(1)}, u32[]{:S(2)}, u32[]{:S(2)}) %collective-permute-start.1) | collective-permute-done | bytes 532512 | tf_op jit(solution)/shard_map/ppermute | solution.py:443
  30.5 2.0 %collective-permute-done.2.y_ref = bf16[208,1280]{1,0:T(8,128)(2,1)S(1)} collective-permute-done((bf16[208,1280]{1,0:T(8,128)(2,1)S(1)}, bf16[208,1280]{1,0:T(8,128)(2,1)S(1)}, u32[]{:S(2)}, u32[]{:S(2)}) %collective-permute-start.2) | collective-permute-done | bytes 532512 | tf_op jit(solution)/shard_map/ppermute | solution.py:443
  32.4 0.5 shard_map.107
  32.9 0.0 copy-start.1
  32.9 1.6 %collective-permute-start.7 = (bf16[80,1280]{1,0:T(8,128)(2,1)S(1)}, bf16[80,1280]{1,0:T(8,128)(2,1)S(1)}, u32[]{:S(2)}, u32[]{:S(2)}) collective-permute-start(bf16[80,1280]{1,0:T(8,128)(2,1)S(1)} %get-tuple-element.40), channel_id=1, source_target_pairs={{0,4},{2,6},{4,0},{6,2},{1,5},{3,7},{5,1},{7,3},{8,12},{10,14},{12... | collective-permute-start | bytes 614408 | tf_op jit(solution)/shard_map/ppermute | solution.py:443
  34.5 0.5 collective-permute-start.8
  35.1 0.0 copy-done
  35.1 0.8 %shard_map.108.back_ref = f32[240,320]{1,0:T(8,128)S(1)} custom-call(bf16[240,2560]{1,0:T(8,128)(2,1)S(1)} %get-tuple-element.36.near_ref, bf16[320,2560]{1,0:T(8,128)(2,1)S(1)} %bitcast.6), custom_call_target="tpu_custom_call" | custom-call | tf_op jit(solution)/shard_map/pallas_call | solution.py:508
  35.9 0.0 copy-done.1
  35.9 1.7 %shard_map.109 = (bf16[80,2560]{1,0:T(8,128)(2,1)S(1)}, bf16[80,2560]{1,0:T(8,128)(2,1)S(1)}, bf16[80,2560]{1,0:T(8,128)(2,1)S(1)}, bf16[240,320]{1,0:T(8,128)(2,1)S(1)}) custom-call(bf16[240,2560]{1,0:T(8,128)(2,1)S(1)} %get-tuple-element.35.near_ref, f32[240,320]{1,0:T(8,128)S(1)} %shard_map.108.back_ref, bf16[320,2560]{1,0:T(8,128)(2,1)S(1)} %bitcast.10, ...), custom_call_target="tpu_custom_call" | custom-call | tf_op jit(solution)/shard_map/pallas_call | solution.py:510
  37.6 0.9 %shard_map.110.refs_6_ = f32[2560,320]{1,0:T(8,128)S(1)} custom-call(bf16[240,2560]{1,0:T(8,128)(2,1)S(1)} %get-tuple-element.35.near_ref, bf16[240,320]{1,0:T(8,128)(2,1)S(1)} %get-tuple-element.44.grad_ref), custom_call_target="tpu_custom_call" | custom-call | tf_op jit(solution)/shard_map/pallas_call | solution.py:513
  38.5 0.0 collective-permute-done.9.refs_2_
  38.6 0.0 collective-permute-done.10.refs_3_
  38.6 1.9 %collective-permute-done.7.refs_0_ = bf16[80,1280]{1,0:T(8,128)(2,1)S(1)} collective-permute-done((bf16[80,1280]{1,0:T(8,128)(2,1)S(1)}, bf16[80,1280]{1,0:T(8,128)(2,1)S(1)}, u32[]{:S(2)}, u32[]{:S(2)}) %collective-permute-start.7) | collective-permute-done | bytes 204832 | tf_op jit(solution)/shard_map/ppermute | solution.py:443
  40.5 0.0 collective-permute-done.8.refs_1_
  40.5 2.1 %shard_map.111 = (bf16[80,320]{1,0:T(8,128)(2,1)S(1)}, f32[4,800,128]{2,1,0:T(8,128)S(1)}, bf16[4,800,128]{2,1,0:T(8,128)(2,1)S(1)}) custom-call(bf16[80,1280]{1,0:T(8,128)(2,1)S(1)} %collective-permute-done.7.refs_0_, bf16[80,1280]{1,0:T(8,128)(2,1)S(1)} %collective-permute-done.8.refs_1_, bf16[80,1280]{1,0:T(8,128)(2,1)S(1)} %collective-permute-done.9.refs_2_, ...), custom_call_target="tpu_custom_call" | custom-call | tf_op jit(solution)/shard_map/pallas_call | solution.py:515
  42.6 0.1 collective-permute-start.12
  42.7 0.4 collective-permute-start.5
  43.1 1.7 %collective-permute-start.6 = (bf16[80,2560]{1,0:T(8,128)(2,1)S(1)}, bf16[80,2560]{1,0:T(8,128)(2,1)S(1)}, u32[]{:S(2)}, u32[]{:S(2)}) collective-permute-start(bf16[80,2560]{1,0:T(8,128)(2,1)S(1)} %get-tuple-element.39), channel_id=1, source_target_pairs={{0,4},{2,6},{4,0},{6,2},{1,5},{3,7},{5,1},{7,3},{8,12},{10,14},{12... | collective-permute-start | bytes 1228808 | tf_op jit(solution)/shard_map/ppermute | solution.py:443
  44.8 0.5 shard_map.112
  45.3 1.5 %collective-permute-start.11 = (bf16[80,2560]{1,0:T(8,128)(2,1)S(1)}, bf16[80,2560]{1,0:T(8,128)(2,1)S(1)}, u32[]{:S(2)}, u32[]{:S(2)}) collective-permute-start(bf16[80,2560]{1,0:T(8,128)(2,1)S(1)} %shard_map.112), channel_id=1, source_target_pairs={{0,6},{2,4},{4,2},{6,0},{1,7},{3,5},{5,3},{7,1},{8,14},{10,12},{12... | collective-permute-start | bytes 1228808 | tf_op jit(solution)/shard_map/ppermute | solution.py:443
  46.8 0.0 collective-permute-done.12.other_ref
  46.8 0.2 shard_map.114
  47.0 1.6 %collective-permute-start.13 = (bf16[800,128]{1,0:T(8,128)(2,1)S(1)}, bf16[800,128]{1,0:T(8,128)(2,1)S(1)}, u32[]{:S(2)}, u32[]{:S(2)}) collective-permute-start(bf16[800,128]{1,0:T(8,128)(2,1)S(1)} %get-tuple-element.49), channel_id=1, source_target_pairs={{0,8},{8,0},{16,24},{24,16},{1,9},{9,1},{17,25},{25,17},{2,10},{10... | collective-permute-start | bytes 614408 | tf_op jit(solution)/shard_map/ppermute | solution.py:443
  48.6 2.6 %collective-permute-start.14 = (bf16[800,128]{1,0:T(8,128)(2,1)S(1)}, bf16[800,128]{1,0:T(8,128)(2,1)S(1)}, u32[]{:S(2)}, u32[]{:S(2)}) collective-permute-start(bf16[800,128]{1,0:T(8,128)(2,1)S(1)} %get-tuple-element.50), channel_id=1, source_target_pairs={{0,16},{8,24},{16,0},{24,8},{1,17},{9,25},{17,1},{25,9},{2,18},{10... | collective-permute-start | bytes 614408 | tf_op jit(solution)/shard_map/ppermute | solution.py:443
  51.2 3.8 %collective-permute-done.5.refs_1_ = bf16[80,2560]{1,0:T(8,128)(2,1)S(1)} collective-permute-done((bf16[80,2560]{1,0:T(8,128)(2,1)S(1)}, bf16[80,2560]{1,0:T(8,128)(2,1)S(1)}, u32[]{:S(2)}, u32[]{:S(2)}) %collective-permute-start.5) | collective-permute-done | bytes 409632 | tf_op jit(solution)/shard_map/ppermute | solution.py:443
  55.1 3.6 %collective-permute-start.15 = (bf16[800,128]{1,0:T(8,128)(2,1)S(1)}, bf16[800,128]{1,0:T(8,128)(2,1)S(1)}, u32[]{:S(2)}, u32[]{:S(2)}) collective-permute-start(bf16[800,128]{1,0:T(8,128)(2,1)S(1)} %get-tuple-element.51), channel_id=1, source_target_pairs={{0,24},{8,16},{16,8},{24,0},{1,25},{9,17},{17,9},{25,1},{2,26},{10... | collective-permute-start | bytes 614408 | tf_op jit(solution)/shard_map/ppermute | solution.py:443
  58.6 4.1 %collective-permute-done.6.refs_2_ = bf16[80,2560]{1,0:T(8,128)(2,1)S(1)} collective-permute-done((bf16[80,2560]{1,0:T(8,128)(2,1)S(1)}, bf16[80,2560]{1,0:T(8,128)(2,1)S(1)}, u32[]{:S(2)}, u32[]{:S(2)}) %collective-permute-start.6) | collective-permute-done | bytes 409632 | tf_op jit(solution)/shard_map/ppermute | solution.py:443
  62.7 1.6 %collective-permute-done.11.refs_3_ = bf16[80,2560]{1,0:T(8,128)(2,1)S(1)} collective-permute-done((bf16[80,2560]{1,0:T(8,128)(2,1)S(1)}, bf16[80,2560]{1,0:T(8,128)(2,1)S(1)}, u32[]{:S(2)}, u32[]{:S(2)}) %collective-permute-start.11) | collective-permute-done | bytes 409632 | tf_op jit(solution)/shard_map/ppermute | solution.py:443
  64.3 1.8 %shard_map.113 = bf16[128,2560]{1,0:T(8,128)(2,1)} custom-call(s32[8,128]{1,0:T(8,128)S(1)} %get-tuple-element.27.slots_ref, f32[8,128]{1,0:T(8,128)S(1)} %get-tuple-element.28.table_ref.gates_ref, f32[128,2560]{1,0:T(8,128)S(1)} %get-tuple-element.29.stream_ref, bf16[80,2560]{1,0:T(8,128)(2,1)S(1)} %get-tuple-element.37.refs_0_, ...), custom_call_target="tpu_custom_call" | custom-call | tf_op jit(solution)/shard_map/pallas_call | solution.py:554
  66.1 0.0 collective-permute-done.13.refs_0_
  66.1 0.0 collective-permute-done.14.refs_1_
  66.2 0.0 collective-permute-done.15.refs_2_
  66.2 0.9 %shard_map.115 = f32[1,320,320]{2,1,0:T(8,128)} custom-call(f32[800,128]{1,0:T(8,128)S(1)} %get-tuple-element.48.own_ref, bf16[800,128]{1,0:T(8,128)(2,1)S(1)} %collective-permute-done.13.refs_0_, bf16[800,128]{1,0:T(8,128)(2,1)S(1)} %collective-permute-done.14.refs_1_, bf16[800,128]{1,0:T(8,128)(2,1)S(1)} %collective-permute-done.15.refs_2_), custom_call_target="tpu_custom_call" | custom-call | tf_op jit(solution)/shard_map/pallas_call | solution.py:525
Async XLA Ops:
  0.6 6.1 %collective-permute-start = (bf16[2,16,2560]{2,1,0:T(8,128)(2,1)}, bf16[2,16,2560]{2,1,0:T(8,128)(2,1)S(1)}, u32[]{:S(2)}, u32[]{:S(2)}) collective-permute-start(bf16[2,16,2560]{2,1,0:T(8,128)(2,1)} %refs_3_.1), channel_id=1, source_target_pairs={{0,1},{1,0},{2,3},{3,2},{4,5},{5,4},{6,7},{7,6},{8,9},{9,8},{10,11... | collective-permute-start | bytes 491528 | tf_op jit(solution)/shard_map/ppermute | solution.py:443
  2.7 16.4 %collective-permute-start.3 = (bf16[224,1280]{1,0:T(8,128)(2,1)S(1)}, bf16[224,1280]{1,0:T(8,128)(2,1)S(1)}, u32[]{:S(2)}, u32[]{:S(2)}) collective-permute-start(bf16[224,1280]{1,0:T(8,128)(2,1)S(1)} %get-tuple-element.32.left_ref), channel_id=1, source_target_pairs={{0,2},{2,0},{4,6},{6,4},{1,3},{3,1},{5,7},{7,5},{8,10},{10,8},{12,... | collective-permute-start | bytes 1720328 | tf_op jit(solution)/shard_map/ppermute | solution.py:443
  5.2 15.8 %collective-permute-start.4 = (bf16[224,1280]{1,0:T(8,128)(2,1)S(1)}, bf16[224,1280]{1,0:T(8,128)(2,1)S(1)}, u32[]{:S(2)}, u32[]{:S(2)}) collective-permute-start(bf16[224,1280]{1,0:T(8,128)(2,1)S(1)} %get-tuple-element.33.right_ref), channel_id=1, source_target_pairs={{0,4},{2,6},{4,0},{6,2},{1,5},{3,7},{5,1},{7,3},{8,12},{10,14},{12... | collective-permute-start | bytes 1720328 | tf_op jit(solution)/shard_map/ppermute | solution.py:443
  11.3 19.1 %collective-permute-start.1 = (bf16[208,1280]{1,0:T(8,128)(2,1)S(1)}, bf16[208,1280]{1,0:T(8,128)(2,1)S(1)}, u32[]{:S(2)}, u32[]{:S(2)}) collective-permute-start(bf16[208,1280]{1,0:T(8,128)(2,1)S(1)} %get-tuple-element.30.left_ref), channel_id=1, source_target_pairs={{0,2},{2,0},{4,6},{6,4},{1,3},{3,1},{5,7},{7,5},{8,10},{10,8},{12,... | collective-permute-start | bytes 1597448 | tf_op jit(solution)/shard_map/ppermute | solution.py:443
  11.9 20.5 %collective-permute-start.2 = (bf16[208,1280]{1,0:T(8,128)(2,1)S(1)}, bf16[208,1280]{1,0:T(8,128)(2,1)S(1)}, u32[]{:S(2)}, u32[]{:S(2)}) collective-permute-start(bf16[208,1280]{1,0:T(8,128)(2,1)S(1)} %get-tuple-element.31.right_ref), channel_id=1, source_target_pairs={{0,4},{2,6},{4,0},{6,2},{1,5},{3,7},{5,1},{7,3},{8,12},{10,14},{12... | collective-permute-start | bytes 1597448 | tf_op jit(solution)/shard_map/ppermute | solution.py:443
  21.6 13.4 %copy-start = (bf16[1,320,2560]{2,1,0:T(8,128)(2,1)S(1)}, bf16[1,320,2560]{2,1,0:T(8,128)(2,1)}, u32[]{:S(2)}) copy-start(bf16[1,320,2560]{2,1,0:T(8,128)(2,1)} %param.16) | copy-start | bytes 4915204
  21.7 16.9 %collective-permute-start.9 = (bf16[80,1280]{1,0:T(8,128)(2,1)S(1)}, bf16[80,1280]{1,0:T(8,128)(2,1)S(1)}, u32[]{:S(2)}, u32[]{:S(2)}) collective-permute-start(bf16[80,1280]{1,0:T(8,128)(2,1)S(1)} %get-tuple-element.42), channel_id=1, source_target_pairs={{0,4},{2,6},{4,0},{6,2},{1,5},{3,7},{5,1},{7,3},{8,12},{10,14},{12... | collective-permute-start | bytes 614408 | tf_op jit(solution)/shard_map/ppermute | solution.py:443
  23.2 15.3 %collective-permute-start.10 = (bf16[80,1280]{1,0:T(8,128)(2,1)S(1)}, bf16[80,1280]{1,0:T(8,128)(2,1)S(1)}, u32[]{:S(2)}, u32[]{:S(2)}) collective-permute-start(bf16[80,1280]{1,0:T(8,128)(2,1)S(1)} %get-tuple-element.43), channel_id=1, source_target_pairs={{0,2},{2,0},{4,6},{6,4},{1,3},{3,1},{5,7},{7,5},{8,10},{10,8},{12,... | collective-permute-start | bytes 614408 | tf_op jit(solution)/shard_map/ppermute | solution.py:443
  32.9 3.0 %copy-start.1 = (bf16[1,2560,320]{1,2,0:T(8,128)(2,1)S(1)}, bf16[1,2560,320]{1,2,0:T(8,128)(2,1)}, u32[]{:S(2)}) copy-start(bf16[1,2560,320]{1,2,0:T(8,128)(2,1)} %param.15) | copy-start | bytes 4915204
  32.9 7.6 %collective-permute-start.7 = (bf16[80,1280]{1,0:T(8,128)(2,1)S(1)}, bf16[80,1280]{1,0:T(8,128)(2,1)S(1)}, u32[]{:S(2)}, u32[]{:S(2)}) collective-permute-start(bf16[80,1280]{1,0:T(8,128)(2,1)S(1)} %get-tuple-element.40), channel_id=1, source_target_pairs={{0,4},{2,6},{4,0},{6,2},{1,5},{3,7},{5,1},{7,3},{8,12},{10,14},{12... | collective-permute-start | bytes 614408 | tf_op jit(solution)/shard_map/ppermute | solution.py:443
  34.5 6.0 %collective-permute-start.8 = (bf16[80,1280]{1,0:T(8,128)(2,1)S(1)}, bf16[80,1280]{1,0:T(8,128)(2,1)S(1)}, u32[]{:S(2)}, u32[]{:S(2)}) collective-permute-start(bf16[80,1280]{1,0:T(8,128)(2,1)S(1)} %get-tuple-element.41), channel_id=1, source_target_pairs={{0,2},{2,0},{4,6},{6,4},{1,3},{3,1},{5,7},{7,5},{8,10},{10,8},{12,... | collective-permute-start | bytes 614408 | tf_op jit(solution)/shard_map/ppermute | solution.py:443
  42.6 4.2 %collective-permute-start.12 = (bf16[4,800,128]{2,1,0:T(8,128)(2,1)S(1)}, bf16[4,800,128]{2,1,0:T(8,128)(2,1)S(1)}, u32[]{:S(2)}, u32[]{:S(2)}) collective-permute-start(bf16[4,800,128]{2,1,0:T(8,128)(2,1)S(1)} %get-tuple-element.47), channel_id=1, source_target_pairs={{0,1},{1,0},{2,3},{3,2},{4,5},{5,4},{6,7},{7,6},{8,9},{9,8},{10,11... | collective-permute-start | bytes 2457608 | tf_op jit(solution)/shard_map/ppermute | solution.py:443
  42.7 12.3 %collective-permute-start.5 = (bf16[80,2560]{1,0:T(8,128)(2,1)S(1)}, bf16[80,2560]{1,0:T(8,128)(2,1)S(1)}, u32[]{:S(2)}, u32[]{:S(2)}) collective-permute-start(bf16[80,2560]{1,0:T(8,128)(2,1)S(1)} %get-tuple-element.38), channel_id=1, source_target_pairs={{0,2},{2,0},{4,6},{6,4},{1,3},{3,1},{5,7},{7,5},{8,10},{10,8},{12,... | collective-permute-start | bytes 1228808 | tf_op jit(solution)/shard_map/ppermute | solution.py:443
  43.1 19.6 %collective-permute-start.6 = (bf16[80,2560]{1,0:T(8,128)(2,1)S(1)}, bf16[80,2560]{1,0:T(8,128)(2,1)S(1)}, u32[]{:S(2)}, u32[]{:S(2)}) collective-permute-start(bf16[80,2560]{1,0:T(8,128)(2,1)S(1)} %get-tuple-element.39), channel_id=1, source_target_pairs={{0,4},{2,6},{4,0},{6,2},{1,5},{3,7},{5,1},{7,3},{8,12},{10,14},{12... | collective-permute-start | bytes 1228808 | tf_op jit(solution)/shard_map/ppermute | solution.py:443
  45.3 19.0 %collective-permute-start.11 = (bf16[80,2560]{1,0:T(8,128)(2,1)S(1)}, bf16[80,2560]{1,0:T(8,128)(2,1)S(1)}, u32[]{:S(2)}, u32[]{:S(2)}) collective-permute-start(bf16[80,2560]{1,0:T(8,128)(2,1)S(1)} %shard_map.112), channel_id=1, source_target_pairs={{0,6},{2,4},{4,2},{6,0},{1,7},{3,5},{5,3},{7,1},{8,14},{10,12},{12... | collective-permute-start | bytes 1228808 | tf_op jit(solution)/shard_map/ppermute | solution.py:443
  47.0 19.1 %collective-permute-start.13 = (bf16[800,128]{1,0:T(8,128)(2,1)S(1)}, bf16[800,128]{1,0:T(8,128)(2,1)S(1)}, u32[]{:S(2)}, u32[]{:S(2)}) collective-permute-start(bf16[800,128]{1,0:T(8,128)(2,1)S(1)} %get-tuple-element.49), channel_id=1, source_target_pairs={{0,8},{8,0},{16,24},{24,16},{1,9},{9,1},{17,25},{25,17},{2,10},{10... | collective-permute-start | bytes 614408 | tf_op jit(solution)/shard_map/ppermute | solution.py:443
  48.6 17.5 %collective-permute-start.14 = (bf16[800,128]{1,0:T(8,128)(2,1)S(1)}, bf16[800,128]{1,0:T(8,128)(2,1)S(1)}, u32[]{:S(2)}, u32[]{:S(2)}) collective-permute-start(bf16[800,128]{1,0:T(8,128)(2,1)S(1)} %get-tuple-element.50), channel_id=1, source_target_pairs={{0,16},{8,24},{16,0},{24,8},{1,17},{9,25},{17,1},{25,9},{2,18},{10... | collective-permute-start | bytes 614408 | tf_op jit(solution)/shard_map/ppermute | solution.py:443
  55.1 11.1 %collective-permute-start.15 = (bf16[800,128]{1,0:T(8,128)(2,1)S(1)}, bf16[800,128]{1,0:T(8,128)(2,1)S(1)}, u32[]{:S(2)}, u32[]{:S(2)}) collective-permute-start(bf16[800,128]{1,0:T(8,128)(2,1)S(1)} %get-tuple-element.51), channel_id=1, source_target_pairs={{0,24},{8,16},{16,8},{24,0},{1,25},{9,17},{17,9},{25,1},{2,26},{10... | collective-permute-start | bytes 614408 | tf_op jit(solution)/shard_map/ppermute | solution.py:443

commit v5 on v4

--- a/solution.py
+++ b/solution.py
@@ -422,21 +422,29 @@
     refs[-1][0] = unpack(total, rows, columns)
 
 
-def combine(count, slots_ref, gates_ref, stream_ref, *refs):
-    back_refs, out_ref = refs[0:count], refs[count]
+def combine_here(slots_ref, gates_ref, stream_ref, here_ref, total_ref):
+    mix_into(slots_ref, gates_ref, 0, stream_ref, (here_ref,), total_ref)
+
+
+def combine_rest(slots_ref, gates_ref, base_ref, *refs):
+    mix_into(slots_ref, gates_ref, 1, base_ref, refs[:-1], refs[-1])
+
+
+def mix_into(slots_ref, gates_ref, first, base_ref, result_refs, out_ref):
     slots = slots_ref[...]
     gates = gates_ref[...].T
-    width = stream_ref.shape[1]
-    picks = [as_bf16(one_hot(slots, k, back_refs[k].shape[0])) for k in range(count)]
-    for at in range(0, width, CHUNK):
+    picks = [
+        as_bf16(one_hot(slots, first + k, ref.shape[0])) for k, ref in enumerate(result_refs)
+    ]
+    for at in range(0, base_ref.shape[1], CHUNK):
         cols = slice(at, at + CHUNK)
-        total = stream_ref[:, cols]
-        for k in range(count):
+        total = base_ref[:, cols]
+        for k, ref in enumerate(result_refs):
             row = lax.dot_general(
-                picks[k], back_refs[k][:, cols], (((0,), (0,)), ((), ())), preferred_element_type=F32
+                picks[k], ref[:, cols], (((0,), (0,)), ((), ())), preferred_element_type=F32
             )
-            total = total + row * gates[:, k : k + 1]
-        out_ref[:, cols] = total.astype(BF16)
+            total = total + row * gates[:, first + k : first + k + 1]
+        out_ref[:, cols] = total.astype(out_ref.dtype)
 
 
 def swap(value, axis, k):
@@ -521,7 +529,7 @@
             functools.partial(add_cores, replicas),
             [shape(packed[1:], F32)] + [shape(packed[1:], BF16)] * (replicas - 1),
         )(keep, swap(send, "seq", 1))
-        received = [swap(sends[k - 1], "dp", k) for k in range(1, replicas)]
+        received = [swap(sends[k - 1], "dp", k) for k in (2, 1, 3)]
         grads_here = call(add_replicas, shape((1, block, hidden_width), F32))(own, *received)
     else:
         rows_shape = [shape((capacity, width), BF16)] * experts
@@ -551,8 +559,9 @@
         grads_here = lax.psum_scatter(whole, ("dp", "seq"), scatter_dimension=0, tiled=True)[None]
     results = [results[0]] + [swap(results[k], "expert", k) for k in range(1, experts)]
 
-    layer_output = call(functools.partial(combine, experts), shape((tokens, width), BF16))(
-        slots, gates, stream, *results
+    base = call(combine_here, shape((tokens, width), F32))(slots, gates, stream, results[0])
+    layer_output = call(combine_rest, shape((tokens, width), BF16))(
+        slots, gates, base, *results[1:]
     )
     return layer_output, grads_here
 

time: 67.9 us -> 67.5 us (level)
    pallas_call x1 -> x2, Pallas kernels: 1.81 us -> 1.98 us  [the longest x1 1.62 us: per_device(): call(combine_rest, shape((tokens, width), BF16))]
where the time goes in v5:
time: 67.5 us; the launch traced here: 66.9 us
  waiting for transfers between devices  28.8 us (43%)
  starting transfers between devices  21 us (31%)
  Pallas kernels  16.3 us (24%)
  between operations  0.77 us (1%)
    ppermute x16, waiting for transfers between devices, swap(): lax.ppermute(value, axis, [(i, i ^ k) for i in range(lax.axis_size(axis))])  28.8 us
    ppermute x16, starting transfers between devices, swap(): lax.ppermute(value, axis, [(i, i ^ k) for i in range(lax.axis_size(axis))])  21 us
    pallas_call x1, Pallas kernels, per_device(): stream, left_rows, right_rows = attend_call(slots, *attend_inputs)  4.59 us
    pallas_call x1, Pallas kernels, per_device(): call(functools.partial(finish_far, replicas), [shape((capacity, hidden_wi...  2.12 us
    pallas_call x1, Pallas kernels, per_device(): call(experts_near, [result_shape] * 3 + [shape(near_narrow, BF16)])  1.71 us
    pallas_call x1, Pallas kernels, per_device(): call(combine_rest, shape((tokens, width), BF16))  1.62 us
    pallas_call x1, Pallas kernels, per_device(): call(split_grads, [first_hop] * 2 + [integers, table], [vmem((2, tokens),...  1.5 us
  transfers between devices with their start and end apart: 16, of which 8 were waited for; matrix products, arithmetic and copies ran while one was open for 0% of the time, Pallas kernels for 20%

profile of v5, /device:TPU:0, one launch (start us, length us, event | category | flops | bytes accessed | tf_op | source)
XLA Modules:
  0.0 66.9 jit_solution(1010866005994282362)
XLA Ops:
  0.6 0.5 collective-permute-start
  1.1 1.5 %shard_map.104 = (bf16[224,1280]{1,0:T(8,128)(2,1)S(1)}, bf16[224,1280]{1,0:T(8,128)(2,1)S(1)}, s32[8,128]{1,0:T(8,128)S(1)}, f32[8,128]{1,0:T(8,128)S(1)}) custom-call(s32[2,128]{1,0:T(2,128)} %bitcast.12, f32[2,128]{1,0:T(2,128)} %bitcast.13, bf16[128,2560]{1,0:T(8,128)(2,1)} %grad_hbm.1), custom_call_target="tpu_custom_call" | custom-call | tf_op jit(solution)/shard_map/pallas_call | solution.py:499
  2.7 2.6 %collective-permute-start.3 = (bf16[224,1280]{1,0:T(8,128)(2,1)S(1)}, bf16[224,1280]{1,0:T(8,128)(2,1)S(1)}, u32[]{:S(2)}, u32[]{:S(2)}) collective-permute-start(bf16[224,1280]{1,0:T(8,128)(2,1)S(1)} %get-tuple-element.32.left_ref), channel_id=1, source_target_pairs={{0,2},{2,0},{4,6},{6,4},{1,3},{3,1},{5,7},{7,5},{8,10},{10,8},{12,... | collective-permute-start | bytes 1720328 | tf_op jit(solution)/shard_map/ppermute | solution.py:451
  5.2 1.5 %collective-permute-start.4 = (bf16[224,1280]{1,0:T(8,128)(2,1)S(1)}, bf16[224,1280]{1,0:T(8,128)(2,1)S(1)}, u32[]{:S(2)}, u32[]{:S(2)}) collective-permute-start(bf16[224,1280]{1,0:T(8,128)(2,1)S(1)} %get-tuple-element.33.right_ref), channel_id=1, source_target_pairs={{0,4},{2,6},{4,0},{6,2},{1,5},{3,7},{5,1},{7,3},{8,12},{10,14},{12... | collective-permute-start | bytes 1720328 | tf_op jit(solution)/shard_map/ppermute | solution.py:451
  6.7 0.0 collective-permute-done.refs_4_
  6.7 4.6 %shard_map.105 = (f32[128,2560]{1,0:T(8,128)S(1)}, bf16[208,1280]{1,0:T(8,128)(2,1)S(1)}, bf16[208,1280]{1,0:T(8,128)(2,1)S(1)}) custom-call(s32[8,128]{1,0:T(8,128)S(1)} %get-tuple-element.27.slots_ref, bf16[128,2560]{1,0:T(8,128)(2,1)} %refs_0_.1, bf16[128,2560]{1,0:T(8,128)(2,1)} %refs_1_.1, f32[2560]{0:T(1024)} %refs_2_.1, bf16[2,16,2560]{2,1,0:T(8,128)(2,1)} %refs_3_.1, ...), custom_call_target="tpu_custom_call" | custom-call | tf_op jit(solution)/shard_map/pallas_call | solution.py:506
  11.3 0.6 collective-permute-start.1
  11.9 0.1 collective-permute-start.2
  12.0 7.1 %collective-permute-done.3.x_ref = bf16[224,1280]{1,0:T(8,128)(2,1)S(1)} collective-permute-done((bf16[224,1280]{1,0:T(8,128)(2,1)S(1)}, bf16[224,1280]{1,0:T(8,128)(2,1)S(1)}, u32[]{:S(2)}, u32[]{:S(2)}) %collective-permute-start.3) | collective-permute-done | bytes 573472 | tf_op jit(solution)/shard_map/ppermute | solution.py:451
  19.1 2.0 %collective-permute-done.4.y_ref = bf16[224,1280]{1,0:T(8,128)(2,1)S(1)} collective-permute-done((bf16[224,1280]{1,0:T(8,128)(2,1)S(1)}, bf16[224,1280]{1,0:T(8,128)(2,1)S(1)}, u32[]{:S(2)}, u32[]{:S(2)}) %collective-permute-start.4) | collective-permute-done | bytes 573472 | tf_op jit(solution)/shard_map/ppermute | solution.py:451
  21.0 0.6 shard_map.106
  21.6 0.0 copy-start
  21.7 1.6 %collective-permute-start.9 = (bf16[80,1280]{1,0:T(8,128)(2,1)S(1)}, bf16[80,1280]{1,0:T(8,128)(2,1)S(1)}, u32[]{:S(2)}, u32[]{:S(2)}) collective-permute-start(bf16[80,1280]{1,0:T(8,128)(2,1)S(1)} %get-tuple-element.42), channel_id=1, source_target_pairs={{0,4},{2,6},{4,0},{6,2},{1,5},{3,7},{5,1},{7,3},{8,12},{10,14},{12... | collective-permute-start | bytes 614408 | tf_op jit(solution)/shard_map/ppermute | solution.py:451
  23.2 0.5 collective-permute-start.10
  23.8 6.7 %collective-permute-done.1.x_ref = bf16[208,1280]{1,0:T(8,128)(2,1)S(1)} collective-permute-done((bf16[208,1280]{1,0:T(8,128)(2,1)S(1)}, bf16[208,1280]{1,0:T(8,128)(2,1)S(1)}, u32[]{:S(2)}, u32[]{:S(2)}) %collective-permute-start.1) | collective-permute-done | bytes 532512 | tf_op jit(solution)/shard_map/ppermute | solution.py:451
  30.5 2.0 %collective-permute-done.2.y_ref = bf16[208,1280]{1,0:T(8,128)(2,1)S(1)} collective-permute-done((bf16[208,1280]{1,0:T(8,128)(2,1)S(1)}, bf16[208,1280]{1,0:T(8,128)(2,1)S(1)}, u32[]{:S(2)}, u32[]{:S(2)}) %collective-permute-start.2) | collective-permute-done | bytes 532512 | tf_op jit(solution)/shard_map/ppermute | solution.py:451
  32.4 0.5 shard_map.107
  32.9 0.0 copy-start.1
  32.9 1.6 %collective-permute-start.7 = (bf16[80,1280]{1,0:T(8,128)(2,1)S(1)}, bf16[80,1280]{1,0:T(8,128)(2,1)S(1)}, u32[]{:S(2)}, u32[]{:S(2)}) collective-permute-start(bf16[80,1280]{1,0:T(8,128)(2,1)S(1)} %get-tuple-element.40), channel_id=1, source_target_pairs={{0,4},{2,6},{4,0},{6,2},{1,5},{3,7},{5,1},{7,3},{8,12},{10,14},{12... | collective-permute-start | bytes 614408 | tf_op jit(solution)/shard_map/ppermute | solution.py:451
  34.5 0.5 collective-permute-start.8
  35.1 0.0 copy-done
  35.1 0.8 %shard_map.108.back_ref = f32[240,320]{1,0:T(8,128)S(1)} custom-call(bf16[240,2560]{1,0:T(8,128)(2,1)S(1)} %get-tuple-element.36.near_ref, bf16[320,2560]{1,0:T(8,128)(2,1)S(1)} %bitcast.6), custom_call_target="tpu_custom_call" | custom-call | tf_op jit(solution)/shard_map/pallas_call | solution.py:516
  35.9 0.0 copy-done.1
  35.9 1.7 %shard_map.109 = (bf16[80,2560]{1,0:T(8,128)(2,1)S(1)}, bf16[80,2560]{1,0:T(8,128)(2,1)S(1)}, bf16[80,2560]{1,0:T(8,128)(2,1)S(1)}, bf16[240,320]{1,0:T(8,128)(2,1)S(1)}) custom-call(bf16[240,2560]{1,0:T(8,128)(2,1)S(1)} %get-tuple-element.35.near_ref, f32[240,320]{1,0:T(8,128)S(1)} %shard_map.108.back_ref, bf16[320,2560]{1,0:T(8,128)(2,1)S(1)} %bitcast.10, ...), custom_call_target="tpu_custom_call" | custom-call | tf_op jit(solution)/shard_map/pallas_call | solution.py:518
  37.6 0.9 %shard_map.111.refs_6_ = f32[2560,320]{1,0:T(8,128)S(1)} custom-call(bf16[240,2560]{1,0:T(8,128)(2,1)S(1)} %get-tuple-element.35.near_ref, bf16[240,320]{1,0:T(8,128)(2,1)S(1)} %get-tuple-element.44.grad_ref), custom_call_target="tpu_custom_call" | custom-call | tf_op jit(solution)/shard_map/pallas_call | solution.py:521
  38.5 0.0 collective-permute-done.9.refs_2_
  38.6 0.0 collective-permute-done.10.refs_3_
  38.6 1.9 %collective-permute-done.7.refs_0_ = bf16[80,1280]{1,0:T(8,128)(2,1)S(1)} collective-permute-done((bf16[80,1280]{1,0:T(8,128)(2,1)S(1)}, bf16[80,1280]{1,0:T(8,128)(2,1)S(1)}, u32[]{:S(2)}, u32[]{:S(2)}) %collective-permute-start.7) | collective-permute-done | bytes 204832 | tf_op jit(solution)/shard_map/ppermute | solution.py:451
  40.5 0.0 collective-permute-done.8.refs_1_
  40.5 2.1 %shard_map.112 = (bf16[80,320]{1,0:T(8,128)(2,1)S(1)}, f32[4,800,128]{2,1,0:T(8,128)S(1)}, bf16[4,800,128]{2,1,0:T(8,128)(2,1)S(1)}) custom-call(bf16[80,1280]{1,0:T(8,128)(2,1)S(1)} %collective-permute-done.7.refs_0_, bf16[80,1280]{1,0:T(8,128)(2,1)S(1)} %collective-permute-done.8.refs_1_, bf16[80,1280]{1,0:T(8,128)(2,1)S(1)} %collective-permute-done.9.refs_2_, ...), custom_call_target="tpu_custom_call" | custom-call | tf_op jit(solution)/shard_map/pallas_call | solution.py:523
  42.6 0.1 collective-permute-start.12
  42.7 0.4 collective-permute-start.5
  43.1 1.7 %collective-permute-start.6 = (bf16[80,2560]{1,0:T(8,128)(2,1)S(1)}, bf16[80,2560]{1,0:T(8,128)(2,1)S(1)}, u32[]{:S(2)}, u32[]{:S(2)}) collective-permute-start(bf16[80,2560]{1,0:T(8,128)(2,1)S(1)} %get-tuple-element.39), channel_id=1, source_target_pairs={{0,4},{2,6},{4,0},{6,2},{1,5},{3,7},{5,1},{7,3},{8,12},{10,14},{12... | collective-permute-start | bytes 1228808 | tf_op jit(solution)/shard_map/ppermute | solution.py:451
  44.8 0.5 shard_map.113
  45.3 1.5 %collective-permute-start.11 = (bf16[80,2560]{1,0:T(8,128)(2,1)S(1)}, bf16[80,2560]{1,0:T(8,128)(2,1)S(1)}, u32[]{:S(2)}, u32[]{:S(2)}) collective-permute-start(bf16[80,2560]{1,0:T(8,128)(2,1)S(1)} %shard_map.113), channel_id=1, source_target_pairs={{0,6},{2,4},{4,2},{6,0},{1,7},{3,5},{5,3},{7,1},{8,14},{10,12},{12... | collective-permute-start | bytes 1228808 | tf_op jit(solution)/shard_map/ppermute | solution.py:451
  46.8 0.0 collective-permute-done.12.other_ref
  46.8 0.2 shard_map.115
  47.0 2.7 %collective-permute-start.13 = (bf16[800,128]{1,0:T(8,128)(2,1)S(1)}, bf16[800,128]{1,0:T(8,128)(2,1)S(1)}, u32[]{:S(2)}, u32[]{:S(2)}) collective-permute-start(bf16[800,128]{1,0:T(8,128)(2,1)S(1)} %get-tuple-element.49), channel_id=1, source_target_pairs={{0,16},{8,24},{16,0},{24,8},{1,17},{9,25},{17,1},{25,9},{2,18},{10... | collective-permute-start | bytes 614408 | tf_op jit(solution)/shard_map/ppermute | solution.py:451
  49.7 1.5 %collective-permute-start.14 = (bf16[800,128]{1,0:T(8,128)(2,1)S(1)}, bf16[800,128]{1,0:T(8,128)(2,1)S(1)}, u32[]{:S(2)}, u32[]{:S(2)}) collective-permute-start(bf16[800,128]{1,0:T(8,128)(2,1)S(1)} %get-tuple-element.50), channel_id=1, source_target_pairs={{0,8},{8,0},{16,24},{24,16},{1,9},{9,1},{17,25},{25,17},{2,10},{10... | collective-permute-start | bytes 614408 | tf_op jit(solution)/shard_map/ppermute | solution.py:451
  51.2 3.8 %collective-permute-done.5.refs_0_ = bf16[80,2560]{1,0:T(8,128)(2,1)S(1)} collective-permute-done((bf16[80,2560]{1,0:T(8,128)(2,1)S(1)}, bf16[80,2560]{1,0:T(8,128)(2,1)S(1)}, u32[]{:S(2)}, u32[]{:S(2)}) %collective-permute-start.5) | collective-permute-done | bytes 409632 | tf_op jit(solution)/shard_map/ppermute | solution.py:451
  55.1 3.6 %collective-permute-start.15 = (bf16[800,128]{1,0:T(8,128)(2,1)S(1)}, bf16[800,128]{1,0:T(8,128)(2,1)S(1)}, u32[]{:S(2)}, u32[]{:S(2)}) collective-permute-start(bf16[800,128]{1,0:T(8,128)(2,1)S(1)} %get-tuple-element.51), channel_id=1, source_target_pairs={{0,24},{8,16},{16,8},{24,0},{1,25},{9,17},{17,9},{25,1},{2,26},{10... | collective-permute-start | bytes 614408 | tf_op jit(solution)/shard_map/ppermute | solution.py:451
  58.6 0.4 shard_map.110.base_ref
  59.0 3.7 %collective-permute-done.6.refs_1_ = bf16[80,2560]{1,0:T(8,128)(2,1)S(1)} collective-permute-done((bf16[80,2560]{1,0:T(8,128)(2,1)S(1)}, bf16[80,2560]{1,0:T(8,128)(2,1)S(1)}, u32[]{:S(2)}, u32[]{:S(2)}) %collective-permute-start.6) | collective-permute-done | bytes 409632 | tf_op jit(solution)/shard_map/ppermute | solution.py:451
  62.7 1.6 %collective-permute-done.11.refs_2_ = bf16[80,2560]{1,0:T(8,128)(2,1)S(1)} collective-permute-done((bf16[80,2560]{1,0:T(8,128)(2,1)S(1)}, bf16[80,2560]{1,0:T(8,128)(2,1)S(1)}, u32[]{:S(2)}, u32[]{:S(2)}) %collective-permute-start.11) | collective-permute-done | bytes 409632 | tf_op jit(solution)/shard_map/ppermute | solution.py:451
  64.3 1.6 %shard_map.114 = bf16[128,2560]{1,0:T(8,128)(2,1)} custom-call(s32[8,128]{1,0:T(8,128)S(1)} %get-tuple-element.27.slots_ref, f32[8,128]{1,0:T(8,128)S(1)} %get-tuple-element.28.table_ref.gates_ref, f32[128,2560]{1,0:T(8,128)S(1)} %shard_map.110.base_ref, bf16[80,2560]{1,0:T(8,128)(2,1)S(1)} %collective-permute-done.5.refs_0_, ...), custom_call_target="tpu_custom_call" | custom-call | tf_op jit(solution)/shard_map/pallas_call | solution.py:563
  66.0 0.0 collective-permute-done.13.refs_0_
  66.0 0.0 collective-permute-done.14.refs_1_
  66.0 0.0 collective-permute-done.15.refs_2_
  66.0 0.9 %shard_map.116 = f32[1,320,320]{2,1,0:T(8,128)} custom-call(f32[800,128]{1,0:T(8,128)S(1)} %get-tuple-element.48.own_ref, bf16[800,128]{1,0:T(8,128)(2,1)S(1)} %collective-permute-done.13.refs_0_, bf16[800,128]{1,0:T(8,128)(2,1)S(1)} %collective-permute-done.14.refs_1_, bf16[800,128]{1,0:T(8,128)(2,1)S(1)} %collective-permute-done.15.refs_2_), custom_call_target="tpu_custom_call" | custom-call | tf_op jit(solution)/shard_map/pallas_call | solution.py:533
Async XLA Ops:
  0.6 6.1 %collective-permute-start = (bf16[2,16,2560]{2,1,0:T(8,128)(2,1)}, bf16[2,16,2560]{2,1,0:T(8,128)(2,1)S(1)}, u32[]{:S(2)}, u32[]{:S(2)}) collective-permute-start(bf16[2,16,2560]{2,1,0:T(8,128)(2,1)} %refs_3_.1), channel_id=1, source_target_pairs={{0,1},{1,0},{2,3},{3,2},{4,5},{5,4},{6,7},{7,6},{8,9},{9,8},{10,11... | collective-permute-start | bytes 491528 | tf_op jit(solution)/shard_map/ppermute | solution.py:451
  2.7 16.4 %collective-permute-start.3 = (bf16[224,1280]{1,0:T(8,128)(2,1)S(1)}, bf16[224,1280]{1,0:T(8,128)(2,1)S(1)}, u32[]{:S(2)}, u32[]{:S(2)}) collective-permute-start(bf16[224,1280]{1,0:T(8,128)(2,1)S(1)} %get-tuple-element.32.left_ref), channel_id=1, source_target_pairs={{0,2},{2,0},{4,6},{6,4},{1,3},{3,1},{5,7},{7,5},{8,10},{10,8},{12,... | collective-permute-start | bytes 1720328 | tf_op jit(solution)/shard_map/ppermute | solution.py:451
  5.2 15.8 %collective-permute-start.4 = (bf16[224,1280]{1,0:T(8,128)(2,1)S(1)}, bf16[224,1280]{1,0:T(8,128)(2,1)S(1)}, u32[]{:S(2)}, u32[]{:S(2)}) collective-permute-start(bf16[224,1280]{1,0:T(8,128)(2,1)S(1)} %get-tuple-element.33.right_ref), channel_id=1, source_target_pairs={{0,4},{2,6},{4,0},{6,2},{1,5},{3,7},{5,1},{7,3},{8,12},{10,14},{12... | collective-permute-start | bytes 1720328 | tf_op jit(solution)/shard_map/ppermute | solution.py:451
  11.3 19.1 %collective-permute-start.1 = (bf16[208,1280]{1,0:T(8,128)(2,1)S(1)}, bf16[208,1280]{1,0:T(8,128)(2,1)S(1)}, u32[]{:S(2)}, u32[]{:S(2)}) collective-permute-start(bf16[208,1280]{1,0:T(8,128)(2,1)S(1)} %get-tuple-element.30.left_ref), channel_id=1, source_target_pairs={{0,2},{2,0},{4,6},{6,4},{1,3},{3,1},{5,7},{7,5},{8,10},{10,8},{12,... | collective-permute-start | bytes 1597448 | tf_op jit(solution)/shard_map/ppermute | solution.py:451
  11.9 20.5 %collective-permute-start.2 = (bf16[208,1280]{1,0:T(8,128)(2,1)S(1)}, bf16[208,1280]{1,0:T(8,128)(2,1)S(1)}, u32[]{:S(2)}, u32[]{:S(2)}) collective-permute-start(bf16[208,1280]{1,0:T(8,128)(2,1)S(1)} %get-tuple-element.31.right_ref), channel_id=1, source_target_pairs={{0,4},{2,6},{4,0},{6,2},{1,5},{3,7},{5,1},{7,3},{8,12},{10,14},{12... | collective-permute-start | bytes 1597448 | tf_op jit(solution)/shard_map/ppermute | solution.py:451
  21.6 13.4 %copy-start = (bf16[1,320,2560]{2,1,0:T(8,128)(2,1)S(1)}, bf16[1,320,2560]{2,1,0:T(8,128)(2,1)}, u32[]{:S(2)}) copy-start(bf16[1,320,2560]{2,1,0:T(8,128)(2,1)} %param.16) | copy-start | bytes 4915204
  21.7 16.9 %collective-permute-start.9 = (bf16[80,1280]{1,0:T(8,128)(2,1)S(1)}, bf16[80,1280]{1,0:T(8,128)(2,1)S(1)}, u32[]{:S(2)}, u32[]{:S(2)}) collective-permute-start(bf16[80,1280]{1,0:T(8,128)(2,1)S(1)} %get-tuple-element.42), channel_id=1, source_target_pairs={{0,4},{2,6},{4,0},{6,2},{1,5},{3,7},{5,1},{7,3},{8,12},{10,14},{12... | collective-permute-start | bytes 614408 | tf_op jit(solution)/shard_map/ppermute | solution.py:451
  23.2 15.3 %collective-permute-start.10 = (bf16[80,1280]{1,0:T(8,128)(2,1)S(1)}, bf16[80,1280]{1,0:T(8,128)(2,1)S(1)}, u32[]{:S(2)}, u32[]{:S(2)}) collective-permute-start(bf16[80,1280]{1,0:T(8,128)(2,1)S(1)} %get-tuple-element.43), channel_id=1, source_target_pairs={{0,2},{2,0},{4,6},{6,4},{1,3},{3,1},{5,7},{7,5},{8,10},{10,8},{12,... | collective-permute-start | bytes 614408 | tf_op jit(solution)/shard_map/ppermute | solution.py:451
  32.9 3.0 %copy-start.1 = (bf16[1,2560,320]{1,2,0:T(8,128)(2,1)S(1)}, bf16[1,2560,320]{1,2,0:T(8,128)(2,1)}, u32[]{:S(2)}) copy-start(bf16[1,2560,320]{1,2,0:T(8,128)(2,1)} %param.15) | copy-start | bytes 4915204
  32.9 7.6 %collective-permute-start.7 = (bf16[80,1280]{1,0:T(8,128)(2,1)S(1)}, bf16[80,1280]{1,0:T(8,128)(2,1)S(1)}, u32[]{:S(2)}, u32[]{:S(2)}) collective-permute-start(bf16[80,1280]{1,0:T(8,128)(2,1)S(1)} %get-tuple-element.40), channel_id=1, source_target_pairs={{0,4},{2,6},{4,0},{6,2},{1,5},{3,7},{5,1},{7,3},{8,12},{10,14},{12... | collective-permute-start | bytes 614408 | tf_op jit(solution)/shard_map/ppermute | solution.py:451
  34.5 6.0 %collective-permute-start.8 = (bf16[80,1280]{1,0:T(8,128)(2,1)S(1)}, bf16[80,1280]{1,0:T(8,128)(2,1)S(1)}, u32[]{:S(2)}, u32[]{:S(2)}) collective-permute-start(bf16[80,1280]{1,0:T(8,128)(2,1)S(1)} %get-tuple-element.41), channel_id=1, source_target_pairs={{0,2},{2,0},{4,6},{6,4},{1,3},{3,1},{5,7},{7,5},{8,10},{10,8},{12,... | collective-permute-start | bytes 614408 | tf_op jit(solution)/shard_map/ppermute | solution.py:451
  42.6 4.2 %collective-permute-start.12 = (bf16[4,800,128]{2,1,0:T(8,128)(2,1)S(1)}, bf16[4,800,128]{2,1,0:T(8,128)(2,1)S(1)}, u32[]{:S(2)}, u32[]{:S(2)}) collective-permute-start(bf16[4,800,128]{2,1,0:T(8,128)(2,1)S(1)} %get-tuple-element.47), channel_id=1, source_target_pairs={{0,1},{1,0},{2,3},{3,2},{4,5},{5,4},{6,7},{7,6},{8,9},{9,8},{10,11... | collective-permute-start | bytes 2457608 | tf_op jit(solution)/shard_map/ppermute | solution.py:451
  42.7 12.3 %collective-permute-start.5 = (bf16[80,2560]{1,0:T(8,128)(2,1)S(1)}, bf16[80,2560]{1,0:T(8,128)(2,1)S(1)}, u32[]{:S(2)}, u32[]{:S(2)}) collective-permute-start(bf16[80,2560]{1,0:T(8,128)(2,1)S(1)} %get-tuple-element.38), channel_id=1, source_target_pairs={{0,2},{2,0},{4,6},{6,4},{1,3},{3,1},{5,7},{7,5},{8,10},{10,8},{12,... | collective-permute-start | bytes 1228808 | tf_op jit(solution)/shard_map/ppermute | solution.py:451
  43.1 19.6 %collective-permute-start.6 = (bf16[80,2560]{1,0:T(8,128)(2,1)S(1)}, bf16[80,2560]{1,0:T(8,128)(2,1)S(1)}, u32[]{:S(2)}, u32[]{:S(2)}) collective-permute-start(bf16[80,2560]{1,0:T(8,128)(2,1)S(1)} %get-tuple-element.39), channel_id=1, source_target_pairs={{0,4},{2,6},{4,0},{6,2},{1,5},{3,7},{5,1},{7,3},{8,12},{10,14},{12... | collective-permute-start | bytes 1228808 | tf_op jit(solution)/shard_map/ppermute | solution.py:451
  45.3 19.0 %collective-permute-start.11 = (bf16[80,2560]{1,0:T(8,128)(2,1)S(1)}, bf16[80,2560]{1,0:T(8,128)(2,1)S(1)}, u32[]{:S(2)}, u32[]{:S(2)}) collective-permute-start(bf16[80,2560]{1,0:T(8,128)(2,1)S(1)} %shard_map.113), channel_id=1, source_target_pairs={{0,6},{2,4},{4,2},{6,0},{1,7},{3,5},{5,3},{7,1},{8,14},{10,12},{12... | collective-permute-start | bytes 1228808 | tf_op jit(solution)/shard_map/ppermute | solution.py:451
  47.0 18.9 %collective-permute-start.13 = (bf16[800,128]{1,0:T(8,128)(2,1)S(1)}, bf16[800,128]{1,0:T(8,128)(2,1)S(1)}, u32[]{:S(2)}, u32[]{:S(2)}) collective-permute-start(bf16[800,128]{1,0:T(8,128)(2,1)S(1)} %get-tuple-element.49), channel_id=1, source_target_pairs={{0,16},{8,24},{16,0},{24,8},{1,17},{9,25},{17,1},{25,9},{2,18},{10... | collective-permute-start | bytes 614408 | tf_op jit(solution)/shard_map/ppermute | solution.py:451
  49.7 16.3 %collective-permute-start.14 = (bf16[800,128]{1,0:T(8,128)(2,1)S(1)}, bf16[800,128]{1,0:T(8,128)(2,1)S(1)}, u32[]{:S(2)}, u32[]{:S(2)}) collective-permute-start(bf16[800,128]{1,0:T(8,128)(2,1)S(1)} %get-tuple-element.50), channel_id=1, source_target_pairs={{0,8},{8,0},{16,24},{24,16},{1,9},{9,1},{17,25},{25,17},{2,10},{10... | collective-permute-start | bytes 614408 | tf_op jit(solution)/shard_map/ppermute | solution.py:451
  55.1 10.9 %collective-permute-start.15 = (bf16[800,128]{1,0:T(8,128)(2,1)S(1)}, bf16[800,128]{1,0:T(8,128)(2,1)S(1)}, u32[]{:S(2)}, u32[]{:S(2)}) collective-permute-start(bf16[800,128]{1,0:T(8,128)(2,1)S(1)} %get-tuple-element.51), channel_id=1, source_target_pairs={{0,24},{8,16},{16,8},{24,0},{1,25},{9,17},{17,9},{25,1},{2,26},{10... | collective-permute-start | bytes 614408 | tf_op jit(solution)/shard_map/ppermute | solution.py:451

commit v6 on v5

--- a/solution.py
+++ b/solution.py
@@ -262,8 +262,19 @@
     return hidden, slope
 
 
-def back_near(near_ref, out_ref, back_ref):
-    back_ref[...] = hidden_grad(near_ref, out_ref)
+def narrow(left_ref, right_ref, matrix_ref):
+    half = left_ref.shape[1]
+    return sum(
+        lax.dot_general(
+            ref[...], matrix_ref[:, at : at + half], (((1,), (1,)), ((), ())), preferred_element_type=F32
+        )
+        for ref, at in ((left_ref, 0), (right_ref, half))
+    )
+
+
+def back_products(near_ref, left_ref, right_ref, out_ref, near_back_ref, far_back_ref):
+    near_back_ref[...] = hidden_grad(near_ref, out_ref)
+    far_back_ref[...] = narrow(left_ref, right_ref, out_ref)
 
 
 def experts_near(near_ref, back_ref, in_ref, out_ref, *refs):
@@ -285,22 +296,12 @@
 
 
 def finish_far(shards, *refs):
-    left_ref, right_ref, grad_left, grad_right, in_ref, out_ref, total_ref = refs[0:7]
-    hidden_ref, keep_ref, send_ref = refs[7:]
-    half = left_ref.shape[1]
-
-    def narrow(left, right, matrix_ref):
-        return sum(
-            lax.dot_general(
-                ref[...], matrix_ref[:, at : at + half], (((1,), (1,)), ((), ())),
-                preferred_element_type=F32,
-            )
-            for ref, at in ((left, 0), (right, half))
-        )
+    left_ref, right_ref, back_ref, in_ref, total_ref = refs[0:5]
+    hidden_ref, keep_ref, send_ref = refs[5:]
 
     hidden, slope = activate(narrow(left_ref, right_ref, in_ref))
     hidden_ref[...] = hidden
-    grads = (narrow(grad_left, grad_right, out_ref) * slope).astype(BF16)
+    grads = (back_ref[...] * slope).astype(BF16)
     halves = [
         lax.dot_general(ref[...], grads, (((0,), (0,)), ((), ())), preferred_element_type=F32)
         for ref in (left_ref, right_ref)
@@ -513,7 +514,9 @@
             left_rows, right_rows, rows_x, rows_y, slots, others
         )
         far_rows = (swap(pass_left, "expert", 2), swap(pass_right, "expert", 1))
-        back = call(back_near, shape(near_narrow, F32))(near_grads, matrix_out)
+        back, far_back = call(
+            back_products, [shape(near_narrow, F32), shape((capacity, hidden_width), F32)]
+        )(near_grads, *far_grads, matrix_out)
         result_shape = shape((capacity, width), BF16)
         *results, near_pre = call(experts_near, [result_shape] * 3 + [shape(near_narrow, BF16)])(
             near_rows, back, matrix_in, matrix_out
@@ -523,7 +526,7 @@
         hidden, keep, send = call(
             functools.partial(finish_far, replicas),
             [shape((capacity, hidden_width), BF16), shape(packed, F32), shape(packed, BF16)],
-        )(*far_rows, *far_grads, matrix_in, matrix_out, total)
+        )(*far_rows, far_back, matrix_in, total)
         results.append(call(widen, result_shape)(hidden, matrix_out))
         own, *sends = call(
             functools.partial(add_cores, replicas),

time: 67.5 us -> 67.5 us (level)
  no operation moved by 1% of the time
where the time goes in v6:
time: 67.5 us; the launch traced here: 66.8 us
  waiting for transfers between devices  28.6 us (42%)
  starting transfers between devices  21 us (31%)
  Pallas kernels  16.3 us (24%)
  between operations  0.76 us (1%)
    ppermute x16, waiting for transfers between devices, swap(): lax.ppermute(value, axis, [(i, i ^ k) for i in range(lax.axis_size(axis))])  28.6 us
    ppermute x16, starting transfers between devices, swap(): lax.ppermute(value, axis, [(i, i ^ k) for i in range(lax.axis_size(axis))])  21 us
    pallas_call x1, Pallas kernels, per_device(): stream, left_rows, right_rows = attend_call(slots, *attend_inputs)  4.58 us
    pallas_call x1, Pallas kernels, per_device(): call(functools.partial(finish_far, replicas), [shape((capacity, hidden_wi...  1.75 us
    pallas_call x1, Pallas kernels, per_device(): call(experts_near, [result_shape] * 3 + [shape(near_narrow, BF16)])  1.7 us
    pallas_call x1, Pallas kernels, per_device(): call(combine_rest, shape((tokens, width), BF16))  1.59 us
    pallas_call x1, Pallas kernels, per_device(): call(split_grads, [first_hop] * 2 + [integers, table], [vmem((2, tokens),...  1.5 us
  transfers between devices with their start and end apart: 16, of which 8 were waited for; matrix products, arithmetic and copies ran while one was open for 0% of the time, Pallas kernels for 20%

profile of v6, /device:TPU:0, one launch (start us, length us, event | category | flops | bytes accessed | tf_op | source)
XLA Modules:
  0.0 66.8 jit_solution(13099401900953158002)
XLA Ops:
  0.6 0.5 collective-permute-start
  1.1 1.5 %shard_map.104 = (bf16[224,1280]{1,0:T(8,128)(2,1)S(1)}, bf16[224,1280]{1,0:T(8,128)(2,1)S(1)}, s32[8,128]{1,0:T(8,128)S(1)}, f32[8,128]{1,0:T(8,128)S(1)}) custom-call(s32[2,128]{1,0:T(2,128)} %bitcast.11, f32[2,128]{1,0:T(2,128)} %bitcast.12, bf16[128,2560]{1,0:T(8,128)(2,1)} %grad_hbm.1), custom_call_target="tpu_custom_call" | custom-call | tf_op jit(solution)/shard_map/pallas_call | solution.py:500
  2.7 2.6 %collective-permute-start.3 = (bf16[224,1280]{1,0:T(8,128)(2,1)S(1)}, bf16[224,1280]{1,0:T(8,128)(2,1)S(1)}, u32[]{:S(2)}, u32[]{:S(2)}) collective-permute-start(bf16[224,1280]{1,0:T(8,128)(2,1)S(1)} %get-tuple-element.34.left_ref), channel_id=1, source_target_pairs={{0,2},{2,0},{4,6},{6,4},{1,3},{3,1},{5,7},{7,5},{8,10},{10,8},{12,... | collective-permute-start | bytes 1720328 | tf_op jit(solution)/shard_map/ppermute | solution.py:452
  5.2 1.5 %collective-permute-start.4 = (bf16[224,1280]{1,0:T(8,128)(2,1)S(1)}, bf16[224,1280]{1,0:T(8,128)(2,1)S(1)}, u32[]{:S(2)}, u32[]{:S(2)}) collective-permute-start(bf16[224,1280]{1,0:T(8,128)(2,1)S(1)} %get-tuple-element.35.right_ref), channel_id=1, source_target_pairs={{0,4},{2,6},{4,0},{6,2},{1,5},{3,7},{5,1},{7,3},{8,12},{10,14},{12... | collective-permute-start | bytes 1720328 | tf_op jit(solution)/shard_map/ppermute | solution.py:452
  6.7 0.0 collective-permute-done.refs_4_
  6.7 4.6 %shard_map.105 = (f32[128,2560]{1,0:T(8,128)S(1)}, bf16[208,1280]{1,0:T(8,128)(2,1)S(1)}, bf16[208,1280]{1,0:T(8,128)(2,1)S(1)}) custom-call(s32[8,128]{1,0:T(8,128)S(1)} %get-tuple-element.29.slots_ref, bf16[128,2560]{1,0:T(8,128)(2,1)} %refs_0_.1, bf16[128,2560]{1,0:T(8,128)(2,1)} %refs_1_.1, f32[2560]{0:T(1024)} %refs_2_.1, bf16[2,16,2560]{2,1,0:T(8,128)(2,1)} %refs_3_.1, ...), custom_call_target="tpu_custom_call" | custom-call | tf_op jit(solution)/shard_map/pallas_call | solution.py:507
  11.3 0.6 collective-permute-start.1
  11.9 0.1 collective-permute-start.2
  12.0 7.1 %collective-permute-done.3.x_ref = bf16[224,1280]{1,0:T(8,128)(2,1)S(1)} collective-permute-done((bf16[224,1280]{1,0:T(8,128)(2,1)S(1)}, bf16[224,1280]{1,0:T(8,128)(2,1)S(1)}, u32[]{:S(2)}, u32[]{:S(2)}) %collective-permute-start.3) | collective-permute-done | bytes 573472 | tf_op jit(solution)/shard_map/ppermute | solution.py:452
  19.1 2.0 %collective-permute-done.4.y_ref = bf16[224,1280]{1,0:T(8,128)(2,1)S(1)} collective-permute-done((bf16[224,1280]{1,0:T(8,128)(2,1)S(1)}, bf16[224,1280]{1,0:T(8,128)(2,1)S(1)}, u32[]{:S(2)}, u32[]{:S(2)}) %collective-permute-start.4) | collective-permute-done | bytes 573472 | tf_op jit(solution)/shard_map/ppermute | solution.py:452
  21.0 0.6 shard_map.106
  21.7 0.0 copy-start
  21.7 1.6 %collective-permute-start.5 = (bf16[80,1280]{1,0:T(8,128)(2,1)S(1)}, bf16[80,1280]{1,0:T(8,128)(2,1)S(1)}, u32[]{:S(2)}, u32[]{:S(2)}) collective-permute-start(bf16[80,1280]{1,0:T(8,128)(2,1)S(1)} %get-tuple-element.39), channel_id=1, source_target_pairs={{0,4},{2,6},{4,0},{6,2},{1,5},{3,7},{5,1},{7,3},{8,12},{10,14},{12... | collective-permute-start | bytes 614408 | tf_op jit(solution)/shard_map/ppermute | solution.py:452
  23.3 0.5 collective-permute-start.6
  23.8 6.7 %collective-permute-done.1.x_ref = bf16[208,1280]{1,0:T(8,128)(2,1)S(1)} collective-permute-done((bf16[208,1280]{1,0:T(8,128)(2,1)S(1)}, bf16[208,1280]{1,0:T(8,128)(2,1)S(1)}, u32[]{:S(2)}, u32[]{:S(2)}) %collective-permute-start.1) | collective-permute-done | bytes 532512 | tf_op jit(solution)/shard_map/ppermute | solution.py:452
  30.5 2.0 %collective-permute-done.2.y_ref = bf16[208,1280]{1,0:T(8,128)(2,1)S(1)} collective-permute-done((bf16[208,1280]{1,0:T(8,128)(2,1)S(1)}, bf16[208,1280]{1,0:T(8,128)(2,1)S(1)}, u32[]{:S(2)}, u32[]{:S(2)}) %collective-permute-start.2) | collective-permute-done | bytes 532512 | tf_op jit(solution)/shard_map/ppermute | solution.py:452
  32.4 0.5 shard_map.107
  32.9 1.6 %collective-permute-start.9 = (bf16[80,1280]{1,0:T(8,128)(2,1)S(1)}, bf16[80,1280]{1,0:T(8,128)(2,1)S(1)}, u32[]{:S(2)}, u32[]{:S(2)}) collective-permute-start(bf16[80,1280]{1,0:T(8,128)(2,1)S(1)} %get-tuple-element.45), channel_id=1, source_target_pairs={{0,4},{2,6},{4,0},{6,2},{1,5},{3,7},{5,1},{7,3},{8,12},{10,14},{12... | collective-permute-start | bytes 614408 | tf_op jit(solution)/shard_map/ppermute | solution.py:452
  34.5 0.5 collective-permute-start.10
  35.1 1.8 %collective-permute-done.5.left_ref = bf16[80,1280]{1,0:T(8,128)(2,1)S(1)} collective-permute-done((bf16[80,1280]{1,0:T(8,128)(2,1)S(1)}, bf16[80,1280]{1,0:T(8,128)(2,1)S(1)}, u32[]{:S(2)}, u32[]{:S(2)}) %collective-permute-start.5) | collective-permute-done | bytes 204832 | tf_op jit(solution)/shard_map/ppermute | solution.py:452
  36.8 0.0 collective-permute-done.6.right_ref
  36.8 0.0 copy-done
  36.8 0.0 copy-start.1
  36.8 1.2 %shard_map.108 = (f32[240,320]{1,0:T(8,128)S(1)}, f32[80,320]{1,0:T(8,128)S(1)}) custom-call(bf16[240,2560]{1,0:T(8,128)(2,1)S(1)} %get-tuple-element.38.near_ref, bf16[80,1280]{1,0:T(8,128)(2,1)S(1)} %collective-permute-done.5.left_ref, bf16[80,1280]{1,0:T(8,128)(2,1)S(1)} %collective-permute-done.6.right_ref, bf16[320,2560]{1,0:T(8,128)(2,1)S(1)} %bitcast.6), custom_call_target="tpu_custom_call" | custom-call | tf_op jit(solution)/shard_map/pallas_call | solution.py:517
  38.1 0.2 copy-done.1
  38.3 1.7 %shard_map.109 = (bf16[80,2560]{1,0:T(8,128)(2,1)S(1)}, bf16[80,2560]{1,0:T(8,128)(2,1)S(1)}, bf16[80,2560]{1,0:T(8,128)(2,1)S(1)}, bf16[240,320]{1,0:T(8,128)(2,1)S(1)}) custom-call(bf16[240,2560]{1,0:T(8,128)(2,1)S(1)} %get-tuple-element.37.near_ref, f32[240,320]{1,0:T(8,128)S(1)} %get-tuple-element.41.back_ref, bf16[320,2560]{1,0:T(8,128)(2,1)S(1)} %bitcast.9, ...), custom_call_target="tpu_custom_call" | custom-call | tf_op jit(solution)/shard_map/pallas_call | solution.py:521
  40.0 0.9 %shard_map.111.refs_4_ = f32[2560,320]{1,0:T(8,128)S(1)} custom-call(bf16[240,2560]{1,0:T(8,128)(2,1)S(1)} %get-tuple-element.37.near_ref, bf16[240,320]{1,0:T(8,128)(2,1)S(1)} %get-tuple-element.48.grad_ref), custom_call_target="tpu_custom_call" | custom-call | tf_op jit(solution)/shard_map/pallas_call | solution.py:524
  40.9 0.0 collective-permute-done.9.refs_0_
  40.9 0.0 collective-permute-done.10.refs_1_
  40.9 1.7 %shard_map.112 = (bf16[80,320]{1,0:T(8,128)(2,1)S(1)}, f32[4,800,128]{2,1,0:T(8,128)S(1)}, bf16[4,800,128]{2,1,0:T(8,128)(2,1)S(1)}) custom-call(bf16[80,1280]{1,0:T(8,128)(2,1)S(1)} %collective-permute-done.9.refs_0_, bf16[80,1280]{1,0:T(8,128)(2,1)S(1)} %collective-permute-done.10.refs_1_, f32[80,320]{1,0:T(8,128)S(1)} %get-tuple-element.47.refs_2_, ...), custom_call_target="tpu_custom_call" | custom-call | tf_op jit(solution)/shard_map/pallas_call | solution.py:526
  42.7 0.1 collective-permute-start.12
  42.7 0.1 collective-permute-start.7
  42.9 2.0 %collective-permute-start.8 = (bf16[80,2560]{1,0:T(8,128)(2,1)S(1)}, bf16[80,2560]{1,0:T(8,128)(2,1)S(1)}, u32[]{:S(2)}, u32[]{:S(2)}) collective-permute-start(bf16[80,2560]{1,0:T(8,128)(2,1)S(1)} %get-tuple-element.44), channel_id=1, source_target_pairs={{0,4},{2,6},{4,0},{6,2},{1,5},{3,7},{5,1},{7,3},{8,12},{10,14},{12... | collective-permute-start | bytes 1228808 | tf_op jit(solution)/shard_map/ppermute | solution.py:452
  44.9 0.5 shard_map.113
  45.3 1.5 %collective-permute-start.11 = (bf16[80,2560]{1,0:T(8,128)(2,1)S(1)}, bf16[80,2560]{1,0:T(8,128)(2,1)S(1)}, u32[]{:S(2)}, u32[]{:S(2)}) collective-permute-start(bf16[80,2560]{1,0:T(8,128)(2,1)S(1)} %shard_map.113), channel_id=1, source_target_pairs={{0,6},{2,4},{4,2},{6,0},{1,7},{3,5},{5,3},{7,1},{8,14},{10,12},{12... | collective-permute-start | bytes 1228808 | tf_op jit(solution)/shard_map/ppermute | solution.py:452
  46.8 0.0 collective-permute-done.12.other_ref
  46.8 0.2 shard_map.115
  47.0 2.6 %collective-permute-start.13 = (bf16[800,128]{1,0:T(8,128)(2,1)S(1)}, bf16[800,128]{1,0:T(8,128)(2,1)S(1)}, u32[]{:S(2)}, u32[]{:S(2)}) collective-permute-start(bf16[800,128]{1,0:T(8,128)(2,1)S(1)} %get-tuple-element.53), channel_id=1, source_target_pairs={{0,16},{8,24},{16,0},{24,8},{1,17},{9,25},{17,1},{25,9},{2,18},{10... | collective-permute-start | bytes 614408 | tf_op jit(solution)/shard_map/ppermute | solution.py:452
  49.6 1.6 %collective-permute-start.14 = (bf16[800,128]{1,0:T(8,128)(2,1)S(1)}, bf16[800,128]{1,0:T(8,128)(2,1)S(1)}, u32[]{:S(2)}, u32[]{:S(2)}) collective-permute-start(bf16[800,128]{1,0:T(8,128)(2,1)S(1)} %get-tuple-element.54), channel_id=1, source_target_pairs={{0,8},{8,0},{16,24},{24,16},{1,9},{9,1},{17,25},{25,17},{2,10},{10... | collective-permute-start | bytes 614408 | tf_op jit(solution)/shard_map/ppermute | solution.py:452
  51.2 3.8 %collective-permute-done.7.refs_0_ = bf16[80,2560]{1,0:T(8,128)(2,1)S(1)} collective-permute-done((bf16[80,2560]{1,0:T(8,128)(2,1)S(1)}, bf16[80,2560]{1,0:T(8,128)(2,1)S(1)}, u32[]{:S(2)}, u32[]{:S(2)}) %collective-permute-start.7) | collective-permute-done | bytes 409632 | tf_op jit(solution)/shard_map/ppermute | solution.py:452
  55.1 3.6 %collective-permute-start.15 = (bf16[800,128]{1,0:T(8,128)(2,1)S(1)}, bf16[800,128]{1,0:T(8,128)(2,1)S(1)}, u32[]{:S(2)}, u32[]{:S(2)}) collective-permute-start(bf16[800,128]{1,0:T(8,128)(2,1)S(1)} %get-tuple-element.55), channel_id=1, source_target_pairs={{0,24},{8,16},{16,8},{24,0},{1,25},{9,17},{17,9},{25,1},{2,26},{10... | collective-permute-start | bytes 614408 | tf_op jit(solution)/shard_map/ppermute | solution.py:452
  58.7 0.4 shard_map.110.base_ref
  59.0 3.7 %collective-permute-done.8.refs_1_ = bf16[80,2560]{1,0:T(8,128)(2,1)S(1)} collective-permute-done((bf16[80,2560]{1,0:T(8,128)(2,1)S(1)}, bf16[80,2560]{1,0:T(8,128)(2,1)S(1)}, u32[]{:S(2)}, u32[]{:S(2)}) %collective-permute-start.8) | collective-permute-done | bytes 409632 | tf_op jit(solution)/shard_map/ppermute | solution.py:452
  62.7 1.6 %collective-permute-done.11.refs_2_ = bf16[80,2560]{1,0:T(8,128)(2,1)S(1)} collective-permute-done((bf16[80,2560]{1,0:T(8,128)(2,1)S(1)}, bf16[80,2560]{1,0:T(8,128)(2,1)S(1)}, u32[]{:S(2)}, u32[]{:S(2)}) %collective-permute-start.11) | collective-permute-done | bytes 409632 | tf_op jit(solution)/shard_map/ppermute | solution.py:452
  64.3 1.6 %shard_map.114 = bf16[128,2560]{1,0:T(8,128)(2,1)} custom-call(s32[8,128]{1,0:T(8,128)S(1)} %get-tuple-element.29.slots_ref, f32[8,128]{1,0:T(8,128)S(1)} %get-tuple-element.30.table_ref.gates_ref, f32[128,2560]{1,0:T(8,128)S(1)} %shard_map.110.base_ref, bf16[80,2560]{1,0:T(8,128)(2,1)S(1)} %collective-permute-done.7.refs_0_, ...), custom_call_target="tpu_custom_call" | custom-call | tf_op jit(solution)/shard_map/pallas_call | solution.py:566
  65.9 0.0 collective-permute-done.13.refs_0_
  65.9 0.0 collective-permute-done.14.refs_1_
  65.9 0.0 collective-permute-done.15.refs_2_
  66.0 0.9 %shard_map.116 = f32[1,320,320]{2,1,0:T(8,128)} custom-call(f32[800,128]{1,0:T(8,128)S(1)} %get-tuple-element.52.own_ref, bf16[800,128]{1,0:T(8,128)(2,1)S(1)} %collective-permute-done.13.refs_0_, bf16[800,128]{1,0:T(8,128)(2,1)S(1)} %collective-permute-done.14.refs_1_, bf16[800,128]{1,0:T(8,128)(2,1)S(1)} %collective-permute-done.15.refs_2_), custom_call_target="tpu_custom_call" | custom-call | tf_op jit(solution)/shard_map/pallas_call | solution.py:536
Async XLA Ops:
  0.6 6.1 %collective-permute-start = (bf16[2,16,2560]{2,1,0:T(8,128)(2,1)}, bf16[2,16,2560]{2,1,0:T(8,128)(2,1)S(1)}, u32[]{:S(2)}, u32[]{:S(2)}) collective-permute-start(bf16[2,16,2560]{2,1,0:T(8,128)(2,1)} %refs_3_.1), channel_id=1, source_target_pairs={{0,1},{1,0},{2,3},{3,2},{4,5},{5,4},{6,7},{7,6},{8,9},{9,8},{10,11... | collective-permute-start | bytes 491528 | tf_op jit(solution)/shard_map/ppermute | solution.py:452
  2.7 16.4 %collective-permute-start.3 = (bf16[224,1280]{1,0:T(8,128)(2,1)S(1)}, bf16[224,1280]{1,0:T(8,128)(2,1)S(1)}, u32[]{:S(2)}, u32[]{:S(2)}) collective-permute-start(bf16[224,1280]{1,0:T(8,128)(2,1)S(1)} %get-tuple-element.34.left_ref), channel_id=1, source_target_pairs={{0,2},{2,0},{4,6},{6,4},{1,3},{3,1},{5,7},{7,5},{8,10},{10,8},{12,... | collective-permute-start | bytes 1720328 | tf_op jit(solution)/shard_map/ppermute | solution.py:452
  5.2 15.8 %collective-permute-start.4 = (bf16[224,1280]{1,0:T(8,128)(2,1)S(1)}, bf16[224,1280]{1,0:T(8,128)(2,1)S(1)}, u32[]{:S(2)}, u32[]{:S(2)}) collective-permute-start(bf16[224,1280]{1,0:T(8,128)(2,1)S(1)} %get-tuple-element.35.right_ref), channel_id=1, source_target_pairs={{0,4},{2,6},{4,0},{6,2},{1,5},{3,7},{5,1},{7,3},{8,12},{10,14},{12... | collective-permute-start | bytes 1720328 | tf_op jit(solution)/shard_map/ppermute | solution.py:452
  11.3 19.1 %collective-permute-start.1 = (bf16[208,1280]{1,0:T(8,128)(2,1)S(1)}, bf16[208,1280]{1,0:T(8,128)(2,1)S(1)}, u32[]{:S(2)}, u32[]{:S(2)}) collective-permute-start(bf16[208,1280]{1,0:T(8,128)(2,1)S(1)} %get-tuple-element.32.left_ref), channel_id=1, source_target_pairs={{0,2},{2,0},{4,6},{6,4},{1,3},{3,1},{5,7},{7,5},{8,10},{10,8},{12,... | collective-permute-start | bytes 1597448 | tf_op jit(solution)/shard_map/ppermute | solution.py:452
  11.9 20.5 %collective-permute-start.2 = (bf16[208,1280]{1,0:T(8,128)(2,1)S(1)}, bf16[208,1280]{1,0:T(8,128)(2,1)S(1)}, u32[]{:S(2)}, u32[]{:S(2)}) collective-permute-start(bf16[208,1280]{1,0:T(8,128)(2,1)S(1)} %get-tuple-element.33.right_ref), channel_id=1, source_target_pairs={{0,4},{2,6},{4,0},{6,2},{1,5},{3,7},{5,1},{7,3},{8,12},{10,14},{12... | collective-permute-start | bytes 1597448 | tf_op jit(solution)/shard_map/ppermute | solution.py:452
  21.7 15.2 %copy-start = (bf16[1,320,2560]{2,1,0:T(8,128)(2,1)S(1)}, bf16[1,320,2560]{2,1,0:T(8,128)(2,1)}, u32[]{:S(2)}) copy-start(bf16[1,320,2560]{2,1,0:T(8,128)(2,1)} %param.16) | copy-start | bytes 4915204
  21.7 15.2 %collective-permute-start.5 = (bf16[80,1280]{1,0:T(8,128)(2,1)S(1)}, bf16[80,1280]{1,0:T(8,128)(2,1)S(1)}, u32[]{:S(2)}, u32[]{:S(2)}) collective-permute-start(bf16[80,1280]{1,0:T(8,128)(2,1)S(1)} %get-tuple-element.39), channel_id=1, source_target_pairs={{0,4},{2,6},{4,0},{6,2},{1,5},{3,7},{5,1},{7,3},{8,12},{10,14},{12... | collective-permute-start | bytes 614408 | tf_op jit(solution)/shard_map/ppermute | solution.py:452
  23.3 13.6 %collective-permute-start.6 = (bf16[80,1280]{1,0:T(8,128)(2,1)S(1)}, bf16[80,1280]{1,0:T(8,128)(2,1)S(1)}, u32[]{:S(2)}, u32[]{:S(2)}) collective-permute-start(bf16[80,1280]{1,0:T(8,128)(2,1)S(1)} %get-tuple-element.40), channel_id=1, source_target_pairs={{0,2},{2,0},{4,6},{6,4},{1,3},{3,1},{5,7},{7,5},{8,10},{10,8},{12,... | collective-permute-start | bytes 614408 | tf_op jit(solution)/shard_map/ppermute | solution.py:452
  32.9 7.9 %collective-permute-start.9 = (bf16[80,1280]{1,0:T(8,128)(2,1)S(1)}, bf16[80,1280]{1,0:T(8,128)(2,1)S(1)}, u32[]{:S(2)}, u32[]{:S(2)}) collective-permute-start(bf16[80,1280]{1,0:T(8,128)(2,1)S(1)} %get-tuple-element.45), channel_id=1, source_target_pairs={{0,4},{2,6},{4,0},{6,2},{1,5},{3,7},{5,1},{7,3},{8,12},{10,14},{12... | collective-permute-start | bytes 614408 | tf_op jit(solution)/shard_map/ppermute | solution.py:452
  34.5 6.4 %collective-permute-start.10 = (bf16[80,1280]{1,0:T(8,128)(2,1)S(1)}, bf16[80,1280]{1,0:T(8,128)(2,1)S(1)}, u32[]{:S(2)}, u32[]{:S(2)}) collective-permute-start(bf16[80,1280]{1,0:T(8,128)(2,1)S(1)} %get-tuple-element.46), channel_id=1, source_target_pairs={{0,2},{2,0},{4,6},{6,4},{1,3},{3,1},{5,7},{7,5},{8,10},{10,8},{12,... | collective-permute-start | bytes 614408 | tf_op jit(solution)/shard_map/ppermute | solution.py:452
  36.8 1.4 %copy-start.1 = (bf16[1,2560,320]{1,2,0:T(8,128)(2,1)S(1)}, bf16[1,2560,320]{1,2,0:T(8,128)(2,1)}, u32[]{:S(2)}) copy-start(bf16[1,2560,320]{1,2,0:T(8,128)(2,1)} %param.15) | copy-start | bytes 4915204
  42.7 4.2 %collective-permute-start.12 = (bf16[4,800,128]{2,1,0:T(8,128)(2,1)S(1)}, bf16[4,800,128]{2,1,0:T(8,128)(2,1)S(1)}, u32[]{:S(2)}, u32[]{:S(2)}) collective-permute-start(bf16[4,800,128]{2,1,0:T(8,128)(2,1)S(1)} %get-tuple-element.51), channel_id=1, source_target_pairs={{0,1},{1,0},{2,3},{3,2},{4,5},{5,4},{6,7},{7,6},{8,9},{9,8},{10,11... | collective-permute-start | bytes 2457608 | tf_op jit(solution)/shard_map/ppermute | solution.py:452
  42.7 12.3 %collective-permute-start.7 = (bf16[80,2560]{1,0:T(8,128)(2,1)S(1)}, bf16[80,2560]{1,0:T(8,128)(2,1)S(1)}, u32[]{:S(2)}, u32[]{:S(2)}) collective-permute-start(bf16[80,2560]{1,0:T(8,128)(2,1)S(1)} %get-tuple-element.43), channel_id=1, source_target_pairs={{0,2},{2,0},{4,6},{6,4},{1,3},{3,1},{5,7},{7,5},{8,10},{10,8},{12,... | collective-permute-start | bytes 1228808 | tf_op jit(solution)/shard_map/ppermute | solution.py:452
  42.9 19.9 %collective-permute-start.8 = (bf16[80,2560]{1,0:T(8,128)(2,1)S(1)}, bf16[80,2560]{1,0:T(8,128)(2,1)S(1)}, u32[]{:S(2)}, u32[]{:S(2)}) collective-permute-start(bf16[80,2560]{1,0:T(8,128)(2,1)S(1)} %get-tuple-element.44), channel_id=1, source_target_pairs={{0,4},{2,6},{4,0},{6,2},{1,5},{3,7},{5,1},{7,3},{8,12},{10,14},{12... | collective-permute-start | bytes 1228808 | tf_op jit(solution)/shard_map/ppermute | solution.py:452
  45.3 19.0 %collective-permute-start.11 = (bf16[80,2560]{1,0:T(8,128)(2,1)S(1)}, bf16[80,2560]{1,0:T(8,128)(2,1)S(1)}, u32[]{:S(2)}, u32[]{:S(2)}) collective-permute-start(bf16[80,2560]{1,0:T(8,128)(2,1)S(1)} %shard_map.113), channel_id=1, source_target_pairs={{0,6},{2,4},{4,2},{6,0},{1,7},{3,5},{5,3},{7,1},{8,14},{10,12},{12... | collective-permute-start | bytes 1228808 | tf_op jit(solution)/shard_map/ppermute | solution.py:452
  47.0 18.9 %collective-permute-start.13 = (bf16[800,128]{1,0:T(8,128)(2,1)S(1)}, bf16[800,128]{1,0:T(8,128)(2,1)S(1)}, u32[]{:S(2)}, u32[]{:S(2)}) collective-permute-start(bf16[800,128]{1,0:T(8,128)(2,1)S(1)} %get-tuple-element.53), channel_id=1, source_target_pairs={{0,16},{8,24},{16,0},{24,8},{1,17},{9,25},{17,1},{25,9},{2,18},{10... | collective-permute-start | bytes 614408 | tf_op jit(solution)/shard_map/ppermute | solution.py:452
  49.6 16.3 %collective-permute-start.14 = (bf16[800,128]{1,0:T(8,128)(2,1)S(1)}, bf16[800,128]{1,0:T(8,128)(2,1)S(1)}, u32[]{:S(2)}, u32[]{:S(2)}) collective-permute-start(bf16[800,128]{1,0:T(8,128)(2,1)S(1)} %get-tuple-element.54), channel_id=1, source_target_pairs={{0,8},{8,0},{16,24},{24,16},{1,9},{9,1},{17,25},{25,17},{2,10},{10... | collective-permute-start | bytes 614408 | tf_op jit(solution)/shard_map/ppermute | solution.py:452
  55.1 10.9 %collective-permute-start.15 = (bf16[800,128]{1,0:T(8,128)(2,1)S(1)}, bf16[800,128]{1,0:T(8,128)(2,1)S(1)}, u32[]{:S(2)}, u32[]{:S(2)}) collective-permute-start(bf16[800,128]{1,0:T(8,128)(2,1)S(1)} %get-tuple-element.55), channel_id=1, source_target_pairs={{0,24},{8,16},{16,8},{24,0},{1,25},{9,17},{17,9},{25,1},{2,26},{10... | collective-permute-start | bytes 614408 | tf_op jit(solution)/shard_map/ppermute | solution.py:452
